TPU v7x, 32 devices: a whole 2x2x4 slice. The times are simulated.
32 devices in a mesh: inline: 8 (over y, x, core), xline: 4 (over z).
Axes of the slice: x: 2, y: 2, z: 4, core: 2. Of those that a mesh axis runs over, the one named last changes fastest.
Arguments:
- traces: bfloat16 [8192, 2048], P(('inline', 'xline')), may hold values from -6 to 6
- owners: int32 [8192, 1], P(('inline', 'xline')), may hold values from 0 to 31, as said below
- midpoint: int32 [8192], P(('inline', 'xline')), may hold values from 0 to 7
- offset_class: int32 [8192], P(('inline', 'xline')), may hold values from 0 to 3
- offsets: float32 [4], replicated, may hold values from 51 to 1024
- velocities: float32 [16], replicated, may hold values from 1 to 4
Outputs:
- stacked: bfloat16 [256, 16, 2048], P(('inline', 'xline'))
- semblance: float32 [256, 16, 2048], P(('inline', 'xline'))
Inputs may be any that keep to these rules, and one draw needn't show every extreme that they name: The 256 traces of one device name one owner at most 16 times; some owners receive 16 traces from every device, and some owners receive none.
All inputs are finite; a program needn't handle non-finite values.
Results may differ from a plain program's by a relative error of at most 0.0053.
Values may be sent and summed in bfloat16 or wider, within the bound.
No kernel may reach another device: no remote copies, remote signals or barrier semaphores. Data moves between devices by JAX's collectives and lax.ppermute only.
A program may use at most 64 MiB of HBM per device.

v0:
```python
import math

import jax
import jax.numpy as jnp
from jax import lax
from jax.sharding import PartitionSpec as P

HALF_WIN = 4
CMP_DEV = 8


def with_halo(block, sides, width):
    for axis, dim in sides:
        count = lax.axis_size(axis)
        forward = [(i, i + 1) for i in range(count - 1)]
        backward = [(target, source) for source, target in forward]
        low = lax.ppermute(
            lax.slice_in_dim(block, block.shape[dim] - width, None, axis=dim), axis, forward
        )
        high = lax.ppermute(lax.slice_in_dim(block, 0, width, axis=dim), axis, backward)
        block = jnp.concatenate([low, block, high], axis=dim)
    return block


def window_sum(values):
    length = values.shape[-1]
    padded = jnp.pad(values, [(0, 0)] * (values.ndim - 1) + [(HALF_WIN, HALF_WIN)])
    summed = padded[..., 0:length]
    for offset in range(1, 2 * HALF_WIN + 1):
        summed = summed + padded[..., offset : offset + length]
    return summed


def panels(binned, offsets, velocities):
    classes, midpoints, samples = binned.shape
    block_len = math.gcd(128, samples)
    window_len = block_len + 8
    block_count = samples // block_len
    padded = jnp.pad(binned, ((0, 0), (0, 0), (0, window_len)))
    sample_time = jnp.arange(samples).astype(jnp.float32)
    row_grid = jnp.arange(window_len)[:, None]

    def cut_window(plane_rows, start_at):
        return lax.dynamic_slice_in_dim(plane_rows, start_at, window_len, 1)

    cut_blocks = jax.vmap(cut_window, (None, 0))
    cut_classes = jax.vmap(cut_blocks, (0, 0))
    cut_velocities = jax.vmap(cut_classes, (None, 0))

    def per_group(velocity_group):
        vel_count = velocity_group.shape[0]
        slowness = offsets[None, :] / velocity_group[:, None]
        position = jnp.sqrt(
            sample_time[None, None, :] * sample_time[None, None, :]
            + (slowness * slowness)[:, :, None]
        )
        floored = jnp.floor(position)
        fraction = position - floored
        sample_index = jnp.minimum(floored, float(samples)).astype(jnp.int32)
        sample_index = sample_index.reshape(vel_count, classes, block_count, block_len)
        begins = sample_index[..., 0]
        local_row = (sample_index - begins[..., None])[..., None, :]
        low_weight = (
            (1.0 - fraction)
            .astype(jnp.bfloat16)
            .reshape(vel_count, classes, block_count, 1, block_len)
        )
        high_weight = fraction.astype(jnp.bfloat16).reshape(
            vel_count, classes, block_count, 1, block_len
        )
        weights = jnp.where(
            row_grid == local_row,
            low_weight,
            jnp.where(row_grid == local_row + 1, high_weight, jnp.zeros((), jnp.bfloat16)),
        )
        windows = cut_velocities(padded, begins)
        moved_out = jnp.einsum(
            "ghbmr,ghbrq->gmhbq", windows, weights, preferred_element_type=jnp.float32
        )
        summed = jnp.sum(moved_out, axis=2).reshape(vel_count, midpoints, samples)
        energy = jnp.sum(moved_out * moved_out, axis=2).reshape(vel_count, midpoints, samples)
        return (summed, energy)

    vel_group = math.gcd(4, velocities.shape[0])
    summed, energy = lax.map(per_group, velocities.reshape(-1, vel_group))
    summed = jnp.transpose(summed, (2, 0, 1, 3)).reshape(midpoints, -1, samples)
    energy = jnp.transpose(energy, (2, 0, 1, 3)).reshape(midpoints, -1, samples)
    return (summed, energy)


def per_device(traces, owners, midpoint, offset_class, offsets, velocities):
    inline_count = lax.axis_size("inline")
    xline_count = lax.axis_size("xline")
    devices = inline_count * xline_count
    trace_rows, samples = traces.shape
    classes = offsets.shape[0]
    capacity = max(2, 2 * trace_rows // devices)
    target = owners[:, 0]
    onehot_dest = (target[:, None] == jnp.arange(devices)[None, :]).astype(jnp.int32)
    slot_rank = jnp.sum((jnp.cumsum(onehot_dest, axis=0) - onehot_dest) * onehot_dest, axis=1)
    slot_row = target * capacity + slot_rank
    buffer = jnp.zeros((devices * capacity, samples), traces.dtype).at[slot_row].set(traces)
    slot_keys = (
        jnp.full((devices * capacity,), -1, jnp.int32)
        .at[slot_row]
        .set(offset_class * CMP_DEV + midpoint)
    )
    buffer = buffer.reshape(inline_count, xline_count, capacity, samples)
    slot_keys = slot_keys.reshape(inline_count, xline_count, capacity)
    arrived, arrived_keys = (
        lax.all_to_all(
            lax.all_to_all(buffer, "inline", split_axis=0, concat_axis=0, tiled=True),
            "xline",
            split_axis=1,
            concat_axis=1,
            tiled=True,
        ),
        lax.all_to_all(
            lax.all_to_all(slot_keys, "inline", split_axis=0, concat_axis=0, tiled=True),
            "xline",
            split_axis=1,
            concat_axis=1,
            tiled=True,
        ),
    )
    arrived = arrived.reshape(-1, samples)
    arrived_keys = arrived_keys.reshape(-1)
    members = arrived_keys[None, :] == jnp.arange(classes * CMP_DEV)[:, None]
    gathers = jnp.dot(members.astype(jnp.bfloat16), arrived, preferred_element_type=jnp.float32)
    binned = gathers.astype(jnp.bfloat16).reshape(classes, CMP_DEV, samples)
    fold_count = jnp.sum(members.astype(jnp.float32).reshape(classes, CMP_DEV, -1), axis=(0, 2))
    summed, energy = panels(binned, offsets, velocities)
    planes = jnp.stack([window_sum(summed * summed), window_sum(energy)])
    rimmed = with_halo(planes, ((("inline", "xline"), 1),), 1)
    smoothed = rimmed[:, 0:-2] + rimmed[:, 1:-1] + rimmed[:, 2:]
    numerator = smoothed[0]
    denominator = smoothed[1]
    stacked = (summed / jnp.maximum(fold_count, 1.0)[:, None, None]).astype(jnp.bfloat16)
    semblance = numerator / jnp.maximum(classes * denominator, 1.0)
    return (stacked, semblance)


def solution(mesh):
    in_specs = (
        P(("inline", "xline"), None),
        P(("inline", "xline"), None),
        P(("inline", "xline")),
        P(("inline", "xline")),
        P(),
        P(),
    )
    out_specs = (P(("inline", "xline"), None, None), P(("inline", "xline"), None, None))
    return jax.shard_map(
        per_device, mesh=mesh, in_specs=in_specs, out_specs=out_specs, check_vma=False
    )
```

profile of v0, /device:TPU:0, one launch (start us, length us, event | category | flops | bytes accessed | tf_op | source)
XLA Modules:
  0.0 357.0 jit_solution(9286992468880067223)
XLA Ops:
  0.6 0.7 fusion.45
  1.3 0.6 reduce-window.6
  2.1 0.8 fusion.43
  2.9 0.7 compare_select_fusion.1
  3.6 0.7 multiply_add_fusion.1
  4.3 1.4 scatter_custom_fusion
  5.7 0.7 reshape.148
  6.4 5.2 %all-to-all-start = ((s32[8,4,16]{2,1,0:T(4,128)}), s32[8,4,16]{2,1,0:T(4,128)S(1)}, u32[]{:S(2)}, u32[]{:S(2)}) async-start(s32[8,4,16]{2,1,0:T(4,128)} %reshape.148), calls=%async_computation | async-start | bytes 32768 | tf_op jit(solution)/shard_map/all_to_all | solution.py:119
  11.6 4.4 %scatter_custom_fusion.1 = bf16[512,2048]{1,0:T(8,128)(2,1)} fusion(s32[256]{0:T(256)S(1)} %bitcast.77, bf16[256,2048]{1,0:T(8,128)(2,1)} %param.8, bf16[]{:T(256)} %constant.65.clone.1), kind=kCustom, calls=%fused_computation.69 | custom fusion | bytes 2097664 | tf_op jit(solution)/shard_map/scatter | solution.py:102
  16.0 0.3 all-to-all-done
  16.3 3.9 %all-to-all-start.2 = ((bf16[8,4,16,2048]{3,2,1,0:T(8,128)(2,1)}), bf16[8,4,16,2048]{3,2,1,0:T(8,128)(2,1)S(1)}, u32[]{:S(2)}, u32[]{:S(2)}) async-start(bf16[8,4,16,2048]{3,2,1,0:T(8,128)(2,1)} %bitcast.65), calls=%async_computation.2 | async-start | bytes 4194304 | tf_op jit(solution)/shard_map/all_to_all | solution.py:112
  20.2 0.7 reshape.187
  20.9 26.0 %all-to-all-done.2 = bf16[8,4,16,2048]{3,2,1,0:T(8,128)(2,1)S(1)} async-done(((bf16[8,4,16,2048]{3,2,1,0:T(8,128)(2,1)}), bf16[8,4,16,2048]{3,2,1,0:T(8,128)(2,1)S(1)}, u32[]{:S(2)}, u32[]{:S(2)}) %all-to-all-start.2) | async-done | bytes 2097184 | tf_op jit(solution)/shard_map/all_to_all | solution.py:112
  46.8 4.9 %all-to-all-start.1 = ((s32[4,1,128]{2,1,0:T(1,128)}), s32[4,1,128]{2,1,0:T(1,128)S(1)}, u32[]{:S(2)}, u32[]{:S(2)}) async-start(s32[4,1,128]{2,1,0:T(1,128)} %reshape.187), calls=%async_computation.1 | async-start | bytes 4096 | tf_op jit(solution)/shard_map/all_to_all | solution.py:118
  51.7 1.5 copy.88
  53.2 4.0 %all-to-all-done.1 = s32[4,1,128]{2,1,0:T(1,128)S(1)} async-done(((s32[4,1,128]{2,1,0:T(1,128)}), s32[4,1,128]{2,1,0:T(1,128)S(1)}, u32[]{:S(2)}, u32[]{:S(2)}) %all-to-all-start.1) | async-done | bytes 2080 | tf_op jit(solution)/shard_map/all_to_all | solution.py:118
  57.2 3.6 %all-to-all-start.3 = ((bf16[8,4,16,2048]{3,2,0,1:T(8,128)(2,1)}), bf16[8,4,16,2048]{3,2,0,1:T(8,128)(2,1)S(1)}, u32[]{:S(2)}, u32[]{:S(2)}) async-start(bf16[8,4,16,2048]{3,2,0,1:T(8,128)(2,1)} %copy.88), calls=%async_computation.3 | async-start | bytes 4194304 | tf_op jit(solution)/shard_map/all_to_all | solution.py:111
  60.9 0.5 broadcast.261
  61.4 0.7 reduce.6
  62.5 42.5 %all-to-all-done.3 = bf16[8,4,16,2048]{3,2,0,1:T(8,128)(2,1)S(1)} async-done(((bf16[8,4,16,2048]{3,2,0,1:T(8,128)(2,1)}), bf16[8,4,16,2048]{3,2,0,1:T(8,128)(2,1)S(1)}, u32[]{:S(2)}, u32[]{:S(2)}) %all-to-all-start.3) | async-done | bytes 2097184 | tf_op jit(solution)/shard_map/all_to_all | solution.py:111
  105.2 0.4 fusion.27
  105.6 2.5 copy.90
  108.1 3.1 pad.14
  111.2 219.9 %while.16 = (s32[]{:T(128)}, f32[4,4,8,2048]{3,2,1,0:T(8,128)}, f32[4,4,8,2048]{3,2,1,0:T(8,128)}, f32[4]{0:T(128)S(1)}, f32[4,4]{1,0:T(4,128)S(1)}, /*index=5*/bf16[4,8,2184]{1,0,2:T(4,128)(2,1)S(1)}, s32[]{:T(128)}) while((s32[]{:T(128)}, f32[4,4,8,2048]{3,2,1,0:T(8,128)}, f32[4,4,8,2048]{3,2,1,0:T(8,128)}, ...), condition=%wide.region_8.9_spmd.clone.clone, body=%wide.region_5.8_spmd.clone.clone.sunk | while | flops 90249248 | bytes 4195677 | solution.py:85
  111.6 0.6 slice_reduce_fusion.3
  112.5 42.5 %gather_fusion = bf16[256,8,136]{1,0,2:T(8,128)(2,1)} fusion(bf16[4,8,2184]{1,0,2:T(4,128)(2,1)S(1)} %get-tuple-element.244, s32[256]{0:T(256)S(1)} %reshape.194), kind=kCustom, calls=%fused_computation.clone.clone.1 | custom fusion | bytes 1117184 | tf_op jit(solution)/shard_map/while/body/eval_jaxpr/vmap(vmap(vmap()))/gather | solution.py:44
  155.0 10.0 %multiply_reduce_fusion.2 = (f32[4,8,16,128]{3,1,2,0:T(8,128)S(1)}, f32[4,8,16,128]{3,1,2,0:T(8,128)S(1)}) fusion(bf16[4,4,16,8,136]{3,2,1,0,4:T(8,128)(2,1)} %bitcast.66, s32[4,4,16,128]{3,2,1,0:T(8,128)S(1)} %get-tuple-element.217, s32[4,4,16,128]{3,2,1,0:T(8,128)S(1)} %get-tuple-element.218, bf16[4,4,16,128]{3,2,1,0:T(8,128)(2,1)S(1)} %get-tuple-element.219, ...), kind=kOutput, calls=%fused_computation.17.clone.1 | convolution fusion | flops 89784320 | bytes 1474560 | tf_op jit(solution)/shard_map/while/body/eval_jaxpr/ghbmr,ghbrq->gmhbq/dot_general | solution.py:77
  165.0 0.8 bitcast_dynamic-update-slice_fusion.3
  166.1 0.6 slice_reduce_fusion.3
  166.9 43.2 %gather_fusion = bf16[256,8,136]{1,0,2:T(8,128)(2,1)} fusion(bf16[4,8,2184]{1,0,2:T(4,128)(2,1)S(1)} %get-tuple-element.244, s32[256]{0:T(256)S(1)} %reshape.194), kind=kCustom, calls=%fused_computation.clone.clone.1 | custom fusion | bytes 1117184 | tf_op jit(solution)/shard_map/while/body/eval_jaxpr/vmap(vmap(vmap()))/gather | solution.py:44
  210.1 10.0 %multiply_reduce_fusion.2 = (f32[4,8,16,128]{3,1,2,0:T(8,128)S(1)}, f32[4,8,16,128]{3,1,2,0:T(8,128)S(1)}) fusion(bf16[4,4,16,8,136]{3,2,1,0,4:T(8,128)(2,1)} %bitcast.66, s32[4,4,16,128]{3,2,1,0:T(8,128)S(1)} %get-tuple-element.217, s32[4,4,16,128]{3,2,1,0:T(8,128)S(1)} %get-tuple-element.218, bf16[4,4,16,128]{3,2,1,0:T(8,128)(2,1)S(1)} %get-tuple-element.219, ...), kind=kOutput, calls=%fused_computation.17.clone.1 | convolution fusion | flops 89784320 | bytes 1474560 | tf_op jit(solution)/shard_map/while/body/eval_jaxpr/ghbmr,ghbrq->gmhbq/dot_general | solution.py:77
  220.1 0.8 bitcast_dynamic-update-slice_fusion.3
  221.1 0.6 slice_reduce_fusion.3
  222.0 43.2 %gather_fusion = bf16[256,8,136]{1,0,2:T(8,128)(2,1)} fusion(bf16[4,8,2184]{1,0,2:T(4,128)(2,1)S(1)} %get-tuple-element.244, s32[256]{0:T(256)S(1)} %reshape.194), kind=kCustom, calls=%fused_computation.clone.clone.1 | custom fusion | bytes 1117184 | tf_op jit(solution)/shard_map/while/body/eval_jaxpr/vmap(vmap(vmap()))/gather | solution.py:44
  265.2 10.0 %multiply_reduce_fusion.2 = (f32[4,8,16,128]{3,1,2,0:T(8,128)S(1)}, f32[4,8,16,128]{3,1,2,0:T(8,128)S(1)}) fusion(bf16[4,4,16,8,136]{3,2,1,0,4:T(8,128)(2,1)} %bitcast.66, s32[4,4,16,128]{3,2,1,0:T(8,128)S(1)} %get-tuple-element.217, s32[4,4,16,128]{3,2,1,0:T(8,128)S(1)} %get-tuple-element.218, bf16[4,4,16,128]{3,2,1,0:T(8,128)(2,1)S(1)} %get-tuple-element.219, ...), kind=kOutput, calls=%fused_computation.17.clone.1 | convolution fusion | flops 89784320 | bytes 1474560 | tf_op jit(solution)/shard_map/while/body/eval_jaxpr/ghbmr,ghbrq->gmhbq/dot_general | solution.py:77
  275.2 0.8 bitcast_dynamic-update-slice_fusion.3
  276.2 0.6 slice_reduce_fusion.3
  277.1 43.2 %gather_fusion = bf16[256,8,136]{1,0,2:T(8,128)(2,1)} fusion(bf16[4,8,2184]{1,0,2:T(4,128)(2,1)S(1)} %get-tuple-element.244, s32[256]{0:T(256)S(1)} %reshape.194), kind=kCustom, calls=%fused_computation.clone.clone.1 | custom fusion | bytes 1117184 | tf_op jit(solution)/shard_map/while/body/eval_jaxpr/vmap(vmap(vmap()))/gather | solution.py:44
  320.3 10.0 %multiply_reduce_fusion.2 = (f32[4,8,16,128]{3,1,2,0:T(8,128)S(1)}, f32[4,8,16,128]{3,1,2,0:T(8,128)S(1)}) fusion(bf16[4,4,16,8,136]{3,2,1,0,4:T(8,128)(2,1)} %bitcast.66, s32[4,4,16,128]{3,2,1,0:T(8,128)S(1)} %get-tuple-element.217, s32[4,4,16,128]{3,2,1,0:T(8,128)S(1)} %get-tuple-element.218, bf16[4,4,16,128]{3,2,1,0:T(8,128)(2,1)S(1)} %get-tuple-element.219, ...), kind=kOutput, calls=%fused_computation.17.clone.1 | convolution fusion | flops 89784320 | bytes 1474560 | tf_op jit(solution)/shard_map/while/body/eval_jaxpr/ghbmr,ghbrq->gmhbq/dot_general | solution.py:77
  330.3 0.8 bitcast_dynamic-update-slice_fusion.3
  331.1 1.9 copy.94
  333.0 1.4 copy_multiply_fusion
  334.4 4.5 %add_bitcast_fusion = (f32[1,8,16,2048]{3,2,1,0:T(8,128)S(1)}, f32[1,8,16,2048]{3,2,1,0:T(8,128)S(1)}) fusion(f32[8,16,2048]{2,1,0:T(8,128)S(1)} %copy.94, f32[8,16,2048]{2,1,0:T(8,128)S(1)} %get-tuple-element.162), kind=kLoop, calls=%fused_computation.56 | loop fusion | flops 4194304 | bytes 4194304 | tf_op jit(solution)/shard_map/stack | solution.py:133
  339.0 1.3 collective-permute-start
  340.3 1.3 collective-permute-start.1
  341.6 4.4 %collective-permute-done = f32[2,1,16,2048]{3,2,1,0:T(8,128)S(1)} collective-permute-done((f32[2,1,16,2048]{3,2,1,0:T(8,128)S(1)}, f32[2,1,16,2048]{3,2,1,0:T(8,128)S(1)}, u32[]{:S(2)}, u32[]{:S(2)}) %collective-permute-start) | collective-permute-done | bytes 262176 | tf_op jit(solution)/shard_map/ppermute | solution.py:17
  346.0 9.6 %collective-permute-done.1 = f32[2,1,16,2048]{3,2,1,0:T(8,128)S(1)} collective-permute-done((f32[2,1,16,2048]{3,2,1,0:T(8,128)S(1)}, f32[2,1,16,2048]{3,2,1,0:T(8,128)S(1)}, u32[]{:S(2)}, u32[]{:S(2)}) %collective-permute-start.1) | collective-permute-done | bytes 262176 | tf_op jit(solution)/shard_map/ppermute | solution.py:20
  355.9 1.1 fusion.32
  (46 shorter events, 2.9 us)
Async XLA Ops:
  6.4 9.9 %all-to-all-start = ((s32[8,4,16]{2,1,0:T(4,128)}), s32[8,4,16]{2,1,0:T(4,128)S(1)}, u32[]{:S(2)}, u32[]{:S(2)}) async-start(s32[8,4,16]{2,1,0:T(4,128)} %reshape.148), calls=%async_computation | async-start | bytes 32768 | tf_op jit(solution)/shard_map/all_to_all | solution.py:119
  16.3 30.5 %all-to-all-start.2 = ((bf16[8,4,16,2048]{3,2,1,0:T(8,128)(2,1)}), bf16[8,4,16,2048]{3,2,1,0:T(8,128)(2,1)S(1)}, u32[]{:S(2)}, u32[]{:S(2)}) async-start(bf16[8,4,16,2048]{3,2,1,0:T(8,128)(2,1)} %bitcast.65), calls=%async_computation.2 | async-start | bytes 4194304 | tf_op jit(solution)/shard_map/all_to_all | solution.py:112
  46.8 10.3 %all-to-all-start.1 = ((s32[4,1,128]{2,1,0:T(1,128)}), s32[4,1,128]{2,1,0:T(1,128)S(1)}, u32[]{:S(2)}, u32[]{:S(2)}) async-start(s32[4,1,128]{2,1,0:T(1,128)} %reshape.187), calls=%async_computation.1 | async-start | bytes 4096 | tf_op jit(solution)/shard_map/all_to_all | solution.py:118
  53.2 7.6 %copy-start.2 = (f32[16]{0:T(128)S(1)}, f32[16]{0:T(128)}, u32[]{:S(2)}) copy-start(f32[16]{0:T(128)} %param.13) | copy-start | bytes 196
  57.2 47.8 %all-to-all-start.3 = ((bf16[8,4,16,2048]{3,2,0,1:T(8,128)(2,1)}), bf16[8,4,16,2048]{3,2,0,1:T(8,128)(2,1)S(1)}, u32[]{:S(2)}, u32[]{:S(2)}) async-start(bf16[8,4,16,2048]{3,2,0,1:T(8,128)(2,1)} %copy.88), calls=%async_computation.3 | async-start | bytes 4194304 | tf_op jit(solution)/shard_map/all_to_all | solution.py:111
  108.1 3.1 copy-start.1
  331.1 1.9 copy-start
  339.0 7.1 %collective-permute-start = (f32[2,1,16,2048]{3,2,1,0:T(8,128)S(1)}, f32[2,1,16,2048]{3,2,1,0:T(8,128)S(1)}, u32[]{:S(2)}, u32[]{:S(2)}) collective-permute-start(f32[2,1,16,2048]{3,2,1,0:T(8,128)S(1)} %get-tuple-element.160), channel_id=1, source_target_pairs={{0,1},{1,2},{2,3},{3,4},{4,5},{5,6},{6,7},{7,8},{8,9},{9,10},{10,1... | collective-permute-start | bytes 786440 | tf_op jit(solution)/shard_map/ppermute | solution.py:17
  340.3 15.4 %collective-permute-start.1 = (f32[2,1,16,2048]{3,2,1,0:T(8,128)S(1)}, f32[2,1,16,2048]{3,2,1,0:T(8,128)S(1)}, u32[]{:S(2)}, u32[]{:S(2)}) collective-permute-start(f32[2,1,16,2048]{3,2,1,0:T(8,128)S(1)} %get-tuple-element.161), channel_id=1, source_target_pairs={{1,0},{2,1},{3,2},{4,3},{5,4},{6,5},{7,6},{8,7},{9,8},{10,9},{11,1... | collective-permute-start | bytes 786440 | tf_op jit(solution)/shard_map/ppermute | solution.py:20
where the time goes:
time: 357 us
  local copies, waits for them, and re-layouts  193 us (54%)
  waiting for transfers between devices  86.9 us (24%)
  matrix products  40.3 us (11%)
  starting transfers between devices  20.1 us (6%)
  other arithmetic  15.6 us (4%)
    gather x8, local copies, waits for them, and re-layouts, cut_window(): return lax.dynamic_slice_in_dim(plane_rows, start_at, window_len, 1)  172 us
    all_to_all x1, waiting for transfers between devices, per_device(): lax.all_to_all(lax.all_to_all(buffer, 'inline', split_axis=0, concat_axis...  42.5 us
    dot_general x4, matrix products, per_group(): jnp.einsum('ghbmr,ghbrq->gmhbq', windows, weights, preferred_element_type...  39.9 us
    all_to_all x1, waiting for transfers between devices, per_device(): lax.all_to_all(buffer, 'inline', split_axis=0, concat_axis=0, tiled=True)  26 us
    ppermute x1, waiting for transfers between devices, with_halo(): lax.ppermute(lax.slice_in_dim(block, 0, width, axis=dim), axis, backward)  9.64 us
  transfers between devices with their start and end apart: 6, of which 6 were waited for; matrix products, arithmetic and copies ran while one was open for 2% of the time, Pallas kernels for 0%

commit v1 on v0

v1 whole, which is shorter than its diff:
```python
import functools
import math

import jax
import jax.numpy as jnp
from jax import lax
from jax.experimental import pallas as pl
from jax.experimental.pallas import tpu as pltpu
from jax.sharding import PartitionSpec as P

HALF_WIN = 4
CMP_DEV = 8
LANES = 128
F32 = jnp.float32
BF16 = jnp.bfloat16
VMEM = pl.BlockSpec(memory_space=pltpu.VMEM)
SMEM = pl.BlockSpec(memory_space=pltpu.SMEM)

LANE_GATHER = lax.GatherDimensionNumbers(
    offset_dims=(),
    collapsed_slice_dims=(1,),
    start_index_map=(1,),
    operand_batching_dims=(0,),
    start_indices_batching_dims=(0,),
)


def take_lanes(rows, index):
    return lax.gather(
        rows,
        index[..., None],
        LANE_GATHER,
        (1, 1),
        mode=lax.GatherScatterMode.PROMISE_IN_BOUNDS,
    )


def bin_kernel(kept_rows, places_ref, *refs):
    *data, kept_ref, sent_ref, member_ref = refs
    rows = member_ref.shape[0]
    per = data[0].shape[0]

    @pl.when(pl.program_id(0) == 0)
    def _():
        row = lax.broadcasted_iota(jnp.int32, member_ref.shape, 0)
        first = jnp.broadcast_to(places_ref[0:1, :], member_ref.shape)
        second = jnp.broadcast_to(places_ref[1:2, :], member_ref.shape)
        hit = (row == first) | (row == second)
        member_ref[...] = jnp.where(hit, 1.0, 0.0).astype(BF16)

    total = None
    for at, block in enumerate(data):
        part = jnp.dot(
            member_ref[:, at * per : (at + 1) * per], block[...], preferred_element_type=F32
        )
        total = part if total is None else total + part
    kept_ref[...] = total[:kept_rows]
    if kept_rows < rows:
        sent_ref[...] = total[kept_rows:].astype(BF16)
    else:
        sent_ref[...] = jnp.zeros(sent_ref.shape, BF16)


def bin_rows(places, data, starts, cols, rows, kept_rows):
    tile = math.gcd(cols, 256)
    per = data[0].shape[0]
    sent_rows = max(rows - kept_rows, 16)
    in_specs = [pl.BlockSpec(places.shape, lambda t: (0, 0))]
    for start in starts:
        in_specs.append(pl.BlockSpec((per, tile), lambda t, s=start // tile: (0, t + s)))
    return pl.pallas_call(
        functools.partial(bin_kernel, kept_rows),
        grid=(cols // tile,),
        in_specs=in_specs,
        out_specs=[
            pl.BlockSpec((kept_rows, tile), lambda t: (0, t)),
            pl.BlockSpec((sent_rows, tile), lambda t: (0, t)),
        ],
        out_shape=[
            jax.ShapeDtypeStruct((kept_rows, cols), F32),
            jax.ShapeDtypeStruct((sent_rows, cols), BF16),
        ],
        scratch_shapes=[pltpu.VMEM((rows, len(data) * per), BF16)],
        compiler_params=pltpu.CompilerParams(vmem_limit_bytes=40 * 1024 * 1024),
        cost_estimate=pl.CostEstimate(
            flops=2 * rows * len(data) * per * cols,
            bytes_accessed=2 * len(data) * per * cols + 6 * rows * cols,
            transcendentals=0,
        ),
    )(places, *data)


def exchange_rows(traces, key, classes):
    inline_count = lax.axis_size("inline")
    xline_count = lax.axis_size("xline")
    me = lax.axis_index("inline")
    me_x = lax.axis_index("xline")
    per, samples = traces.shape
    dev_rows = CMP_DEV * classes
    line_rows = xline_count * dev_rows
    block_rows = -(-(line_rows + 2 * classes) // 16) * 16
    bits = [1 << b for b in range(inline_count.bit_length() - 1)]

    def swap(value, bit):
        return lax.ppermute(value, "inline", [(i, i ^ bit) for i in range(inline_count)])

    core, others = bits[0], bits[1:]
    orders = [others, others[::-1]] if len(others) > 1 else [others]
    cols = samples // len(orders)

    pair_key = jnp.stack([key, swap(key, core)])
    mate = swap(traces, core)
    totals = []
    for part, order in enumerate(orders):
        start = part * cols
        data, starts, keys = [traces, mate], [start, start], [pair_key]
        done = core
        if order:
            first = order[0]
            done |= first
            far = swap(lax.slice_in_dim(traces, start, start + cols, axis=1), first)
            data += [far, swap(far, core)]
            starts += [0, 0]
            keys.append(swap(pair_key, first))
        rest = order[1:]
        keys = jnp.concatenate(keys).reshape(-1)
        line = keys // line_rows
        local = keys % line_rows

        def row_of(target, at):
            apart = target ^ me
            code = jnp.zeros_like(target)
            for bit in rest:
                code = code * 2 + jnp.where(apart & bit != 0, 1, 0)
            valid = (apart & done == 0) & (target >= 0) & (target < inline_count)
            return jnp.where(valid, code * block_rows + at, -1)

        own_place = row_of(line, local + classes)
        low, high = local < classes, local >= line_rows - classes
        rim_place = jnp.where(
            high,
            row_of(line + 1, local - (line_rows - classes)),
            jnp.where(low, row_of(line - 1, local + classes + line_rows), -1),
        )
        rows = block_rows << len(rest)
        half = rows // 2 if rest else rows
        kept, sent = bin_rows(jnp.stack([own_place, rim_place]), data, starts, cols, rows, half)
        for at, bit in enumerate(rest):
            if at:
                half = kept.shape[0] // 2
                sent = kept[half:].astype(BF16)
                kept = kept[:half]
            kept = kept + swap(sent, bit).astype(F32)
        totals.append(kept)
    total = jnp.concatenate(totals, axis=1) if len(totals) > 1 else totals[0]

    window = dev_rows + 2 * classes
    rounded = total.astype(BF16)
    power_of_two = xline_count & (xline_count - 1) == 0
    result = lax.dynamic_slice_in_dim(total, me_x * dev_rows, window, 0)
    for step in range(xline_count - 1, 0, -1):
        if power_of_two:
            target = me_x ^ step
            pairs = [(i, i ^ step) for i in range(xline_count)]
        else:
            target = (me_x + step) % xline_count
            pairs = [(i, (i + step) % xline_count) for i in range(xline_count)]
        block = lax.dynamic_slice_in_dim(rounded, target * dev_rows, window, 0)
        result = result + lax.ppermute(block, "xline", pairs).astype(F32)
    return result


def panel_kernel(
    classes,
    vels,
    blocks_ref,
    scale_ref,
    rows_ref,
    local_ref,
    low_ref,
    high_ref,
    stacked_ref,
    semblance_ref,
    plane_ref,
    source_ref,
    rim_source_ref,
    sum_ref,
    energy_ref,
    rim_ref,
    window_ref,
):
    count = rows_ref.shape[1] // LANES
    mids = CMP_DEV
    lane = lax.broadcasted_iota(jnp.int32, (8, LANES), 1)
    sub = lax.broadcasted_iota(jnp.int32, (8, LANES), 0)
    sub16 = lax.broadcasted_iota(jnp.int32, (16, LANES), 0)

    for at in range(count):
        block = rows_ref[:, at * LANES : (at + 1) * LANES]
        plane_ref[at] = block.astype(BF16).astype(F32)
    plane_ref[count] = jnp.zeros(plane_ref.shape[1:], F32)

    def later(here, after):
        return jnp.where(
            lane == LANES - 1,
            pltpu.roll(after, LANES - 1, 1),
            pltpu.roll(here, LANES - 1, 1),
        )

    def rim_rows(at):
        return jnp.where(
            sub < classes, plane_ref[at, 0:8, :], plane_ref[at, mids * classes : mids * classes + 8, :]
        )

    zeros = jnp.zeros((16, LANES), BF16)
    for at in range(count):
        for h in range(classes):
            here = plane_ref[at, pl.ds(classes + h, mids, stride=classes), :]
            after = plane_ref[at + 1, pl.ds(classes + h, mids, stride=classes), :]
            source_ref[h, at] = jnp.concatenate([here, later(here, after)], axis=0).astype(BF16)
        here, after = rim_rows(at), rim_rows(at + 1)
        rim_source_ref[at] = jnp.concatenate([here, later(here, after)], axis=0).astype(BF16)
    for at in (count, count + 1):
        for h in range(classes):
            source_ref[h, at] = zeros
        rim_source_ref[at] = zeros

    own_class = [sub16 % classes == h for h in range(classes)]

    def per_velocity(j, _):
        for at in range(count):
            base = [blocks_ref[(j * count + at) * classes + h] for h in range(classes)]
            total = energy = None
            for h in range(classes):
                index = jnp.broadcast_to(local_ref[j, at, h : h + 1, :], (16, LANES)).astype(
                    jnp.int16
                )
                low = jnp.broadcast_to(low_ref[j, at, h : h + 1, :], (8, LANES))
                high = jnp.broadcast_to(high_ref[j, at, h : h + 1, :], (8, LANES))
                inner = index & (LANES - 1)
                got = jnp.where(
                    index < LANES,
                    take_lanes(source_ref[h, base[h]], inner),
                    take_lanes(source_ref[h, base[h] + 1], inner),
                ).astype(F32)
                moved = low * got[:8] + high * got[8:]
                total = moved if total is None else total + moved
                energy = moved * moved if energy is None else energy + moved * moved
            sum_ref[at, pl.ds(j, mids, stride=vels), :] = total
            energy_ref[at, pl.ds(j, mids, stride=vels), :] = energy
            near = rim_source_ref[base[0]]
            far = rim_source_ref[base[0] + 1]
            for h in range(1, classes):
                near = jnp.where(own_class[h], rim_source_ref[base[h]], near)
                far = jnp.where(own_class[h], rim_source_ref[base[h] + 1], far)
            local = local_ref[j, at]
            index = jnp.concatenate([local, local], axis=0).astype(jnp.int16)
            inner = index & (LANES - 1)
            got = jnp.where(
                index < LANES, take_lanes(near, inner), take_lanes(far, inner)
            ).astype(F32)
            rim_ref[at, pl.ds(j, 8, stride=vels), :] = (
                low_ref[j, at] * got[:8] + high_ref[j, at] * got[8:]
            )
        return 0

    lax.fori_loop(0, vels, per_velocity, 0)

    shape = (mids, vels, LANES)
    rows = mids * vels
    edge = jnp.zeros(window_ref.shape[1:], BF16)
    window_ref[0] = edge
    window_ref[count + 1] = edge

    def three(low, mid, high):
        return jnp.concatenate([low, mid[:-1]], axis=0) + mid + jnp.concatenate([mid[1:], high], axis=0)

    def per_block(at, _):
        total = sum_ref[at].reshape(shape)
        rim = rim_ref[at].reshape(2, classes, vels, LANES)
        rim_sum = jnp.sum(rim, axis=1)
        rim_power = rim_sum * rim_sum
        rim_energy = jnp.sum(rim * rim, axis=1)
        power = three(rim_power[0:1], total * total, rim_power[1:2])
        energy = three(rim_energy[0:1], energy_ref[at].reshape(shape), rim_energy[1:2])
        both = jnp.concatenate([power.reshape(rows, LANES), energy.reshape(rows, LANES)], axis=0)
        top = both.astype(BF16)
        window_ref[at + 1, : 2 * rows] = top
        window_ref[at + 1, 2 * rows :] = (both - top.astype(F32)).astype(BF16)
        where = pl.ds(pl.multiple_of(at * LANES, LANES), LANES)
        for m in range(mids):
            stacked_ref[m, :, where] = (total[m] * scale_ref[m]).astype(BF16)
        return 0

    lax.fori_loop(0, count, per_block, 0)

    source = lax.broadcasted_iota(jnp.int32, (3 * LANES, LANES), 0) - LANES
    target = lax.broadcasted_iota(jnp.int32, (3 * LANES, LANES), 1)
    band = jnp.where(jnp.abs(source - target) <= HALF_WIN, 1.0, 0.0).astype(BF16)

    def per_window(at, _):
        wide = jnp.concatenate([window_ref[at], window_ref[at + 1], window_ref[at + 2]], axis=1)
        summed = jnp.dot(wide, band, preferred_element_type=F32)
        summed = summed[: 2 * rows] + summed[2 * rows :]
        numerator, denominator = summed[:rows], summed[rows:]
        where = pl.ds(pl.multiple_of(at * LANES, LANES), LANES)
        semblance = numerator / jnp.maximum(classes * denominator, 1.0)
        semblance_ref[:, :, where] = semblance.reshape(shape)
        return 0

    lax.fori_loop(0, count, per_window, 0)


def panels(rows, scale, blocks, local, low, high):
    vels, count, _, _ = local.shape
    classes = local.shape[2] // 2
    samples = rows.shape[1]
    rim = 2 * classes
    return pl.pallas_call(
        functools.partial(panel_kernel, classes, vels),
        in_specs=[SMEM, SMEM, VMEM, VMEM, VMEM, VMEM],
        out_specs=[VMEM, VMEM],
        out_shape=[
            jax.ShapeDtypeStruct((CMP_DEV, vels, samples), BF16),
            jax.ShapeDtypeStruct((CMP_DEV, vels, samples), F32),
        ],
        scratch_shapes=[
            pltpu.VMEM((count + 1, rows.shape[0], LANES), F32),
            pltpu.VMEM((classes, count + 2, 16, LANES), BF16),
            pltpu.VMEM((count + 2, 16, LANES), BF16),
            pltpu.VMEM((count, CMP_DEV * vels, LANES), F32),
            pltpu.VMEM((count, CMP_DEV * vels, LANES), F32),
            pltpu.VMEM((count, rim * vels, LANES), F32),
            pltpu.VMEM((count + 2, 4 * CMP_DEV * vels, LANES), BF16),
        ],
        compiler_params=pltpu.CompilerParams(vmem_limit_bytes=40 * 1024 * 1024),
        cost_estimate=pl.CostEstimate(
            flops=40 * CMP_DEV * vels * classes * samples,
            bytes_accessed=8 * 1024 * 1024,
            transcendentals=0,
        ),
    )(blocks, scale, rows, local, low, high)


def moveout(offsets, velocities, samples):
    count = samples // LANES
    slowness = offsets[None, :] / velocities[:, None]
    sample_time = jnp.arange(samples).astype(F32).reshape(1, count, 1, LANES)
    position = jnp.sqrt(sample_time * sample_time + (slowness * slowness)[:, None, :, None])
    floored = jnp.floor(position)
    fraction = position - floored
    sample_index = jnp.minimum(floored, float(samples)).astype(jnp.int32)
    blocks = jnp.min(sample_index, axis=-1) // LANES
    local = sample_index - (blocks * LANES)[..., None]
    low = lax.reduce_precision(1.0 - fraction, 8, 7)
    high = lax.reduce_precision(fraction, 8, 7)
    twice = [jnp.concatenate([v, v], axis=2) for v in (local, low, high)]
    return (blocks.reshape(-1), *twice)


def per_device(traces, owners, midpoint, offset_class, offsets, velocities):
    devices = lax.axis_size("inline") * lax.axis_size("xline")
    samples = traces.shape[1]
    classes = offsets.shape[0]
    key = (owners[:, 0] * CMP_DEV + midpoint) * classes + offset_class
    slots = jnp.arange(devices * CMP_DEV)
    counts = jnp.sum((key[:, None] // classes == slots[None, :]).astype(F32), axis=0)
    counts = lax.all_to_all(
        counts.reshape(devices, CMP_DEV), ("inline", "xline"), split_axis=0, concat_axis=0, tiled=True
    )
    scale = 1.0 / jnp.maximum(jnp.sum(counts, axis=0), 1.0)
    tables = moveout(offsets, velocities, samples)
    rows = exchange_rows(traces, key, classes)
    stacked, semblance = panels(rows, scale, *tables)
    return (stacked, semblance)


def solution(mesh):
    in_specs = (
        P(("inline", "xline"), None),
        P(("inline", "xline"), None),
        P(("inline", "xline")),
        P(("inline", "xline")),
        P(),
        P(),
    )
    out_specs = (P(("inline", "xline"), None, None), P(("inline", "xline"), None, None))
    return jax.shard_map(
        per_device, mesh=mesh, in_specs=in_specs, out_specs=out_specs, check_vma=False
    )
```

time: 357 us -> 81.1 us (0.23)
  local copies, waits for them, and re-layouts: 193 us -> 4.77 us
  waiting for transfers between devices: 86.9 us -> 20.2 us
  matrix products: 40.3 us -> 0 us
  Pallas kernels: 0 us -> 22.1 us
    gather x8 -> x0, local copies, waits for them, and re-layouts: 172 us -> none  [cut_window(): return lax.dynamic_slice_in_dim(plane_rows, start_at, window_len, 1)]
    all_to_all x4 -> x1, waiting for transfers between devices: 72.8 us -> 0.01 us  [per_device(): lax.all_to_all(counts.reshape(devices, CMP_DEV), ('inline', 'xline'), spl...]
    dot_general x5 -> x0, matrix products: 40.3 us -> none  [the longest x4 39.9 us: per_group(): jnp.einsum('ghbmr,ghbrq->gmhbq', windows, weights, preferred_element_type...]
    pallas_call x0 -> x3, Pallas kernels: none -> 22.1 us  [the longest x1 14.6 us: panels(): pl.pallas_call(functools.partial(panel_kernel, classes, vels), in_specs=[...]
    all_to_all x4 -> x1, starting transfers between devices: 17.5 us -> 3.97 us  [per_device(): lax.all_to_all(counts.reshape(devices, CMP_DEV), ('inline', 'xline'), spl...]
    ppermute x2 -> x13, starting transfers between devices: 2.6 us -> 15.4 us  [the longest x10 10.9 us: swap(): lax.ppermute(value, 'inline', [(i, i ^ bit) for i in range(inline_count)])]
    ppermute x2 -> x13, waiting for transfers between devices: 14.1 us -> 20.2 us  [the longest x3 12.4 us: exchange_rows(): result = result + lax.ppermute(block, 'xline', pairs).astype(F32)]
    scatter x2 -> x0, local copies, waits for them, and re-layouts: 5.82 us -> none  [the longest x1 4.43 us: per_device(): jnp.zeros((devices * capacity, samples), traces.dtype).at[slot_row]]
  transfers between devices with their start and end apart: 6 -> 14, of which waited for: 6 -> 6; matrix products, arithmetic and copies ran while one was open for 2% -> 16% of each run, Pallas kernels for 0% -> 9%
where the time goes in v1:
time: 81.1 us; the launch traced here: 80.7 us
  Pallas kernels  22.1 us (27%)
  waiting for transfers between devices  20.2 us (25%)
  starting transfers between devices  19.3 us (24%)
  other arithmetic  13.5 us (17%)
  local copies, waits for them, and re-layouts  4.77 us (6%)
  between operations  0.92 us (1%)
    pallas_call x1, Pallas kernels, panels(): pl.pallas_call(functools.partial(panel_kernel, classes, vels), in_specs=[...  14.6 us
    ppermute x3, waiting for transfers between devices, exchange_rows(): result = result + lax.ppermute(block, 'xline', pairs).astype(F32)  12.4 us
    ppermute x10, starting transfers between devices, swap(): lax.ppermute(value, 'inline', [(i, i ^ bit) for i in range(inline_count)])  10.9 us
    ppermute x10, waiting for transfers between devices, swap(): lax.ppermute(value, 'inline', [(i, i ^ bit) for i in range(inline_count)])  7.78 us
    pallas_call x2, Pallas kernels, bin_rows(): pl.pallas_call(functools.partial(bin_kernel, kept_rows), grid=(cols // ti...  7.43 us
    reduce_min x1, other arithmetic, moveout(): blocks = jnp.min(sample_index, axis=-1) // LANES  4.46 us
    ppermute x3, starting transfers between devices, exchange_rows(): result = result + lax.ppermute(block, 'xline', pairs).astype(F32)  4.45 us
    all_to_all x1, starting transfers between devices, per_device(): lax.all_to_all(counts.reshape(devices, CMP_DEV), ('inline', 'xline'), spl...  3.97 us
  transfers between devices with their start and end apart: 14, of which 6 were waited for; matrix products, arithmetic and copies ran while one was open for 16% of the time, Pallas kernels for 9%

profile of v1, /device:TPU:0, one launch (start us, length us, event | category | flops | bytes accessed | tf_op | source)
XLA Modules:
  0.0 80.7 jit_solution(11100776076579903099)
XLA Ops:
  0.6 0.7 broadcast_multiply_fusion
  1.3 0.7 and_select_fusion.10
  2.0 0.0 copy-start.7
  2.0 0.5 collective-permute-start
  2.6 0.1 collective-permute-start.2
  2.6 2.2 %fusion.26 = (bf16[256,1024]{1,0:T(8,128)(2,1)}, bf16[256,1024]{1,0:T(8,128)(2,1)}) fusion(bf16[256,2048]{1,0:T(8,128)(2,1)} %refs_0_.3), kind=kLoop, calls=%fused_computation.94 | loop fusion | bytes 2097152 | tf_op jit(solution)/shard_map/slice | solution.py:121
  4.9 2.9 %collective-permute-start.7 = (bf16[256,1024]{1,0:T(8,128)(2,1)}, bf16[256,1024]{1,0:T(8,128)(2,1)}, u32[]{:S(2)}, u32[]{:S(2)}) collective-permute-start(bf16[256,1024]{1,0:T(8,128)(2,1)} %get-tuple-element.18), channel_id=1, source_target_pairs={{0,16},{4,20},{8,24},{12,28},{16,0},{20,4},{24,8},{28,12},{1,17},{... | collective-permute-start | bytes 1572872 | tf_op jit(solution)/shard_map/ppermute | solution.py:105
  7.8 1.5 %collective-permute-start.3 = (bf16[256,1024]{1,0:T(8,128)(2,1)}, bf16[256,1024]{1,0:T(8,128)(2,1)}, u32[]{:S(2)}, u32[]{:S(2)}) collective-permute-start(bf16[256,1024]{1,0:T(8,128)(2,1)} %get-tuple-element.19), channel_id=1, source_target_pairs={{0,8},{4,12},{8,0},{12,4},{16,24},{20,28},{24,16},{28,20},{1,9},{5... | collective-permute-start | bytes 1572872 | tf_op jit(solution)/shard_map/ppermute | solution.py:105
  9.3 0.1 convert_reduce_fusion
  9.4 0.7 all_to_all.6
  10.1 4.0 %all-to-all-start = ((f32[32,1,8]{2,1,0:T(1,128)}), f32[32,1,8]{2,1,0:T(1,128)S(1)}, u32[]{:S(2)}, u32[]{:S(2)}) async-start(f32[32,1,8]{2,1,0:T(1,128)} %bitcast.1), calls=%async_computation | async-start | bytes 32768 | tf_op jit(solution)/shard_map/all_to_all | solution.py:368
  14.1 0.1 divide_multiply_fusion
  14.2 1.5 %fusion.4 = (f32[16,16,4,128]{3,2,1,0:T(4,128)}, f32[16,16,4,128]{3,2,1,0:T(4,128)}) fusion(f32[16,4]{1,0:T(8,128)S(1)} %divide_multiply_fusion, f32[16,128]{1,0:T(8,128)S(1)} %convert_multiply_fusion), kind=kLoop, calls=%fused_computation.16 | loop fusion | flops 786432 | bytes 1057024 | tf_op jit(solution)/shard_map/reduce_precision | solution.py:356
  15.7 4.5 %fusion.3 = s32[16,16,4]{2,1,0:T(8,128)S(1)} fusion(f32[16,4]{1,0:T(8,128)S(1)} %divide_multiply_fusion, f32[16,128]{1,0:T(8,128)S(1)} %convert_multiply_fusion), kind=kLoop, calls=%fused_computation.15 | loop fusion | flops 654336 | bytes 12544 | tf_op jit(solution)/shard_map/reduce_min | solution.py:353
  20.2 0.1 fusion.10
  20.3 0.1 reduce_min.12
  20.4 1.3 %fusion.2 = s32[16,16,4,128]{3,2,1,0:T(4,128)} fusion(s32[16,16,4]{2,1,0:T(8,128)S(1)} %fusion.10, f32[16,4]{1,0:T(8,128)S(1)} %divide_multiply_fusion, f32[16,128]{1,0:T(8,128)S(1)} %convert_multiply_fusion), kind=kLoop, calls=%fused_computation.14 | loop fusion | flops 655360 | bytes 536832 | tf_op jit(solution)/shard_map/sub | solution.py:354
  21.8 1.8 %collective-permute-start.1 = (s32[2,256]{1,0:T(2,128)S(1)}, s32[2,256]{1,0:T(2,128)S(1)}, u32[]{:S(2)}, u32[]{:S(2)}) collective-permute-start(s32[2,256]{1,0:T(2,128)S(1)} %pad_add_fusion.4), channel_id=1, source_target_pairs={{0,8},{4,12},{8,0},{12,4},{16,24},{20,28},{24,16},{28,20},{1,9},{5... | collective-permute-start | bytes 6152 | tf_op jit(solution)/shard_map/ppermute | solution.py:105
  23.6 1.5 %collective-permute-start.6 = (s32[2,256]{1,0:T(2,128)S(1)}, s32[2,256]{1,0:T(2,128)S(1)}, u32[]{:S(2)}, u32[]{:S(2)}) collective-permute-start(s32[2,256]{1,0:T(2,128)S(1)} %pad_add_fusion.4), channel_id=1, source_target_pairs={{0,16},{4,20},{8,24},{12,28},{16,0},{20,4},{24,8},{28,12},{1,17},{... | collective-permute-start | bytes 6152 | tf_op jit(solution)/shard_map/ppermute | solution.py:105
  25.1 1.7 %pad_maximum_fusion.1 = (f32[16,16,8,128]{3,2,1,0:T(8,128)S(1)}, f32[16,16,8,128]{3,2,1,0:T(8,128)S(1)}) fusion(f32[16,16,4,128]{3,2,1,0:T(4,128)} %get-tuple-element.24, f32[16,16,4,128]{3,2,1,0:T(4,128)S(1)} %copy-done.5), kind=kLoop, calls=%fused_computation.5 | loop fusion | flops 524288 | bytes 3145728 | tf_op jit(solution)/shard_map/concatenate | solution.py:357
  26.8 0.4 collective-permute-done.6
  27.2 0.1 and_select_fusion.3
  27.3 0.0 collective-permute-done.7.refs_2_
  27.3 0.1 collective-permute-start.8
  27.4 0.0 collective-permute-done.3.refs_2_
  27.4 0.5 collective-permute-start.4
  28.0 1.5 %collective-permute-done.8.refs_3_ = bf16[256,1024]{1,0:T(8,128)(2,1)S(1)} collective-permute-done((bf16[256,1024]{1,0:T(8,128)(2,1)}, bf16[256,1024]{1,0:T(8,128)(2,1)S(1)}, u32[]{:S(2)}, u32[]{:S(2)}) %collective-permute-start.8) | collective-permute-done | bytes 524320 | tf_op jit(solution)/shard_map/ppermute | solution.py:105
  29.5 0.0 collective-permute-done.2.refs_1_
  29.5 3.3 %shard_map.78 = (f32[144,1024]{1,0:T(8,128)S(1)}, bf16[144,1024]{1,0:T(8,128)(2,1)S(1)}) custom-call(s32[2,1024]{1,0:T(2,128)S(1)} %pad_add_fusion.2.places_ref, bf16[256,2048]{1,0:T(8,128)(2,1)S(1)} %copy-done, bf16[256,2048]{1,0:T(8,128)(2,1)} %collective-permute-done.2.refs_1_, bf16[256,1024]{1,0:T(8,128)(2,1)} %collective-permute-done.7.refs_2_, ...), custom_call_target="tpu_custom_call" | custom-call | flops 603979776 | bytes 3866624 | tf_op jit(solution)/shard_map/pallas_call | solution.py:71
  32.8 0.8 %copy-done.1 = f32[144,1024]{1,0:T(8,128)} copy-done((f32[144,1024]{1,0:T(8,128)}, f32[144,1024]{1,0:T(8,128)S(1)}, u32[]{:S(2)}) %copy-start.1) | copy-done | bytes 589848
  33.7 0.3 collective-permute-start.9
  34.0 4.1 %shard_map.77 = (f32[144,1024]{1,0:T(8,128)S(1)}, bf16[144,1024]{1,0:T(8,128)(2,1)}) custom-call(s32[2,1024]{1,0:T(2,128)S(1)} %pad_add_fusion.1.places_ref, bf16[256,2048]{1,0:T(8,128)(2,1)S(1)} %copy-done, bf16[256,2048]{1,0:T(8,128)(2,1)} %collective-permute-done.2.refs_1_, bf16[256,1024]{1,0:T(8,128)(2,1)} %collective-permute-done.3.refs_2_, ...), custom_call_target="tpu_custom_call" | custom-call | flops 603979776 | bytes 3866624 | tf_op jit(solution)/shard_map/pallas_call | solution.py:71
  38.1 0.8 %copy-done.2 = f32[144,1024]{1,0:T(8,128)} copy-done((f32[144,1024]{1,0:T(8,128)}, f32[144,1024]{1,0:T(8,128)S(1)}, u32[]{:S(2)}) %copy-start.2) | copy-done | bytes 589848
  38.9 1.8 %collective-permute-start.5 = (bf16[144,1024]{1,0:T(8,128)(2,1)}, bf16[144,1024]{1,0:T(8,128)(2,1)}, u32[]{:S(2)}, u32[]{:S(2)}) collective-permute-start(bf16[144,1024]{1,0:T(8,128)(2,1)} %get-tuple-element.7), channel_id=1, source_target_pairs={{0,16},{4,20},{8,24},{12,28},{16,0},{20,4},{24,8},{28,12},{1,17},{... | collective-permute-start | bytes 884744 | tf_op jit(solution)/shard_map/ppermute | solution.py:105
  40.7 0.2 pad_add_fusion.local_ref
  40.9 0.1 reduce_sum.19
  40.9 1.9 %collective-permute-done.9 = bf16[144,1024]{1,0:T(8,128)(2,1)} collective-permute-done((bf16[144,1024]{1,0:T(8,128)(2,1)S(1)}, bf16[144,1024]{1,0:T(8,128)(2,1)}, u32[]{:S(2)}, u32[]{:S(2)}) %collective-permute-start.9) | collective-permute-done | bytes 294944 | tf_op jit(solution)/shard_map/ppermute | solution.py:105
  42.8 1.2 %convert_add_fusion = f32[144,1024]{1,0:T(8,128)S(1)} fusion(f32[144,1024]{1,0:T(8,128)} %copy-done.1, bf16[144,1024]{1,0:T(8,128)(2,1)} %collective-permute-done.9), kind=kLoop, calls=%fused_computation.9 | loop fusion | flops 294912 | bytes 1474560 | tf_op jit(solution)/shard_map/add | solution.py:153
  44.0 4.0 %collective-permute-done.5 = bf16[144,1024]{1,0:T(8,128)(2,1)} collective-permute-done((bf16[144,1024]{1,0:T(8,128)(2,1)}, bf16[144,1024]{1,0:T(8,128)(2,1)}, u32[]{:S(2)}, u32[]{:S(2)}) %collective-permute-start.5) | collective-permute-done | bytes 294944 | tf_op jit(solution)/shard_map/ppermute | solution.py:105
  48.0 1.0 %convert_add_fusion.1 = f32[144,1024]{1,0:T(8,128)S(1)} fusion(f32[144,1024]{1,0:T(8,128)S(1)} %copy-done.3, bf16[144,1024]{1,0:T(8,128)(2,1)} %collective-permute-done.5), kind=kLoop, calls=%fused_computation.10 | loop fusion | flops 294912 | bytes 1474560 | tf_op jit(solution)/shard_map/add | solution.py:153
  49.0 0.1 fusion
  49.2 3.7 %collective-permute-start.10 = (bf16[40,2048]{1,0:T(8,128)(2,1)S(1)}, bf16[40,2048]{1,0:T(8,128)(2,1)S(1)}, u32[]{:S(2)}, u32[]{:S(2)}) collective-permute-start(bf16[40,2048]{1,0:T(8,128)(2,1)S(1)} %get-tuple-element.20), channel_id=1, source_target_pairs={{0,3},{1,2},{2,1},{3,0},{4,7},{5,6},{6,5},{7,4},{8,11},{9,10},{10,... | collective-permute-start | bytes 491528 | tf_op jit(solution)/shard_map/ppermute | solution.py:169
  52.8 0.8 collective-permute-start.12
  53.6 4.5 %collective-permute-done.10 = bf16[40,2048]{1,0:T(8,128)(2,1)S(1)} collective-permute-done((bf16[40,2048]{1,0:T(8,128)(2,1)S(1)}, bf16[40,2048]{1,0:T(8,128)(2,1)S(1)}, u32[]{:S(2)}, u32[]{:S(2)}) %collective-permute-start.10) | collective-permute-done | bytes 163872 | tf_op jit(solution)/shard_map/ppermute | solution.py:169
  58.2 7.8 %collective-permute-done.11 = bf16[40,2048]{1,0:T(8,128)(2,1)S(1)} collective-permute-done((bf16[40,2048]{1,0:T(8,128)(2,1)S(1)}, bf16[40,2048]{1,0:T(8,128)(2,1)S(1)}, u32[]{:S(2)}, u32[]{:S(2)}) %collective-permute-start.11) | collective-permute-done | bytes 163872 | tf_op jit(solution)/shard_map/ppermute | solution.py:169
  66.0 0.0 collective-permute-done.12
  66.0 0.1 fusion.8.rows_ref
  66.1 14.6 %shard_map.79 = (bf16[8,16,2048]{2,1,0:T(8,128)(2,1)}, f32[8,16,2048]{2,1,0:T(8,128)}) custom-call(s32[1024]{0:T(1024)S(1)} %add_select_fusion.1.blocks_ref, f32[8]{0:T(128)S(1)} %maximum_divide_fusion.scale_ref, f32[40,2048]{1,0:T(8,128)S(1)} %fusion.8.rows_ref, s32[16,16,8,128]{3,2,1,0:T(8,128)S(1)} %pad_add_fusion.local_ref, ...), custom_call_target="tpu_custom_call" | custom-call | flops 41943040 | bytes 8388608 | tf_op jit(solution)/shard_map/pallas_call | solution.py:319
  (30 shorter events, 0.3 us)
Async XLA Ops:
  2.0 12.1 %copy-start.6 = (f32[16]{0:T(128)S(1)}, f32[16]{0:T(128)}, u32[]{:S(2)}) copy-start(f32[16]{0:T(128)} %param.11) | copy-start | bytes 196
  2.0 12.1 %copy-start.7 = (f32[4]{0:T(128)S(1)}, f32[4]{0:T(128)}, u32[]{:S(2)}) copy-start(f32[4]{0:T(128)} %param.10) | copy-start | bytes 52
  2.0 19.7 %collective-permute-start = (s32[256]{0:T(256)S(1)}, s32[256]{0:T(256)S(1)}, u32[]{:S(2)}, u32[]{:S(2)}) collective-permute-start(s32[256]{0:T(256)S(1)} %get-tuple-element.17), channel_id=1, source_target_pairs={{0,4},{4,0},{8,12},{12,8},{16,20},{20,16},{24,28},{28,24},{1,5},{5... | collective-permute-start | bytes 3080 | tf_op jit(solution)/shard_map/ppermute | solution.py:105
  2.6 27.0 %collective-permute-start.2 = (bf16[256,2048]{1,0:T(8,128)(2,1)}, bf16[256,2048]{1,0:T(8,128)(2,1)}, u32[]{:S(2)}, u32[]{:S(2)}) collective-permute-start(bf16[256,2048]{1,0:T(8,128)(2,1)} %refs_0_.3), channel_id=1, source_target_pairs={{0,4},{4,0},{8,12},{12,8},{16,20},{20,16},{24,28},{28,24},{1,5},{5... | collective-permute-start | bytes 3145736 | tf_op jit(solution)/shard_map/ppermute | solution.py:105
  4.9 22.5 %collective-permute-start.7 = (bf16[256,1024]{1,0:T(8,128)(2,1)}, bf16[256,1024]{1,0:T(8,128)(2,1)}, u32[]{:S(2)}, u32[]{:S(2)}) collective-permute-start(bf16[256,1024]{1,0:T(8,128)(2,1)} %get-tuple-element.18), channel_id=1, source_target_pairs={{0,16},{4,20},{8,24},{12,28},{16,0},{20,4},{24,8},{28,12},{1,17},{... | collective-permute-start | bytes 1572872 | tf_op jit(solution)/shard_map/ppermute | solution.py:105
  7.8 19.6 %collective-permute-start.3 = (bf16[256,1024]{1,0:T(8,128)(2,1)}, bf16[256,1024]{1,0:T(8,128)(2,1)}, u32[]{:S(2)}, u32[]{:S(2)}) collective-permute-start(bf16[256,1024]{1,0:T(8,128)(2,1)} %get-tuple-element.19), channel_id=1, source_target_pairs={{0,8},{4,12},{8,0},{12,4},{16,24},{20,28},{24,16},{28,20},{1,9},{5... | collective-permute-start | bytes 1572872 | tf_op jit(solution)/shard_map/ppermute | solution.py:105
  10.1 30.8 %all-to-all-start = ((f32[32,1,8]{2,1,0:T(1,128)}), f32[32,1,8]{2,1,0:T(1,128)S(1)}, u32[]{:S(2)}, u32[]{:S(2)}) async-start(f32[32,1,8]{2,1,0:T(1,128)} %bitcast.1), calls=%async_computation | async-start | bytes 32768 | tf_op jit(solution)/shard_map/all_to_all | solution.py:368
  20.4 4.7 %copy-start.5 = (f32[16,16,4,128]{3,2,1,0:T(4,128)S(1)}, f32[16,16,4,128]{3,2,1,0:T(4,128)}, u32[]{:S(2)}) copy-start(f32[16,16,4,128]{3,2,1,0:T(4,128)} %get-tuple-element.23) | copy-start | bytes 1572868
  21.8 5.0 %collective-permute-start.1 = (s32[2,256]{1,0:T(2,128)S(1)}, s32[2,256]{1,0:T(2,128)S(1)}, u32[]{:S(2)}, u32[]{:S(2)}) collective-permute-start(s32[2,256]{1,0:T(2,128)S(1)} %pad_add_fusion.4), channel_id=1, source_target_pairs={{0,8},{4,12},{8,0},{12,4},{16,24},{20,28},{24,16},{28,20},{1,9},{5... | collective-permute-start | bytes 6152 | tf_op jit(solution)/shard_map/ppermute | solution.py:105
  23.6 3.6 %collective-permute-start.6 = (s32[2,256]{1,0:T(2,128)S(1)}, s32[2,256]{1,0:T(2,128)S(1)}, u32[]{:S(2)}, u32[]{:S(2)}) collective-permute-start(s32[2,256]{1,0:T(2,128)S(1)} %pad_add_fusion.4), channel_id=1, source_target_pairs={{0,16},{4,20},{8,24},{12,28},{16,0},{20,4},{24,8},{28,12},{1,17},{... | collective-permute-start | bytes 6152 | tf_op jit(solution)/shard_map/ppermute | solution.py:105
  25.1 4.5 %copy-start = (bf16[256,2048]{1,0:T(8,128)(2,1)S(1)}, bf16[256,2048]{1,0:T(8,128)(2,1)}, u32[]{:S(2)}) copy-start(bf16[256,2048]{1,0:T(8,128)(2,1)} %refs_0_.3) | copy-start | bytes 3145732
  27.3 2.2 %collective-permute-start.8 = (bf16[256,1024]{1,0:T(8,128)(2,1)}, bf16[256,1024]{1,0:T(8,128)(2,1)S(1)}, u32[]{:S(2)}, u32[]{:S(2)}) collective-permute-start(bf16[256,1024]{1,0:T(8,128)(2,1)} %collective-permute-done.7.refs_2_), channel_id=1, source_target_pairs={{0,4},{4,0},{8,12},{12,8},{16,20},{20,16},{24,28},{28,24},{1,5},{5... | collective-permute-start | bytes 1572872 | tf_op jit(solution)/shard_map/ppermute | solution.py:105
  27.4 6.5 %collective-permute-start.4 = (bf16[256,1024]{1,0:T(8,128)(2,1)}, bf16[256,1024]{1,0:T(8,128)(2,1)S(1)}, u32[]{:S(2)}, u32[]{:S(2)}) collective-permute-start(bf16[256,1024]{1,0:T(8,128)(2,1)} %collective-permute-done.3.refs_2_), channel_id=1, source_target_pairs={{0,4},{4,0},{8,12},{12,8},{16,20},{20,16},{24,28},{28,24},{1,5},{5... | collective-permute-start | bytes 1572872 | tf_op jit(solution)/shard_map/ppermute | solution.py:105
  32.8 0.8 %copy-start.1 = (f32[144,1024]{1,0:T(8,128)}, f32[144,1024]{1,0:T(8,128)S(1)}, u32[]{:S(2)}) copy-start(f32[144,1024]{1,0:T(8,128)S(1)} %get-tuple-element.8) | copy-start | bytes 1769476
  33.7 9.1 %collective-permute-start.9 = (bf16[144,1024]{1,0:T(8,128)(2,1)S(1)}, bf16[144,1024]{1,0:T(8,128)(2,1)}, u32[]{:S(2)}, u32[]{:S(2)}) collective-permute-start(bf16[144,1024]{1,0:T(8,128)(2,1)S(1)} %get-tuple-element.9), channel_id=1, source_target_pairs={{0,8},{4,12},{8,0},{12,4},{16,24},{20,28},{24,16},{28,20},{1,9},{5... | collective-permute-start | bytes 884744 | tf_op jit(solution)/shard_map/ppermute | solution.py:105
  33.9 6.7 %copy-start.4 = (s32[16,16,4,128]{3,2,1,0:T(4,128)S(1)}, s32[16,16,4,128]{3,2,1,0:T(4,128)}, u32[]{:S(2)}) copy-start(s32[16,16,4,128]{3,2,1,0:T(4,128)} %fusion.2) | copy-start | bytes 1572868
  38.1 0.8 %copy-start.2 = (f32[144,1024]{1,0:T(8,128)}, f32[144,1024]{1,0:T(8,128)S(1)}, u32[]{:S(2)}) copy-start(f32[144,1024]{1,0:T(8,128)S(1)} %get-tuple-element.6) | copy-start | bytes 1769476
  38.9 9.1 %collective-permute-start.5 = (bf16[144,1024]{1,0:T(8,128)(2,1)}, bf16[144,1024]{1,0:T(8,128)(2,1)}, u32[]{:S(2)}, u32[]{:S(2)}) collective-permute-start(bf16[144,1024]{1,0:T(8,128)(2,1)} %get-tuple-element.7), channel_id=1, source_target_pairs={{0,16},{4,20},{8,24},{12,28},{16,0},{20,4},{24,8},{28,12},{1,17},{... | collective-permute-start | bytes 884744 | tf_op jit(solution)/shard_map/ppermute | solution.py:105
  40.9 7.1 %copy-start.3 = (f32[144,1024]{1,0:T(8,128)S(1)}, f32[144,1024]{1,0:T(8,128)}, u32[]{:S(2)}) copy-start(f32[144,1024]{1,0:T(8,128)} %copy-done.2) | copy-start | bytes 1769476
  49.2 9.0 %collective-permute-start.10 = (bf16[40,2048]{1,0:T(8,128)(2,1)S(1)}, bf16[40,2048]{1,0:T(8,128)(2,1)S(1)}, u32[]{:S(2)}, u32[]{:S(2)}) collective-permute-start(bf16[40,2048]{1,0:T(8,128)(2,1)S(1)} %get-tuple-element.20), channel_id=1, source_target_pairs={{0,3},{1,2},{2,1},{3,0},{4,7},{5,6},{6,5},{7,4},{8,11},{9,10},{10,... | collective-permute-start | bytes 491528 | tf_op jit(solution)/shard_map/ppermute | solution.py:169
  52.8 13.2 %collective-permute-start.11 = (bf16[40,2048]{1,0:T(8,128)(2,1)S(1)}, bf16[40,2048]{1,0:T(8,128)(2,1)S(1)}, u32[]{:S(2)}, u32[]{:S(2)}) collective-permute-start(bf16[40,2048]{1,0:T(8,128)(2,1)S(1)} %get-tuple-element.22), channel_id=1, source_target_pairs={{0,2},{1,3},{2,0},{3,1},{4,6},{5,7},{6,4},{7,5},{8,10},{9,11},{10,... | collective-permute-start | bytes 491528 | tf_op jit(solution)/shard_map/ppermute | solution.py:169
  52.8 13.2 %collective-permute-start.12 = (bf16[40,2048]{1,0:T(8,128)(2,1)S(1)}, bf16[40,2048]{1,0:T(8,128)(2,1)S(1)}, u32[]{:S(2)}, u32[]{:S(2)}) collective-permute-start(bf16[40,2048]{1,0:T(8,128)(2,1)S(1)} %get-tuple-element.21), channel_id=1, source_target_pairs={{0,1},{1,0},{2,3},{3,2},{4,5},{5,4},{6,7},{7,6},{8,9},{9,8},{10,11... | collective-permute-start | bytes 491528 | tf_op jit(solution)/shard_map/ppermute | solution.py:169

commit v2 on v1

v2 whole, which is shorter than its diff:
```python
import functools
import math

import jax
import jax.numpy as jnp
from jax import lax
from jax.experimental import pallas as pl
from jax.experimental.pallas import tpu as pltpu
from jax.sharding import PartitionSpec as P

HALF_WIN = 4
CMP_DEV = 8
LANES = 128
F32 = jnp.float32
BF16 = jnp.bfloat16
VMEM = pl.BlockSpec(memory_space=pltpu.VMEM)
SMEM = pl.BlockSpec(memory_space=pltpu.SMEM)

LANE_GATHER = lax.GatherDimensionNumbers(
    offset_dims=(),
    collapsed_slice_dims=(1,),
    start_index_map=(1,),
    operand_batching_dims=(0,),
    start_indices_batching_dims=(0,),
)


def take_lanes(rows, index):
    return lax.gather(
        rows,
        index[..., None],
        LANE_GATHER,
        (1, 1),
        mode=lax.GatherScatterMode.PROMISE_IN_BOUNDS,
    )


def bin_kernel(kept_rows, member_ref, *refs):
    *data, kept_ref, sent_ref = refs
    per, cols = data[0].shape
    tile = math.gcd(cols, 256)
    for start in range(0, cols, tile):
        where = slice(start, start + tile)
        total = None
        for at, block in enumerate(data):
            part = jnp.dot(
                member_ref[:, at * per : (at + 1) * per],
                block[:, where],
                preferred_element_type=F32,
            )
            total = part if total is None else total + part
        kept_ref[:, where] = total[:kept_rows]
        if kept_rows < total.shape[0]:
            sent_ref[:, where] = total[kept_rows:].astype(BF16)
        else:
            sent_ref[:, where] = jnp.zeros((sent_ref.shape[0], tile), BF16)


def bin_rows(member, data, starts, cols, kept_rows):
    rows = member.shape[0]
    per = data[0].shape[0]
    sent_rows = max(rows - kept_rows, 16)
    in_specs = [pl.BlockSpec(member.shape, lambda t: (0, 0))]
    for start in starts:
        in_specs.append(pl.BlockSpec((per, cols), lambda t, s=start // cols: (0, s)))
    return pl.pallas_call(
        functools.partial(bin_kernel, kept_rows),
        grid=(1,),
        in_specs=in_specs,
        out_specs=[
            pl.BlockSpec((kept_rows, cols), lambda t: (0, 0)),
            pl.BlockSpec((sent_rows, cols), lambda t: (0, 0)),
        ],
        out_shape=[
            jax.ShapeDtypeStruct((kept_rows, cols), F32),
            jax.ShapeDtypeStruct((sent_rows, cols), BF16),
        ],
        compiler_params=pltpu.CompilerParams(vmem_limit_bytes=40 * 1024 * 1024),
        cost_estimate=pl.CostEstimate(
            flops=2 * rows * len(data) * per * cols,
            bytes_accessed=2 * len(data) * per * cols + 6 * rows * cols,
            transcendentals=0,
        ),
    )(member, *data)


class Plan:
    def __init__(self, traces, key, classes):
        self.inline = lax.axis_size("inline")
        self.xline = lax.axis_size("xline")
        self.me = lax.axis_index("inline")
        self.me_x = lax.axis_index("xline")
        self.classes = classes
        self.traces = traces
        self.dev_rows = CMP_DEV * classes
        self.line_rows = self.xline * self.dev_rows
        self.block_rows = -(-(self.line_rows + 2 * classes) // 16) * 16
        bits = [1 << b for b in range(self.inline.bit_length() - 1)]
        self.core, others = bits[0], bits[1:]
        self.orders = [others, others[::-1]] if len(others) > 1 else [others]
        self.mate = self.swap(traces, self.core)
        pair = jnp.stack([key, self.swap(key, self.core)])
        self.keys = []
        for order in self.orders:
            keys = [pair] + [self.swap(pair, bit) for bit in order[:1]]
            self.keys.append(jnp.concatenate(keys).reshape(-1))
        self.members = [self.member(at) for at in range(len(self.orders))]

    def swap(self, value, bit):
        return lax.ppermute(value, "inline", [(i, i ^ bit) for i in range(self.inline)])

    def code_of(self, at, target):
        order = self.orders[at]
        apart = target ^ self.me
        code = jnp.zeros_like(target)
        done = self.core
        for place, bit in enumerate(order):
            if place:
                code = code * 2 + jnp.where(apart & bit != 0, 1, 0)
            else:
                done |= bit
        valid = (apart & done == 0) & (target >= 0) & (target < self.inline)
        return jnp.where(valid, code, -1)

    def codes(self, at):
        return 1 << max(len(self.orders[at]) - 1, 0)

    def member(self, at):
        keys = self.keys[at]
        classes, line_rows = self.classes, self.line_rows
        line, local = keys // line_rows, keys % line_rows

        def row_of(target, row):
            code = self.code_of(at, target)
            return jnp.where(code >= 0, code * self.block_rows + row, -1)

        own = row_of(line, local + classes)
        rim = jnp.where(
            local >= line_rows - classes,
            row_of(line + 1, local - (line_rows - classes)),
            jnp.where(local < classes, row_of(line - 1, local + classes + line_rows), -1),
        )
        row = jnp.arange(self.codes(at) * self.block_rows)[:, None]
        return ((row == own[None, :]) | (row == rim[None, :])).astype(BF16)

    def reduce_lines(self, at, kept, sent):
        for place, bit in enumerate(self.orders[at][1:]):
            if place:
                half = kept.shape[0] // 2
                kept, sent = kept[:half], kept[half:].astype(sent.dtype)
            kept = kept + self.swap(sent, bit).astype(F32)
        return kept

    def reduce_xline(self, total, sent, stride, window):
        power_of_two = self.xline & (self.xline - 1) == 0
        result = lax.dynamic_slice_in_dim(total, self.me_x * stride, window, 0)
        for step in range(self.xline - 1, 0, -1):
            if power_of_two:
                target = self.me_x ^ step
                pairs = [(i, i ^ step) for i in range(self.xline)]
            else:
                target = (self.me_x + step) % self.xline
                pairs = [(i, (i + step) % self.xline) for i in range(self.xline)]
            block = lax.dynamic_slice_in_dim(sent, target * stride, window, 0)
            result = result + lax.ppermute(block, "xline", pairs).astype(F32)
        return result

    def raw(self, start, cols):
        width = cols // len(self.orders)
        parts = []
        for at, order in enumerate(self.orders):
            begin = start + at * width
            data, starts = [self.traces, self.mate], [begin, begin]
            if order:
                far = self.swap(lax.slice_in_dim(self.traces, begin, begin + width, axis=1), order[0])
                data += [far, self.swap(far, self.core)]
                starts += [0, 0]
            parts.append((data, starts, width))
        return parts

    def rows(self, parts):
        totals = []
        for at, (data, starts, width) in enumerate(parts):
            rows = self.members[at].shape[0]
            kept_rows = rows // 2 if len(self.orders[at]) > 1 else rows
            kept, sent = bin_rows(self.members[at], data, starts, width, kept_rows)
            totals.append(self.reduce_lines(at, kept, sent))
        total = jnp.concatenate(totals, axis=1) if len(totals) > 1 else totals[0]
        window = self.dev_rows + 2 * self.classes
        return self.reduce_xline(total, total.astype(BF16), self.dev_rows, window)

    def fold(self):
        keys = self.keys[0]
        line, local = keys // self.line_rows, keys % self.line_rows
        slots = self.xline * CMP_DEV
        code = self.code_of(0, line)
        slot = jnp.where(code >= 0, code * slots + local // self.classes, -1)
        every = jnp.arange(self.codes(0) * slots)
        counts = jnp.sum((slot[None, :] == every[:, None]).astype(F32), axis=1)
        half = counts.shape[0] // 2 if self.codes(0) > 1 else counts.shape[0]
        counts = self.reduce_lines(0, counts[:half], counts[half:])
        return self.reduce_xline(counts, counts, CMP_DEV, CMP_DEV)


def panel_kernel(classes, vels, first, last, count, chunks, *refs):
    blocks_ref, scale_ref = refs[:2]
    rows_refs = refs[2 : 2 + chunks]
    local_ref, low_ref, high_ref = refs[2 + chunks : 5 + chunks]
    at = 5 + chunks
    if last < count:
        later_ref = refs[at]
        at += 3
    stacked_out, semblance_out = refs[at : at + 2]
    at += 2
    if first > 0:
        carry_ref = refs[at]
        at += 1
    (
        plane_ref,
        source_ref,
        rim_source_ref,
        sum_ref,
        energy_ref,
        rim_ref,
        window_ref,
        stacked_ref,
        semblance_ref,
        copies,
    ) = refs[at:]
    mids = CMP_DEV
    span = last - first
    held = count - first
    lane = lax.broadcasted_iota(jnp.int32, (8, LANES), 1)
    sub = lax.broadcasted_iota(jnp.int32, (8, LANES), 0)
    sub16 = lax.broadcasted_iota(jnp.int32, (16, LANES), 0)

    block_at = 0
    for rows_ref in rows_refs:
        for inner in range(rows_ref.shape[1] // LANES):
            block = rows_ref[:, inner * LANES : (inner + 1) * LANES]
            plane_ref[block_at] = block.astype(BF16).astype(F32)
            block_at += 1
    plane_ref[held] = jnp.zeros(plane_ref.shape[1:], F32)

    def later(here, after):
        return jnp.where(
            lane == LANES - 1,
            pltpu.roll(after, LANES - 1, 1),
            pltpu.roll(here, LANES - 1, 1),
        )

    def rim_rows(at):
        return jnp.where(
            sub < classes, plane_ref[at, 0:8, :], plane_ref[at, mids * classes : mids * classes + 8, :]
        )

    zeros = jnp.zeros((16, LANES), BF16)
    for at in range(held):
        for h in range(classes):
            here = plane_ref[at, pl.ds(classes + h, mids, stride=classes), :]
            after = plane_ref[at + 1, pl.ds(classes + h, mids, stride=classes), :]
            source_ref[h, at] = jnp.concatenate([here, later(here, after)], axis=0).astype(BF16)
        here, after = rim_rows(at), rim_rows(at + 1)
        rim_source_ref[at] = jnp.concatenate([here, later(here, after)], axis=0).astype(BF16)
    for at in (held, held + 1):
        for h in range(classes):
            source_ref[h, at] = zeros
        rim_source_ref[at] = zeros

    own_class = [sub16 % classes == h for h in range(classes)]
    group = 2 * classes

    def per_velocity(j, _):
        for at in range(span):
            where = slice(at * LANES, (at + 1) * LANES)
            base = [blocks_ref[(j * classes + h) * count + first + at] - first for h in range(classes)]
            total = energy = None
            for h in range(classes):
                row = slice(h, h + 1)
                index = jnp.broadcast_to(local_ref[j, row, where], (16, LANES)).astype(jnp.int16)
                low = jnp.broadcast_to(low_ref[j, row, where], (8, LANES))
                high = jnp.broadcast_to(high_ref[j, row, where], (8, LANES))
                inner = index & (LANES - 1)
                got = jnp.where(
                    index < LANES,
                    take_lanes(source_ref[h, base[h]], inner),
                    take_lanes(source_ref[h, base[h] + 1], inner),
                ).astype(F32)
                moved = low * got[:8] + high * got[8:]
                total = moved if total is None else total + moved
                energy = moved * moved if energy is None else energy + moved * moved
            sum_ref[at, pl.ds(j, mids, stride=vels), :] = total
            energy_ref[at, pl.ds(j, mids, stride=vels), :] = energy
            near = rim_source_ref[base[0]]
            far = rim_source_ref[base[0] + 1]
            for h in range(1, classes):
                near = jnp.where(own_class[h], rim_source_ref[base[h]], near)
                far = jnp.where(own_class[h], rim_source_ref[base[h] + 1], far)
            local = local_ref[j, :, where]
            index = jnp.concatenate([local, local], axis=0).astype(jnp.int16)
            inner = index & (LANES - 1)
            got = jnp.where(
                index < LANES, take_lanes(near, inner), take_lanes(far, inner)
            ).astype(F32)
            rim_ref[at, pl.ds(j, group, stride=vels), :] = (
                low_ref[j, :, where] * got[:8] + high_ref[j, :, where] * got[8:]
            )
        return 0

    lax.fori_loop(0, vels, per_velocity, 0)

    shape = (mids, vels, LANES)
    rows = mids * vels
    edge = jnp.zeros(window_ref.shape[1:], BF16)
    window_ref[0] = edge
    if last < count:
        window_ref[span + 1] = later_ref[0]
        window_ref[span + 2] = later_ref[1]
    else:
        window_ref[span + 1] = edge

    def three(low, mid, high):
        return jnp.concatenate([low, mid[:-1]], axis=0) + mid + jnp.concatenate([mid[1:], high], axis=0)

    def per_block(at, _):
        total = sum_ref[at].reshape(shape)
        rim = rim_ref[at].reshape(2, classes, vels, LANES)
        rim_sum = jnp.sum(rim, axis=1)
        rim_power = rim_sum * rim_sum
        rim_energy = jnp.sum(rim * rim, axis=1)
        power = three(rim_power[0:1], total * total, rim_power[1:2])
        energy = three(rim_energy[0:1], energy_ref[at].reshape(shape), rim_energy[1:2])
        window_ref[at + 1, :rows] = power.reshape(rows, LANES).astype(BF16)
        window_ref[at + 1, rows:] = energy.reshape(rows, LANES).astype(BF16)
        where = pl.ds(pl.multiple_of(at * LANES, LANES), LANES)
        for m in range(mids):
            stacked_ref[m, :, where] = (total[m] * scale_ref[m]).astype(BF16)
        return 0

    lax.fori_loop(0, span, per_block, 0)
    stacked_copy = pltpu.make_async_copy(
        stacked_ref, stacked_out.at[:, :, first * LANES : last * LANES], copies.at[0]
    )
    stacked_copy.start()

    def band(blocks):
        shape = ((blocks + 2) * LANES, blocks * LANES)
        source = lax.broadcasted_iota(jnp.int32, shape, 0) - LANES
        target = lax.broadcasted_iota(jnp.int32, shape, 1)
        return jnp.where(jnp.abs(source - target) <= HALF_WIN, 1.0, 0.0).astype(BF16)

    begin = 0 if first == 0 else 1
    end = span + 1 if last < count else span
    wide = band(2)
    narrow = band(1)
    at = begin
    while at < end:
        blocks = min(2, end - at)
        values = jnp.concatenate([window_ref[at + i] for i in range(blocks + 2)], axis=1)
        summed = jnp.dot(values, wide if blocks == 2 else narrow, preferred_element_type=F32)
        semblance = summed[:rows] / jnp.maximum(classes * summed[rows:], 1.0)
        semblance_ref[:, :, (at - begin) * LANES : (at - begin + blocks) * LANES] = semblance.reshape(
            mids, vels, blocks * LANES
        )
        at += blocks
    semblance_copy = pltpu.make_async_copy(
        semblance_ref,
        semblance_out.at[:, :, (first + begin) * LANES : (first + end) * LANES],
        copies.at[1],
    )
    semblance_copy.start()
    if first > 0:
        carry_ref[0] = window_ref[1]
        carry_ref[1] = window_ref[2]
    stacked_copy.wait()
    semblance_copy.wait()


def panels(first, last, count, classes, vels, scale, blocks, tables, rows, later):
    span = last - first
    held = count - first
    samples = count * LANES
    group = 2 * classes
    window_rows = 2 * CMP_DEV * vels
    done = span - (first > 0) + (last < count)
    outs = [
        jax.ShapeDtypeStruct((CMP_DEV, vels, samples), BF16),
        jax.ShapeDtypeStruct((CMP_DEV, vels, samples), F32),
    ]
    specs = [pl.BlockSpec(memory_space=pl.ANY)] * 2
    if first > 0:
        outs.append(jax.ShapeDtypeStruct((2, window_rows, LANES), BF16))
        specs.append(VMEM)
    operands = [blocks, scale, *rows, *tables]
    in_specs = [SMEM, SMEM] + [VMEM] * (len(rows) + len(tables))
    aliases = {}
    if later is not None:
        stacked, semblance, carry = later
        aliases = {len(operands) + 1: 0, len(operands) + 2: 1}
        operands += [carry, stacked, semblance]
        in_specs += [VMEM, pl.BlockSpec(memory_space=pl.ANY), pl.BlockSpec(memory_space=pl.ANY)]
    return pl.pallas_call(
        functools.partial(panel_kernel, classes, vels, first, last, count, len(rows)),
        in_specs=in_specs,
        out_specs=specs,
        out_shape=outs,
        input_output_aliases=aliases,
        scratch_shapes=[
            pltpu.VMEM((held + 1, rows[0].shape[0], LANES), F32),
            pltpu.VMEM((classes, held + 2, 16, LANES), BF16),
            pltpu.VMEM((held + 2, 16, LANES), BF16),
            pltpu.VMEM((span, CMP_DEV * vels, LANES), F32),
            pltpu.VMEM((span, CMP_DEV * vels, LANES), F32),
            pltpu.VMEM((span, group * vels, LANES), F32),
            pltpu.VMEM((span + 3, window_rows, LANES), BF16),
            pltpu.VMEM((CMP_DEV, vels, span * LANES), BF16),
            pltpu.VMEM((CMP_DEV, vels, done * LANES), F32),
            pltpu.SemaphoreType.DMA((2,)),
        ],
        compiler_params=pltpu.CompilerParams(vmem_limit_bytes=40 * 1024 * 1024),
        cost_estimate=pl.CostEstimate(
            flops=40 * CMP_DEV * vels * classes * span * LANES,
            bytes_accessed=(1 + span) * 512 * 1024,
            transcendentals=0,
        ),
    )(*operands)


def first_blocks(offsets, velocities, count):
    slowness = (offsets[None, :] / velocities[:, None]).reshape(-1, 1)
    sample_time = (jnp.arange(count) * LANES).astype(F32)[None, :]
    position = jnp.sqrt(sample_time * sample_time + slowness * slowness)
    index = jnp.floor(position - 0.01).astype(jnp.int32)
    return jnp.minimum(index, count * LANES) // LANES


def moveout(offsets, velocities, blocks, samples, start, stop):
    vels, classes = velocities.shape[0], offsets.shape[0]
    slowness = offsets[None, :] / velocities[:, None]
    slowness = jnp.concatenate([slowness, slowness], axis=1).reshape(-1, 1)
    sample_time = jnp.arange(start, stop).astype(F32)[None, :]
    position = jnp.sqrt(sample_time * sample_time + slowness * slowness)
    floored = jnp.floor(position)
    fraction = position - floored
    sample_index = jnp.minimum(floored, float(samples)).astype(jnp.int32)
    base = blocks.reshape(vels, classes, -1)[:, :, start // LANES : stop // LANES] * LANES
    base = jnp.concatenate([base, base], axis=1).reshape(vels * 2 * classes, -1)
    local = sample_index - jnp.repeat(base, LANES, axis=1)
    low = lax.reduce_precision(1.0 - fraction, 8, 7)
    high = lax.reduce_precision(fraction, 8, 7)
    return [v.reshape(vels, 2 * classes, stop - start) for v in (local, low, high)]


def per_device(traces, owners, midpoint, offset_class, offsets, velocities):
    samples = traces.shape[1]
    classes, vels = offsets.shape[0], velocities.shape[0]
    count = samples // LANES
    key = (owners[:, 0] * CMP_DEV + midpoint) * classes + offset_class
    plan = Plan(traces, key, classes)
    cuts = [0, samples // 2, samples]
    chunks = list(zip(cuts[:-1], cuts[1:]))[::-1]
    raw = [plan.raw(start, stop - start) for start, stop in chunks]
    scale = 1.0 / jnp.maximum(plan.fold(), 1.0)
    blocks = first_blocks(offsets, velocities, count)
    rows = []
    out = None
    for (start, stop), parts in zip(chunks, raw):
        tables = moveout(offsets, velocities, blocks, samples, start, stop)
        rows.insert(0, plan.rows(parts))
        out = panels(
            start // LANES,
            stop // LANES,
            count,
            classes,
            vels,
            scale,
            blocks.reshape(-1),
            tables,
            rows,
            out,
        )
    return (out[0], out[1])


def solution(mesh):
    in_specs = (
        P(("inline", "xline"), None),
        P(("inline", "xline"), None),
        P(("inline", "xline")),
        P(("inline", "xline")),
        P(),
        P(),
    )
    out_specs = (P(("inline", "xline"), None, None), P(("inline", "xline"), None, None))
    return jax.shard_map(
        per_device, mesh=mesh, in_specs=in_specs, out_specs=out_specs, check_vma=False
    )
```

time: 81.1 us -> 72.1 us (0.89); the launches traced: 80.7 us -> 70.9 us
  starting transfers between devices: 19.3 us -> 29.3 us
  other arithmetic: 13.5 us -> 6.08 us
  waiting for transfers between devices: 20.2 us -> 14.2 us
  Pallas kernels: 22.1 us -> 16.2 us
    ppermute x13 -> x26, starting transfers between devices: 15.4 us -> 29.3 us  [the longest x9 15.5 us: reduce_xline(): result = result + lax.ppermute(block, 'xline', pairs).astype(F32)]
    ppermute x13 -> x26, waiting for transfers between devices: 20.2 us -> 14.2 us  [the longest x17 10.8 us: swap(): lax.ppermute(value, 'inline', [(i, i ^ bit) for i in range(self.inline)])]
    pallas_call x3 -> x6, Pallas kernels: 22.1 us -> 16.2 us  [the longest x2 13.3 us: panels(): pl.pallas_call(functools.partial(panel_kernel, classes, vels, first, last...]
    reduce_min x1 -> x0, other arithmetic: 4.46 us -> none  [moveout(): blocks = jnp.min(sample_index, axis=-1) // LANES]
    all_to_all x1 -> x0, starting transfers between devices: 3.97 us -> none  [per_device(): lax.all_to_all(counts.reshape(devices, CMP_DEV), ('inline', 'xline'), spl...]
    concatenate x2 -> x0, other arithmetic: 1.83 us -> none  [moveout(): twice = [jnp.concatenate([v, v], axis=2) for v in (local, low, high)]]
    unnamed x18 -> x20, local copies, waits for them, and re-layouts: 1.67 us -> 0.04 us
    add x3 -> x8, other arithmetic: 2.31 us -> 0.92 us  [the longest x1 0.7 us: per_device(): key = (owners[:, 0] * CMP_DEV + midpoint) * classes + offset_class]
  transfers between devices with their start and end apart: 14 -> 26, of which waited for: 6 -> 6; matrix products, arithmetic and copies ran while one was open for 16% -> 12% of each run, Pallas kernels for 9% -> 13%
where the time goes in v2:
time: 72.1 us; the launch traced here: 70.9 us
  starting transfers between devices  29.3 us (41%)
  Pallas kernels  16.2 us (22%)
  waiting for transfers between devices  14.2 us (20%)
  other arithmetic  6.08 us (8%)
  local copies, waits for them, and re-layouts  4.06 us (6%)
  between operations  1.01 us (1%)
    ppermute x9, starting transfers between devices, reduce_xline(): result = result + lax.ppermute(block, 'xline', pairs).astype(F32)  15.5 us
    ppermute x17, starting transfers between devices, swap(): lax.ppermute(value, 'inline', [(i, i ^ bit) for i in range(self.inline)])  13.8 us
    pallas_call x2, Pallas kernels, panels(): pl.pallas_call(functools.partial(panel_kernel, classes, vels, first, last...  13.3 us
    ppermute x17, waiting for transfers between devices, swap(): lax.ppermute(value, 'inline', [(i, i ^ bit) for i in range(self.inline)])  10.8 us
    ppermute x9, waiting for transfers between devices, reduce_xline(): result = result + lax.ppermute(block, 'xline', pairs).astype(F32)  3.44 us
    pallas_call x4, Pallas kernels, bin_rows(): pl.pallas_call(functools.partial(bin_kernel, kept_rows), grid=(1,), in_sp...  2.87 us
    slice x1, local copies, waits for them, and re-layouts, raw(): lax.slice_in_dim(self.traces, begin, begin + width, axis=1)  2.19 us
    reduce_precision x1, other arithmetic, moveout(): high = lax.reduce_precision(fraction, 8, 7)  1.55 us
  transfers between devices with their start and end apart: 26, of which 6 were waited for; matrix products, arithmetic and copies ran while one was open for 12% of the time, Pallas kernels for 13%

profile of v2, /device:TPU:0, one launch (start us, length us, event | category | flops | bytes accessed | tf_op | source)
XLA Modules:
  0.0 70.9 jit_solution(5277327612409760421)
XLA Ops:
  0.6 0.7 broadcast_multiply_fusion
  1.3 0.7 multiply_add_fusion
  2.0 0.5 collective-permute-start
  2.6 2.2 %fusion.51 = (bf16[256,512]{1,0:T(8,128)(2,1)}, bf16[256,512]{1,0:T(8,128)(2,1)}, bf16[256,512]{1,0:T(8,128)(2,1)}, bf16[256,512]{1,0:T(8,128)(2,1)}) fusion(bf16[256,2048]{1,0:T(8,128)(2,1)} %refs_0_.7), kind=kLoop, calls=%fused_computation.151 | loop fusion | bytes 2097152 | tf_op jit(solution)/shard_map/slice | solution.py:175
  4.8 2.9 %collective-permute-start.7 = (bf16[256,512]{1,0:T(8,128)(2,1)}, bf16[256,512]{1,0:T(8,128)(2,1)}, u32[]{:S(2)}, u32[]{:S(2)}) collective-permute-start(bf16[256,512]{1,0:T(8,128)(2,1)} %get-tuple-element.27), channel_id=1, source_target_pairs={{0,8},{4,12},{8,0},{12,4},{16,24},{20,28},{24,16},{28,20},{1,9},{5... | collective-permute-start | bytes 786440 | tf_op jit(solution)/shard_map/ppermute | solution.py:110
  7.7 1.5 %collective-permute-start.11 = (bf16[256,512]{1,0:T(8,128)(2,1)}, bf16[256,512]{1,0:T(8,128)(2,1)S(1)}, u32[]{:S(2)}, u32[]{:S(2)}) collective-permute-start(bf16[256,512]{1,0:T(8,128)(2,1)} %get-tuple-element.26), channel_id=1, source_target_pairs={{0,16},{4,20},{8,24},{12,28},{16,0},{20,4},{24,8},{28,12},{1,17},{... | collective-permute-start | bytes 786440 | tf_op jit(solution)/shard_map/ppermute | solution.py:110
  9.3 0.1 mul.160
  9.4 0.1 add_select_fusion
  9.7 0.1 copy.10
  9.8 0.1 slice_multiply_fusion
  10.0 0.2 broadcast_in_dim.57
  10.2 0.1 reshape.432
  10.3 0.2 broadcast_in_dim.56
  10.5 0.9 %reshape.430 = s32[16,8,1024]{2,1,0:T(8,128)} reshape(s32[128,8,128]{2,1,0:T(8,128)S(1)} %broadcast_in_dim.56) | data formatting | bytes 1048576 | tf_op jit(solution)/shard_map/reshape | solution.py:448
  11.4 1.6 %fusion.10 = (f32[16,8,1024]{2,1,0:T(8,128)S(1)}, f32[16,8,1024]{2,1,0:T(8,128)S(1)}, f32[16,8,1024]{2,1,0:T(8,128)}, f32[16,8,1024]{2,1,0:T(8,128)}) fusion(f32[1024]{0:T(1024)S(1)} %get-tuple-element.61, f32[16,8]{1,0:T(8,128)S(1)} %maximum_multiply_fusion, f32[1024]{0:T(1024)S(1)} %get-tuple-element.62), kind=kLoop, calls=%fused_computation.26 | loop fusion | flops 1572864 | bytes 2105856 | tf_op jit(solution)/shard_map/reduce_precision | solution.py:450
  13.0 1.5 %fusion.9 = (s32[16,8,1024]{2,1,0:T(8,128)}, s32[16,8,1024]{2,1,0:T(8,128)}) fusion(s32[16,8,1024]{2,1,0:T(8,128)S(1)} %reshape.432, f32[1024]{0:T(1024)S(1)} %get-tuple-element.61, f32[16,8]{1,0:T(8,128)S(1)} %maximum_multiply_fusion, s32[16,8,1024]{2,1,0:T(8,128)S(1)} %copy-done.5, f32[1024]{0:T(1024)S(1)} %get-tuple-element.62), kind=kLoop, calls=%fused_computation.23 | loop fusion | flops 1310720 | bytes 2105856 | tf_op jit(solution)/shard_map/sub | solution.py:448
  14.5 0.6 collective-permute-start.10
  15.1 0.1 collective-permute-start.1
  15.2 3.0 %collective-permute-done.10 = s32[2,256]{1,0:T(2,128)S(1)} collective-permute-done((s32[2,256]{1,0:T(2,128)S(1)}, s32[2,256]{1,0:T(2,128)S(1)}, u32[]{:S(2)}, u32[]{:S(2)}) %collective-permute-start.10) | collective-permute-done | bytes 2080 | tf_op jit(solution)/shard_map/ppermute | solution.py:110
  18.2 0.5 collective-permute-start.17
  18.8 0.1 convert_reduce_fusion
  19.0 1.5 %collective-permute-start.2 = (f32[32]{0:T(128)S(1)}, f32[32]{0:T(128)S(1)}, u32[]{:S(2)}, u32[]{:S(2)}) collective-permute-start(f32[32]{0:T(128)S(1)} %slice.25), channel_id=1, source_target_pairs={{0,16},{4,20},{8,24},{12,28},{16,0},{20,4},{24,8},{28,12},{1,17},{... | collective-permute-start | bytes 392 | tf_op jit(solution)/shard_map/ppermute | solution.py:110
  20.5 0.3 fusion.1.member_ref
  20.8 0.3 fusion.3.member_ref
  21.1 1.5 %collective-permute-done.2 = f32[32]{0:T(128)S(1)} collective-permute-done((f32[32]{0:T(128)S(1)}, f32[32]{0:T(128)S(1)}, u32[]{:S(2)}, u32[]{:S(2)}) %collective-permute-start.2) | collective-permute-done | bytes 160 | tf_op jit(solution)/shard_map/ppermute | solution.py:110
  22.5 1.5 %collective-permute-start.20 = (bf16[256,512]{1,0:T(8,128)(2,1)S(1)}, bf16[256,512]{1,0:T(8,128)(2,1)S(1)}, u32[]{:S(2)}, u32[]{:S(2)}) collective-permute-start(bf16[256,512]{1,0:T(8,128)(2,1)S(1)} %copy-done.6), channel_id=1, source_target_pairs={{0,16},{4,20},{8,24},{12,28},{16,0},{20,4},{24,8},{28,12},{1,17},{... | collective-permute-start | bytes 786440 | tf_op jit(solution)/shard_map/ppermute | solution.py:110
  24.0 0.9 %collective-permute-done.17.refs_2_ = bf16[256,512]{1,0:T(8,128)(2,1)S(1)} collective-permute-done((bf16[256,512]{1,0:T(8,128)(2,1)}, bf16[256,512]{1,0:T(8,128)(2,1)S(1)}, u32[]{:S(2)}, u32[]{:S(2)}) %collective-permute-start.17) | collective-permute-done | bytes 262176 | tf_op jit(solution)/shard_map/ppermute | solution.py:110
  25.0 0.5 collective-permute-start.8
  25.5 1.6 %collective-permute-start.5 = (f32[8]{0:T(128)S(1)}, f32[8]{0:T(128)S(1)}, u32[]{:S(2)}, u32[]{:S(2)}) collective-permute-start(f32[8]{0:T(128)S(1)} %get-tuple-element.54), channel_id=1, source_target_pairs={{0,1},{1,0},{2,3},{3,2},{4,5},{5,4},{6,7},{7,6},{8,9},{9,8},{10,11... | collective-permute-start | bytes 104 | tf_op jit(solution)/shard_map/ppermute | solution.py:165
  27.1 2.6 %collective-permute-start.4 = (f32[8]{0:T(128)S(1)}, f32[8]{0:T(128)S(1)}, u32[]{:S(2)}, u32[]{:S(2)}) collective-permute-start(f32[8]{0:T(128)S(1)} %get-tuple-element.55), channel_id=1, source_target_pairs={{0,2},{1,3},{2,0},{3,1},{4,6},{5,7},{6,4},{7,5},{8,10},{9,11},{10,... | collective-permute-start | bytes 104 | tf_op jit(solution)/shard_map/ppermute | solution.py:165
  29.7 0.5 shard_map.79
  30.2 2.5 %collective-permute-start.3 = (f32[8]{0:T(128)S(1)}, f32[8]{0:T(128)S(1)}, u32[]{:S(2)}, u32[]{:S(2)}) collective-permute-start(f32[8]{0:T(128)S(1)} %get-tuple-element.53), channel_id=1, source_target_pairs={{0,3},{1,2},{2,1},{3,0},{4,7},{5,6},{6,5},{7,4},{8,11},{9,10},{10,... | collective-permute-start | bytes 104 | tf_op jit(solution)/shard_map/ppermute | solution.py:165
  32.7 1.0 %collective-permute-start.19 = (bf16[144,512]{1,0:T(8,128)(2,1)S(1)}, bf16[144,512]{1,0:T(8,128)(2,1)S(1)}, u32[]{:S(2)}, u32[]{:S(2)}) collective-permute-start(bf16[144,512]{1,0:T(8,128)(2,1)S(1)} %get-tuple-element.18), channel_id=1, source_target_pairs={{0,16},{4,20},{8,24},{12,28},{16,0},{20,4},{24,8},{28,12},{1,17},{... | collective-permute-start | bytes 442376 | tf_op jit(solution)/shard_map/ppermute | solution.py:110
  33.7 2.0 %collective-permute-done.3 = f32[8]{0:T(128)S(1)} collective-permute-done((f32[8]{0:T(128)S(1)}, f32[8]{0:T(128)S(1)}, u32[]{:S(2)}, u32[]{:S(2)}) %collective-permute-start.3) | collective-permute-done | bytes 64 | tf_op jit(solution)/shard_map/ppermute | solution.py:165
  35.7 1.5 %shard_map.77 = (f32[144,512]{1,0:T(8,128)S(1)}, bf16[144,512]{1,0:T(8,128)(2,1)S(1)}) custom-call(bf16[288,1024]{1,0:T(8,128)(2,1)S(1)} %fusion.1.member_ref, bf16[256,2048]{1,0:T(8,128)(2,1)S(1)} %copy-done, bf16[256,2048]{1,0:T(8,128)(2,1)S(1)} %collective-permute-done.6.refs_1_, bf16[256,512]{1,0:T(8,128)(2,1)} %collective-permute-done.7.refs_2_, ...), custom_call_target="tpu_custom_call" | custom-call | flops 301989888 | bytes 1933312 | tf_op jit(solution)/shard_map/pallas_call | solution.py:66
  37.2 1.0 %collective-permute-start.9 = (bf16[144,512]{1,0:T(8,128)(2,1)S(1)}, bf16[144,512]{1,0:T(8,128)(2,1)S(1)}, u32[]{:S(2)}, u32[]{:S(2)}) collective-permute-start(bf16[144,512]{1,0:T(8,128)(2,1)S(1)} %get-tuple-element.14), channel_id=1, source_target_pairs={{0,16},{4,20},{8,24},{12,28},{16,0},{20,4},{24,8},{28,12},{1,17},{... | collective-permute-start | bytes 442376 | tf_op jit(solution)/shard_map/ppermute | solution.py:110
  38.1 0.5 shard_map.78
  38.6 0.6 collective-permute-start.13
  39.2 0.5 shard_map.80
  39.7 1.6 %collective-permute-start.22 = (bf16[144,512]{1,0:T(8,128)(2,1)S(1)}, bf16[144,512]{1,0:T(8,128)(2,1)S(1)}, u32[]{:S(2)}, u32[]{:S(2)}) collective-permute-start(bf16[144,512]{1,0:T(8,128)(2,1)S(1)} %get-tuple-element.20), channel_id=1, source_target_pairs={{0,8},{4,12},{8,0},{12,4},{16,24},{20,28},{24,16},{28,20},{1,9},{5... | collective-permute-start | bytes 442376 | tf_op jit(solution)/shard_map/ppermute | solution.py:110
  41.3 5.4 %collective-permute-done.22 = bf16[144,512]{1,0:T(8,128)(2,1)S(1)} collective-permute-done((bf16[144,512]{1,0:T(8,128)(2,1)S(1)}, bf16[144,512]{1,0:T(8,128)(2,1)S(1)}, u32[]{:S(2)}, u32[]{:S(2)}) %collective-permute-start.22) | collective-permute-done | bytes 147488 | tf_op jit(solution)/shard_map/ppermute | solution.py:110
  46.9 1.7 %collective-permute-start.24 = (bf16[40,1024]{1,0:T(8,128)(2,1)S(1)}, bf16[40,1024]{1,0:T(8,128)(2,1)S(1)}, u32[]{:S(2)}, u32[]{:S(2)}) collective-permute-start(bf16[40,1024]{1,0:T(8,128)(2,1)S(1)} %get-tuple-element.30), channel_id=1, source_target_pairs={{0,2},{1,3},{2,0},{3,1},{4,6},{5,7},{6,4},{7,5},{8,10},{9,11},{10,... | collective-permute-start | bytes 245768 | tf_op jit(solution)/shard_map/ppermute | solution.py:165
  48.6 2.7 %collective-permute-start.23 = (bf16[40,1024]{1,0:T(8,128)(2,1)S(1)}, bf16[40,1024]{1,0:T(8,128)(2,1)S(1)}, u32[]{:S(2)}, u32[]{:S(2)}) collective-permute-start(bf16[40,1024]{1,0:T(8,128)(2,1)S(1)} %get-tuple-element.28), channel_id=1, source_target_pairs={{0,3},{1,2},{2,1},{3,0},{4,7},{5,6},{6,5},{7,4},{8,11},{9,10},{10,... | collective-permute-start | bytes 245768 | tf_op jit(solution)/shard_map/ppermute | solution.py:165
  51.5 1.7 %collective-permute-start.15 = (bf16[40,1024]{1,0:T(8,128)(2,1)S(1)}, bf16[40,1024]{1,0:T(8,128)(2,1)S(1)}, u32[]{:S(2)}, u32[]{:S(2)}) collective-permute-start(bf16[40,1024]{1,0:T(8,128)(2,1)S(1)} %get-tuple-element.33), channel_id=1, source_target_pairs={{0,2},{1,3},{2,0},{3,1},{4,6},{5,7},{6,4},{7,5},{8,10},{9,11},{10,... | collective-permute-start | bytes 245768 | tf_op jit(solution)/shard_map/ppermute | solution.py:165
  53.2 2.7 %collective-permute-start.14 = (bf16[40,1024]{1,0:T(8,128)(2,1)S(1)}, bf16[40,1024]{1,0:T(8,128)(2,1)S(1)}, u32[]{:S(2)}, u32[]{:S(2)}) collective-permute-start(bf16[40,1024]{1,0:T(8,128)(2,1)S(1)} %get-tuple-element.31), channel_id=1, source_target_pairs={{0,3},{1,2},{2,1},{3,0},{4,7},{5,6},{6,5},{7,4},{8,11},{9,10},{10,... | collective-permute-start | bytes 245768 | tf_op jit(solution)/shard_map/ppermute | solution.py:165
  55.9 1.5 %collective-permute-done.24 = bf16[40,1024]{1,0:T(8,128)(2,1)S(1)} collective-permute-done((bf16[40,1024]{1,0:T(8,128)(2,1)S(1)}, bf16[40,1024]{1,0:T(8,128)(2,1)S(1)}, u32[]{:S(2)}, u32[]{:S(2)}) %collective-permute-start.24) | collective-permute-done | bytes 81952 | tf_op jit(solution)/shard_map/ppermute | solution.py:165
  57.4 6.6 %shard_map.81 = (bf16[8,16,2048]{2,1,0:T(8,128)(2,1)}, f32[8,16,2048]{2,1,0:T(8,128)}, bf16[2,256,128]{2,1,0:T(8,128)(2,1)S(1)}) custom-call(s32[1024]{0:T(1024)S(1)} %add_select_fusion.6.refs_0_, f32[8]{0:T(128)S(1)} %maximum_divide_fusion.refs_1_, f32[40,1024]{1,0:T(8,128)S(1)} %fusion.15.refs_2_.refs_3_, s32[16,8,1024]{2,1,0:T(8,128)S(1)} %copy-done.1, ...), custom_call_target="tpu_custom_call" | custom-call | flops 20971520 | bytes 4718592 | tf_op jit(solution)/shard_map/pallas_call | solution.py:402
  64.2 6.7 %shard_map.82 = (bf16[8,16,2048]{2,1,0:T(8,128)(2,1)}, f32[8,16,2048]{2,1,0:T(8,128)}) custom-call(s32[1024]{0:T(1024)S(1)} %add_select_fusion.6.refs_0_, f32[8]{0:T(128)S(1)} %maximum_divide_fusion.refs_1_, f32[40,1024]{1,0:T(8,128)S(1)} %fusion.19.refs_2_, f32[40,1024]{1,0:T(8,128)S(1)} %fusion.15.refs_2_.refs_3_, ...), custom_call_target="tpu_custom_call", output_to_operand_aliasing={{0}: (8, {}), {1}: (9, {})} | custom-call | flops 20971520 | bytes 4718592 | tf_op jit(solution)/shard_map/pallas_call | solution.py:402
  (71 shorter events, 1.3 us)
Async XLA Ops:
  2.0 7.2 %copy-start.7 = (f32[16]{0:T(128)S(1)}, f32[16]{0:T(128)}, u32[]{:S(2)}) copy-start(f32[16]{0:T(128)} %param.11) | copy-start | bytes 196
  2.0 7.2 %copy-start.8 = (f32[4]{0:T(128)S(1)}, f32[4]{0:T(128)}, u32[]{:S(2)}) copy-start(f32[4]{0:T(128)} %param.10) | copy-start | bytes 52
  2.0 12.5 %collective-permute-start = (s32[256]{0:T(256)S(1)}, s32[256]{0:T(256)S(1)}, u32[]{:S(2)}, u32[]{:S(2)}) collective-permute-start(s32[256]{0:T(256)S(1)} %multiply_add_fusion), channel_id=1, source_target_pairs={{0,4},{4,0},{8,12},{12,8},{16,20},{20,16},{24,28},{28,24},{1,5},{5... | collective-permute-start | bytes 3080 | tf_op jit(solution)/shard_map/ppermute | solution.py:110
  2.5 27.2 %collective-permute-start.6 = (bf16[256,2048]{1,0:T(8,128)(2,1)}, bf16[256,2048]{1,0:T(8,128)(2,1)S(1)}, u32[]{:S(2)}, u32[]{:S(2)}) collective-permute-start(bf16[256,2048]{1,0:T(8,128)(2,1)} %refs_0_.7), channel_id=1, source_target_pairs={{0,4},{4,0},{8,12},{12,8},{16,20},{20,16},{24,28},{28,24},{1,5},{5... | collective-permute-start | bytes 3145736 | tf_op jit(solution)/shard_map/ppermute | solution.py:110
  4.8 20.2 %collective-permute-start.7 = (bf16[256,512]{1,0:T(8,128)(2,1)}, bf16[256,512]{1,0:T(8,128)(2,1)}, u32[]{:S(2)}, u32[]{:S(2)}) collective-permute-start(bf16[256,512]{1,0:T(8,128)(2,1)} %get-tuple-element.27), channel_id=1, source_target_pairs={{0,8},{4,12},{8,0},{12,4},{16,24},{20,28},{24,16},{28,20},{1,9},{5... | collective-permute-start | bytes 786440 | tf_op jit(solution)/shard_map/ppermute | solution.py:110
  7.7 17.8 %collective-permute-start.11 = (bf16[256,512]{1,0:T(8,128)(2,1)}, bf16[256,512]{1,0:T(8,128)(2,1)S(1)}, u32[]{:S(2)}, u32[]{:S(2)}) collective-permute-start(bf16[256,512]{1,0:T(8,128)(2,1)} %get-tuple-element.26), channel_id=1, source_target_pairs={{0,16},{4,20},{8,24},{12,28},{16,0},{20,4},{24,8},{28,12},{1,17},{... | collective-permute-start | bytes 786440 | tf_op jit(solution)/shard_map/ppermute | solution.py:110
  11.4 1.6 %copy-start.5 = (s32[16,8,1024]{2,1,0:T(8,128)S(1)}, s32[16,8,1024]{2,1,0:T(8,128)}, u32[]{:S(2)}) copy-start(s32[16,8,1024]{2,1,0:T(8,128)} %reshape.430) | copy-start | bytes 1572868
  14.5 15.3 %copy-start = (bf16[256,2048]{1,0:T(8,128)(2,1)S(1)}, bf16[256,2048]{1,0:T(8,128)(2,1)}, u32[]{:S(2)}) copy-start(bf16[256,2048]{1,0:T(8,128)(2,1)} %refs_0_.7) | copy-start | bytes 3145732
  14.5 3.7 %collective-permute-start.10 = (s32[2,256]{1,0:T(2,128)S(1)}, s32[2,256]{1,0:T(2,128)S(1)}, u32[]{:S(2)}, u32[]{:S(2)}) collective-permute-start(s32[2,256]{1,0:T(2,128)S(1)} %pad_add_fusion.1), channel_id=1, source_target_pairs={{0,16},{4,20},{8,24},{12,28},{16,0},{20,4},{24,8},{28,12},{1,17},{... | collective-permute-start | bytes 6152 | tf_op jit(solution)/shard_map/ppermute | solution.py:110
  15.1 3.6 %collective-permute-start.1 = (s32[2,256]{1,0:T(2,128)S(1)}, s32[2,256]{1,0:T(2,128)S(1)}, u32[]{:S(2)}, u32[]{:S(2)}) collective-permute-start(s32[2,256]{1,0:T(2,128)S(1)} %pad_add_fusion.1), channel_id=1, source_target_pairs={{0,8},{4,12},{8,0},{12,4},{16,24},{20,28},{24,16},{28,20},{1,9},{5... | collective-permute-start | bytes 6152 | tf_op jit(solution)/shard_map/ppermute | solution.py:110
  15.2 7.3 %copy-start.6 = (bf16[256,512]{1,0:T(8,128)(2,1)S(1)}, bf16[256,512]{1,0:T(8,128)(2,1)}, u32[]{:S(2)}) copy-start(bf16[256,512]{1,0:T(8,128)(2,1)} %get-tuple-element.24) | copy-start | bytes 786436
  18.2 6.8 %collective-permute-start.17 = (bf16[256,512]{1,0:T(8,128)(2,1)}, bf16[256,512]{1,0:T(8,128)(2,1)S(1)}, u32[]{:S(2)}, u32[]{:S(2)}) collective-permute-start(bf16[256,512]{1,0:T(8,128)(2,1)} %get-tuple-element.25), channel_id=1, source_target_pairs={{0,8},{4,12},{8,0},{12,4},{16,24},{20,28},{24,16},{28,20},{1,9},{5... | collective-permute-start | bytes 786440 | tf_op jit(solution)/shard_map/ppermute | solution.py:110
  19.0 3.5 %collective-permute-start.2 = (f32[32]{0:T(128)S(1)}, f32[32]{0:T(128)S(1)}, u32[]{:S(2)}, u32[]{:S(2)}) collective-permute-start(f32[32]{0:T(128)S(1)} %slice.25), channel_id=1, source_target_pairs={{0,16},{4,20},{8,24},{12,28},{16,0},{20,4},{24,8},{28,12},{1,17},{... | collective-permute-start | bytes 392 | tf_op jit(solution)/shard_map/ppermute | solution.py:110
  22.5 10.2 %collective-permute-start.20 = (bf16[256,512]{1,0:T(8,128)(2,1)S(1)}, bf16[256,512]{1,0:T(8,128)(2,1)S(1)}, u32[]{:S(2)}, u32[]{:S(2)}) collective-permute-start(bf16[256,512]{1,0:T(8,128)(2,1)S(1)} %copy-done.6), channel_id=1, source_target_pairs={{0,16},{4,20},{8,24},{12,28},{16,0},{20,4},{24,8},{28,12},{1,17},{... | collective-permute-start | bytes 786440 | tf_op jit(solution)/shard_map/ppermute | solution.py:110
  24.9 2.2 %collective-permute-start.18 = (bf16[256,512]{1,0:T(8,128)(2,1)S(1)}, bf16[256,512]{1,0:T(8,128)(2,1)S(1)}, u32[]{:S(2)}, u32[]{:S(2)}) collective-permute-start(bf16[256,512]{1,0:T(8,128)(2,1)S(1)} %collective-permute-done.17.refs_2_), channel_id=1, source_target_pairs={{0,4},{4,0},{8,12},{12,8},{16,20},{20,16},{24,28},{28,24},{1,5},{5... | collective-permute-start | bytes 786440 | tf_op jit(solution)/shard_map/ppermute | solution.py:110
  25.0 10.8 %collective-permute-start.8 = (bf16[256,512]{1,0:T(8,128)(2,1)}, bf16[256,512]{1,0:T(8,128)(2,1)S(1)}, u32[]{:S(2)}, u32[]{:S(2)}) collective-permute-start(bf16[256,512]{1,0:T(8,128)(2,1)} %collective-permute-done.7.refs_2_), channel_id=1, source_target_pairs={{0,4},{4,0},{8,12},{12,8},{16,20},{20,16},{24,28},{28,24},{1,5},{5... | collective-permute-start | bytes 786440 | tf_op jit(solution)/shard_map/ppermute | solution.py:110
  25.5 4.7 %collective-permute-start.5 = (f32[8]{0:T(128)S(1)}, f32[8]{0:T(128)S(1)}, u32[]{:S(2)}, u32[]{:S(2)}) collective-permute-start(f32[8]{0:T(128)S(1)} %get-tuple-element.54), channel_id=1, source_target_pairs={{0,1},{1,0},{2,3},{3,2},{4,5},{5,4},{6,7},{7,6},{8,9},{9,8},{10,11... | collective-permute-start | bytes 104 | tf_op jit(solution)/shard_map/ppermute | solution.py:165
  27.1 5.6 %collective-permute-start.4 = (f32[8]{0:T(128)S(1)}, f32[8]{0:T(128)S(1)}, u32[]{:S(2)}, u32[]{:S(2)}) collective-permute-start(f32[8]{0:T(128)S(1)} %get-tuple-element.55), channel_id=1, source_target_pairs={{0,2},{1,3},{2,0},{3,1},{4,6},{5,7},{6,4},{7,5},{8,10},{9,11},{10,... | collective-permute-start | bytes 104 | tf_op jit(solution)/shard_map/ppermute | solution.py:165
  29.7 8.4 %collective-permute-start.12 = (bf16[256,512]{1,0:T(8,128)(2,1)S(1)}, bf16[256,512]{1,0:T(8,128)(2,1)S(1)}, u32[]{:S(2)}, u32[]{:S(2)}) collective-permute-start(bf16[256,512]{1,0:T(8,128)(2,1)S(1)} %collective-permute-done.11.refs_2_), channel_id=1, source_target_pairs={{0,4},{4,0},{8,12},{12,8},{16,20},{20,16},{24,28},{28,24},{1,5},{5... | collective-permute-start | bytes 786440 | tf_op jit(solution)/shard_map/ppermute | solution.py:110
  30.2 5.4 %collective-permute-start.3 = (f32[8]{0:T(128)S(1)}, f32[8]{0:T(128)S(1)}, u32[]{:S(2)}, u32[]{:S(2)}) collective-permute-start(f32[8]{0:T(128)S(1)} %get-tuple-element.53), channel_id=1, source_target_pairs={{0,3},{1,2},{2,1},{3,0},{4,7},{5,6},{6,5},{7,4},{8,11},{9,10},{10,... | collective-permute-start | bytes 104 | tf_op jit(solution)/shard_map/ppermute | solution.py:165
  32.7 6.5 %collective-permute-start.21 = (bf16[256,512]{1,0:T(8,128)(2,1)S(1)}, bf16[256,512]{1,0:T(8,128)(2,1)S(1)}, u32[]{:S(2)}, u32[]{:S(2)}) collective-permute-start(bf16[256,512]{1,0:T(8,128)(2,1)S(1)} %collective-permute-done.20.refs_2_), channel_id=1, source_target_pairs={{0,4},{4,0},{8,12},{12,8},{16,20},{20,16},{24,28},{28,24},{1,5},{5... | collective-permute-start | bytes 786440 | tf_op jit(solution)/shard_map/ppermute | solution.py:110
  32.7 8.5 %collective-permute-start.19 = (bf16[144,512]{1,0:T(8,128)(2,1)S(1)}, bf16[144,512]{1,0:T(8,128)(2,1)S(1)}, u32[]{:S(2)}, u32[]{:S(2)}) collective-permute-start(bf16[144,512]{1,0:T(8,128)(2,1)S(1)} %get-tuple-element.18), channel_id=1, source_target_pairs={{0,16},{4,20},{8,24},{12,28},{16,0},{20,4},{24,8},{28,12},{1,17},{... | collective-permute-start | bytes 442376 | tf_op jit(solution)/shard_map/ppermute | solution.py:110
  37.2 14.1 %collective-permute-start.9 = (bf16[144,512]{1,0:T(8,128)(2,1)S(1)}, bf16[144,512]{1,0:T(8,128)(2,1)S(1)}, u32[]{:S(2)}, u32[]{:S(2)}) collective-permute-start(bf16[144,512]{1,0:T(8,128)(2,1)S(1)} %get-tuple-element.14), channel_id=1, source_target_pairs={{0,16},{4,20},{8,24},{12,28},{16,0},{20,4},{24,8},{28,12},{1,17},{... | collective-permute-start | bytes 442376 | tf_op jit(solution)/shard_map/ppermute | solution.py:110
  38.6 12.7 %collective-permute-start.13 = (bf16[144,512]{1,0:T(8,128)(2,1)S(1)}, bf16[144,512]{1,0:T(8,128)(2,1)S(1)}, u32[]{:S(2)}, u32[]{:S(2)}) collective-permute-start(bf16[144,512]{1,0:T(8,128)(2,1)S(1)} %get-tuple-element.16), channel_id=1, source_target_pairs={{0,8},{4,12},{8,0},{12,4},{16,24},{20,28},{24,16},{28,20},{1,9},{5... | collective-permute-start | bytes 442376 | tf_op jit(solution)/shard_map/ppermute | solution.py:110
  39.7 7.0 %collective-permute-start.22 = (bf16[144,512]{1,0:T(8,128)(2,1)S(1)}, bf16[144,512]{1,0:T(8,128)(2,1)S(1)}, u32[]{:S(2)}, u32[]{:S(2)}) collective-permute-start(bf16[144,512]{1,0:T(8,128)(2,1)S(1)} %get-tuple-element.20), channel_id=1, source_target_pairs={{0,8},{4,12},{8,0},{12,4},{16,24},{20,28},{24,16},{28,20},{1,9},{5... | collective-permute-start | bytes 442376 | tf_op jit(solution)/shard_map/ppermute | solution.py:110
  46.8 6.4 %collective-permute-start.25 = (bf16[40,1024]{1,0:T(8,128)(2,1)S(1)}, bf16[40,1024]{1,0:T(8,128)(2,1)S(1)}, u32[]{:S(2)}, u32[]{:S(2)}) collective-permute-start(bf16[40,1024]{1,0:T(8,128)(2,1)S(1)} %get-tuple-element.29), channel_id=1, source_target_pairs={{0,1},{1,0},{2,3},{3,2},{4,5},{5,4},{6,7},{7,6},{8,9},{9,8},{10,11... | collective-permute-start | bytes 245768 | tf_op jit(solution)/shard_map/ppermute | solution.py:165
  46.9 10.5 %collective-permute-start.24 = (bf16[40,1024]{1,0:T(8,128)(2,1)S(1)}, bf16[40,1024]{1,0:T(8,128)(2,1)S(1)}, u32[]{:S(2)}, u32[]{:S(2)}) collective-permute-start(bf16[40,1024]{1,0:T(8,128)(2,1)S(1)} %get-tuple-element.30), channel_id=1, source_target_pairs={{0,2},{1,3},{2,0},{3,1},{4,6},{5,7},{6,4},{7,5},{8,10},{9,11},{10,... | collective-permute-start | bytes 245768 | tf_op jit(solution)/shard_map/ppermute | solution.py:165
  48.6 8.8 %collective-permute-start.23 = (bf16[40,1024]{1,0:T(8,128)(2,1)S(1)}, bf16[40,1024]{1,0:T(8,128)(2,1)S(1)}, u32[]{:S(2)}, u32[]{:S(2)}) collective-permute-start(bf16[40,1024]{1,0:T(8,128)(2,1)S(1)} %get-tuple-element.28), channel_id=1, source_target_pairs={{0,3},{1,2},{2,1},{3,0},{4,7},{5,6},{6,5},{7,4},{8,11},{9,10},{10,... | collective-permute-start | bytes 245768 | tf_op jit(solution)/shard_map/ppermute | solution.py:165
  51.3 6.1 %copy-start.1 = (s32[16,8,1024]{2,1,0:T(8,128)S(1)}, s32[16,8,1024]{2,1,0:T(8,128)}, u32[]{:S(2)}) copy-start(s32[16,8,1024]{2,1,0:T(8,128)} %get-tuple-element.42.refs_3_) | copy-start | bytes 1572868
  51.4 12.6 %collective-permute-start.16 = (bf16[40,1024]{1,0:T(8,128)(2,1)S(1)}, bf16[40,1024]{1,0:T(8,128)(2,1)S(1)}, u32[]{:S(2)}, u32[]{:S(2)}) collective-permute-start(bf16[40,1024]{1,0:T(8,128)(2,1)S(1)} %get-tuple-element.32), channel_id=1, source_target_pairs={{0,1},{1,0},{2,3},{3,2},{4,5},{5,4},{6,7},{7,6},{8,9},{9,8},{10,11... | collective-permute-start | bytes 245768 | tf_op jit(solution)/shard_map/ppermute | solution.py:165
  51.5 12.6 %collective-permute-start.15 = (bf16[40,1024]{1,0:T(8,128)(2,1)S(1)}, bf16[40,1024]{1,0:T(8,128)(2,1)S(1)}, u32[]{:S(2)}, u32[]{:S(2)}) collective-permute-start(bf16[40,1024]{1,0:T(8,128)(2,1)S(1)} %get-tuple-element.33), channel_id=1, source_target_pairs={{0,2},{1,3},{2,0},{3,1},{4,6},{5,7},{6,4},{7,5},{8,10},{9,11},{10,... | collective-permute-start | bytes 245768 | tf_op jit(solution)/shard_map/ppermute | solution.py:165
  53.2 10.9 %collective-permute-start.14 = (bf16[40,1024]{1,0:T(8,128)(2,1)S(1)}, bf16[40,1024]{1,0:T(8,128)(2,1)S(1)}, u32[]{:S(2)}, u32[]{:S(2)}) collective-permute-start(bf16[40,1024]{1,0:T(8,128)(2,1)S(1)} %get-tuple-element.31), channel_id=1, source_target_pairs={{0,3},{1,2},{2,1},{3,0},{4,7},{5,6},{6,5},{7,4},{8,11},{9,10},{10,... | collective-permute-start | bytes 245768 | tf_op jit(solution)/shard_map/ppermute | solution.py:165
  57.4 6.7 %copy-start.2 = (f32[16,8,1024]{2,1,0:T(8,128)S(1)}, f32[16,8,1024]{2,1,0:T(8,128)}, u32[]{:S(2)}) copy-start(f32[16,8,1024]{2,1,0:T(8,128)} %get-tuple-element.40.refs_5_) | copy-start | bytes 1572868
  57.4 6.7 %copy-start.3 = (f32[16,8,1024]{2,1,0:T(8,128)S(1)}, f32[16,8,1024]{2,1,0:T(8,128)}, u32[]{:S(2)}) copy-start(f32[16,8,1024]{2,1,0:T(8,128)} %get-tuple-element.41.refs_6_) | copy-start | bytes 1572868
  57.4 6.7 %copy-start.4 = (s32[16,8,1024]{2,1,0:T(8,128)S(1)}, s32[16,8,1024]{2,1,0:T(8,128)}, u32[]{:S(2)}) copy-start(s32[16,8,1024]{2,1,0:T(8,128)} %get-tuple-element.43.refs_4_) | copy-start | bytes 1572868

commit v3 on v2

v3 whole, which is shorter than its diff:
```python
import functools
import math

import jax
import jax.numpy as jnp
from jax import lax
from jax.experimental import pallas as pl
from jax.experimental.pallas import tpu as pltpu
from jax.sharding import PartitionSpec as P

HALF_WIN = 4
CMP_DEV = 8
LANES = 128
VMEM_BYTES = 16 * 1024 * 1024
F32 = jnp.float32
BF16 = jnp.bfloat16
VMEM = pl.BlockSpec(memory_space=pltpu.VMEM)
SMEM = pl.BlockSpec(memory_space=pltpu.SMEM)
ANY = pl.BlockSpec(memory_space=pl.ANY)
TOKEN = jax.ShapeDtypeStruct((8, LANES), F32)

LANE_GATHER = lax.GatherDimensionNumbers(
    offset_dims=(),
    collapsed_slice_dims=(1,),
    start_index_map=(1,),
    operand_batching_dims=(0,),
    start_indices_batching_dims=(0,),
)


def take_lanes(rows, index):
    return lax.gather(
        rows,
        index[..., None],
        LANE_GATHER,
        (1, 1),
        mode=lax.GatherScatterMode.PROMISE_IN_BOUNDS,
    )


def bin_kernel(kept_rows, width, count, member_ref, *refs):
    data, (kept_ref, sent_ref, token_ref) = refs[:count], refs[-3:]
    token_ref[...] = jnp.zeros(token_ref.shape, F32)
    per = data[0].shape[0]
    cols = kept_ref.shape[1]
    tile = math.gcd(width, 256)
    for start in range(0, cols, tile):
        where = slice(start, min(start + tile, cols))
        total = None
        for at, block in enumerate(data):
            values = block[:, where] if start < width else jnp.ones((per, cols - width), BF16)
            part = jnp.dot(
                member_ref[:, at * per : (at + 1) * per], values, preferred_element_type=F32
            )
            total = part if total is None else total + part
        kept_ref[:, where] = total[:kept_rows]
        if kept_rows < total.shape[0]:
            sent_ref[:, where] = total[kept_rows:].astype(BF16)
        else:
            sent_ref[:, where] = jnp.zeros((sent_ref.shape[0], total.shape[1]), BF16)


def bin_rows(member, data, start, width, counted, kept_rows, after):
    rows = member.shape[0]
    per = data[0].shape[0]
    cols = width + (LANES if counted else 0)
    sent_rows = max(rows - kept_rows, 16)
    in_specs = [pl.BlockSpec(member.shape, lambda t: (0, 0))]
    in_specs += [pl.BlockSpec((per, width), lambda t: (0, start // width))] * len(data)
    in_specs += [ANY] * len(after)
    return pl.pallas_call(
        functools.partial(bin_kernel, kept_rows, width, len(data)),
        grid=(1,),
        in_specs=in_specs,
        out_specs=[
            pl.BlockSpec((kept_rows, cols), lambda t: (0, 0)),
            pl.BlockSpec((sent_rows, cols), lambda t: (0, 0)),
            pl.BlockSpec(TOKEN.shape, lambda t: (0, 0)),
        ],
        out_shape=[
            jax.ShapeDtypeStruct((kept_rows, cols), F32),
            jax.ShapeDtypeStruct((sent_rows, cols), BF16),
            TOKEN,
        ],
        compiler_params=pltpu.CompilerParams(vmem_limit_bytes=VMEM_BYTES),
        cost_estimate=pl.CostEstimate(
            flops=2 * rows * len(data) * per * cols,
            bytes_accessed=2 * len(data) * per * cols + 6 * rows * cols,
            transcendentals=0,
        ),
    )(member, *data, *after)


class Plan:
    def __init__(self, traces, key, classes):
        self.inline = lax.axis_size("inline")
        self.xline = lax.axis_size("xline")
        self.me = lax.axis_index("inline")
        self.me_x = lax.axis_index("xline")
        self.classes = classes
        self.dev_rows = CMP_DEV * classes
        self.line_rows = self.xline * self.dev_rows
        bits = [1 << b for b in range(self.inline.bit_length() - 1)]
        self.core, others = bits[0], bits[1:]
        self.orders = [others, others[::-1]] if len(others) > 1 else [others]
        self.codes = 1 << len(others)
        unit = 8 if self.codes % 4 == 0 else 16
        self.block_rows = -(-(self.line_rows + 2 * classes) // unit) * unit
        self.data = [traces, self.swap(traces, self.core)]
        self.keys = jnp.concatenate([key, self.swap(key, self.core)])
        self.members = [self.member(order) for order in self.orders]
        places = [self.me_x] + [target for target, _ in self.targets()]
        self.places = jnp.stack(places) * self.dev_rows

    def swap(self, value, bit):
        return lax.ppermute(value, "inline", [(i, i ^ bit) for i in range(self.inline)])

    def member(self, order):
        classes, line_rows = self.classes, self.line_rows
        line, local = self.keys // line_rows, self.keys % line_rows

        def row_of(target, row):
            apart = target ^ self.me
            code = jnp.zeros_like(target)
            for bit in order:
                code = code * 2 + jnp.where(apart & bit != 0, 1, 0)
            valid = (apart & self.core == 0) & (target >= 0) & (target < self.inline)
            return jnp.where(valid, code * self.block_rows + row, -1)

        own = row_of(line, local + classes)
        rim = jnp.where(
            local >= line_rows - classes,
            row_of(line + 1, local - (line_rows - classes)),
            jnp.where(local < classes, row_of(line - 1, local + classes + line_rows), -1),
        )
        row = jnp.arange(self.codes * self.block_rows)[:, None]
        return ((row == own[None, :]) | (row == rim[None, :])).astype(BF16)

    def bin(self, start, cols, counted, after):
        width = cols // len(self.orders)
        rows = self.codes * self.block_rows
        parts = []
        for at, order in enumerate(self.orders):
            count_here = counted and at == len(self.orders) - 1
            parts.append(
                bin_rows(
                    self.members[at],
                    self.data,
                    start + at * width,
                    width,
                    count_here,
                    rows // 2 if order else rows,
                    after,
                )
            )
        return parts

    def exchange(self, place, parts):
        return [
            (kept, self.swap(sent, order[place])) for order, (kept, sent, *_) in zip(self.orders, parts)
        ]

    def targets(self):
        steps = []
        for step in range(self.xline - 1, 0, -1):
            if self.xline & (self.xline - 1) == 0:
                target = self.me_x ^ step
                pairs = [(i, i ^ step) for i in range(self.xline)]
            else:
                target = (self.me_x + step) % self.xline
                pairs = [(i, (i + step) % self.xline) for i in range(self.xline)]
            steps.append((target, pairs))
        return steps

    def merge(self, parts, after):
        half = parts[0][0].shape[0] // 2
        shapes = []
        for kept, _ in parts:
            shapes.append(jax.ShapeDtypeStruct((half, kept.shape[1]), F32))
            shapes.append(jax.ShapeDtypeStruct((half, kept.shape[1]), BF16))
        flat = [value for part in parts for value in part]
        outs = pl.pallas_call(
            functools.partial(merge_kernel, len(parts)),
            in_specs=[VMEM] * len(flat) + [ANY] * len(after),
            out_specs=[VMEM] * (len(shapes) + 1),
            out_shape=shapes + [TOKEN],
            compiler_params=pltpu.CompilerParams(vmem_limit_bytes=VMEM_BYTES),
            cost_estimate=cost_of(flat),
        )(*flat, *after)
        return list(zip(outs[0:-1:2], outs[1:-1:2])), outs[-1]

    def spread(self, parts, after):
        window = self.dev_rows + 2 * self.classes
        cols = sum(kept.shape[1] for kept, _ in parts)
        flat = [value for part in parts for value in part]
        kinds = [F32] + [BF16] * (self.xline - 1)
        return pl.pallas_call(
            functools.partial(spread_kernel, len(parts), len(kinds)),
            in_specs=[SMEM] + [VMEM] * len(flat) + [ANY] * len(after),
            out_specs=[VMEM] * (len(kinds) + 1),
            out_shape=[jax.ShapeDtypeStruct((window, cols), kind) for kind in kinds] + [TOKEN],
            scratch_shapes=[pltpu.VMEM((parts[0][0].shape[0], cols), F32)],
            compiler_params=pltpu.CompilerParams(vmem_limit_bytes=VMEM_BYTES),
            cost_estimate=cost_of(flat),
        )(self.places, *flat, *after)

    def across(self, blocks):
        own, *sent = blocks
        return [own] + [
            lax.ppermute(block, "xline", pairs) for block, (_, pairs) in zip(sent, self.targets())
        ]


def cost_of(values):
    size = sum(value.size * value.dtype.itemsize for value in values)
    return pl.CostEstimate(flops=0, bytes_accessed=2 * size, transcendentals=0)


def merge_kernel(count, *refs):
    ins, outs, token_ref = refs[: 2 * count], refs[-2 * count - 1 : -1], refs[-1]
    token_ref[...] = jnp.zeros(token_ref.shape, F32)
    for at in range(count):
        kept, sent = ins[2 * at : 2 * at + 2]
        half = kept.shape[0] // 2
        total = kept[...] + sent[...].astype(F32)
        outs[2 * at][...] = total[:half]
        outs[2 * at + 1][...] = total[half:].astype(BF16)


def spread_kernel(count, blocks, places_ref, *refs):
    ins, outs, token_ref, total_ref = refs[: 2 * count], refs[-blocks - 2 : -2], refs[-2], refs[-1]
    token_ref[...] = jnp.zeros(token_ref.shape, F32)
    start = 0
    for at in range(count):
        kept, sent = ins[2 * at : 2 * at + 2]
        stop = start + kept.shape[1]
        total_ref[:, start:stop] = kept[...] + sent[...].astype(F32)
        start = stop
    for at, out in enumerate(outs):
        place = pl.multiple_of(places_ref[at], 8)
        out[...] = total_ref[pl.ds(place, out.shape[0]), :].astype(out.dtype)


def panel_kernel(classes, vels, first, last, count, pieces, waits, *refs):
    blocks_ref = refs[0]
    at = 1
    chunk_refs = []
    for number in pieces:
        chunk_refs.append(refs[at : at + number])
        at += number
    local_ref, low_ref, high_ref = refs[at : at + 3]
    at += 3 + waits
    if last < count:
        later_ref = refs[at]
        at += 3
    stacked_out, semblance_out = refs[at : at + 2]
    at += 2
    if first > 0:
        carry_ref = refs[at]
        at += 1
    (
        plane_ref,
        source_ref,
        rim_source_ref,
        sum_ref,
        energy_ref,
        rim_ref,
        window_ref,
        scale_ref,
        stacked_ref,
        semblance_ref,
        copies,
    ) = refs[at:]
    mids = CMP_DEV
    span = last - first
    held = count - first
    lane = lax.broadcasted_iota(jnp.int32, (8, LANES), 1)
    sub = lax.broadcasted_iota(jnp.int32, (8, LANES), 0)
    sub16 = lax.broadcasted_iota(jnp.int32, (16, LANES), 0)

    block_at = 0
    for piece_refs in chunk_refs:
        for inner in range(piece_refs[0].shape[1] // LANES):
            where = slice(inner * LANES, (inner + 1) * LANES)
            block = piece_refs[0][:, where]
            for piece_ref in piece_refs[1:]:
                block = block + piece_ref[:, where].astype(F32)
            plane_ref[block_at] = block.astype(BF16).astype(F32) if block_at < held else block
            block_at += 1
    fold = None
    for h in range(classes):
        counts = plane_ref[held, pl.ds(classes + h, mids, stride=classes), :]
        fold = counts if fold is None else fold + counts
    scale_ref[...] = 1.0 / jnp.maximum(fold, 1.0)
    plane_ref[held] = jnp.zeros(plane_ref.shape[1:], F32)

    def later(here, after):
        return jnp.where(
            lane == LANES - 1,
            pltpu.roll(after, LANES - 1, 1),
            pltpu.roll(here, LANES - 1, 1),
        )

    def rim_rows(at):
        return jnp.where(
            sub < classes, plane_ref[at, 0:8, :], plane_ref[at, mids * classes : mids * classes + 8, :]
        )

    zeros = jnp.zeros((16, LANES), BF16)
    for at in range(held):
        for h in range(classes):
            here = plane_ref[at, pl.ds(classes + h, mids, stride=classes), :]
            after = plane_ref[at + 1, pl.ds(classes + h, mids, stride=classes), :]
            source_ref[h, at] = jnp.concatenate([here, later(here, after)], axis=0).astype(BF16)
        here, after = rim_rows(at), rim_rows(at + 1)
        rim_source_ref[at] = jnp.concatenate([here, later(here, after)], axis=0).astype(BF16)
    for at in (held, held + 1):
        for h in range(classes):
            source_ref[h, at] = zeros
        rim_source_ref[at] = zeros

    own_class = [sub16 % classes == h for h in range(classes)]
    group = 2 * classes

    def per_velocity(j, _):
        for at in range(span):
            where = slice(at * LANES, (at + 1) * LANES)
            base = [blocks_ref[h, j * span + at] - first for h in range(classes)]
            total = energy = None
            for h in range(classes):
                row = slice(h, h + 1)
                index = jnp.broadcast_to(local_ref[j, row, where], (16, LANES)).astype(jnp.int16)
                low = jnp.broadcast_to(low_ref[j, row, where], (8, LANES))
                high = jnp.broadcast_to(high_ref[j, row, where], (8, LANES))
                inner = index & (LANES - 1)
                got = jnp.where(
                    index < LANES,
                    take_lanes(source_ref[h, base[h]], inner),
                    take_lanes(source_ref[h, base[h] + 1], inner),
                ).astype(F32)
                moved = low * got[:8] + high * got[8:]
                total = moved if total is None else total + moved
                energy = moved * moved if energy is None else energy + moved * moved
            sum_ref[at, pl.ds(j, mids, stride=vels), :] = total
            energy_ref[at, pl.ds(j, mids, stride=vels), :] = energy
            near = rim_source_ref[base[0]]
            far = rim_source_ref[base[0] + 1]
            for h in range(1, classes):
                near = jnp.where(own_class[h], rim_source_ref[base[h]], near)
                far = jnp.where(own_class[h], rim_source_ref[base[h] + 1], far)
            local = local_ref[j, :, where]
            index = jnp.concatenate([local, local], axis=0).astype(jnp.int16)
            inner = index & (LANES - 1)
            got = jnp.where(
                index < LANES, take_lanes(near, inner), take_lanes(far, inner)
            ).astype(F32)
            rim_ref[at, pl.ds(j, group, stride=vels), :] = (
                low_ref[j, :, where] * got[:8] + high_ref[j, :, where] * got[8:]
            )
        return 0

    lax.fori_loop(0, vels, per_velocity, 0, unroll=2)

    shape = (mids, vels, LANES)
    rows = mids * vels
    edge = jnp.zeros(window_ref.shape[1:], BF16)
    window_ref[0] = edge
    if last < count:
        window_ref[span + 1] = later_ref[0]
        window_ref[span + 2] = later_ref[1]
    else:
        window_ref[span + 1] = edge

    def three(low, mid, high):
        return jnp.concatenate([low, mid[:-1]], axis=0) + mid + jnp.concatenate([mid[1:], high], axis=0)

    def per_block(at, _):
        total = sum_ref[at].reshape(shape)
        rim = rim_ref[at].reshape(2, classes, vels, LANES)
        rim_sum = jnp.sum(rim, axis=1)
        rim_power = rim_sum * rim_sum
        rim_energy = jnp.sum(rim * rim, axis=1)
        power = three(rim_power[0:1], total * total, rim_power[1:2])
        energy = three(rim_energy[0:1], energy_ref[at].reshape(shape), rim_energy[1:2])
        window_ref[at + 1, :rows] = power.reshape(rows, LANES).astype(BF16)
        window_ref[at + 1, rows:] = energy.reshape(rows, LANES).astype(BF16)
        where = pl.ds(pl.multiple_of(at * LANES, LANES), LANES)
        for m in range(mids):
            stacked_ref[m, :, where] = (total[m] * scale_ref[m : m + 1, :]).astype(BF16)
        return 0

    lax.fori_loop(0, span, per_block, 0)
    stacked_copy = pltpu.make_async_copy(
        stacked_ref, stacked_out.at[:, :, first * LANES : last * LANES], copies.at[0]
    )
    stacked_copy.start()

    def band(blocks):
        shape = ((blocks + 2) * LANES, blocks * LANES)
        source = lax.broadcasted_iota(jnp.int32, shape, 0) - LANES
        target = lax.broadcasted_iota(jnp.int32, shape, 1)
        return jnp.where(jnp.abs(source - target) <= HALF_WIN, 1.0, 0.0).astype(BF16)

    begin = 0 if first == 0 else 1
    end = span + 1 if last < count else span
    wide = band(2)
    narrow = band(1)
    at = begin
    while at < end:
        blocks = min(2, end - at)
        values = jnp.concatenate([window_ref[at + i] for i in range(blocks + 2)], axis=1)
        summed = jnp.dot(values, wide if blocks == 2 else narrow, preferred_element_type=F32)
        semblance = summed[:rows] / jnp.maximum(classes * summed[rows:], 1.0)
        semblance_ref[:, :, (at - begin) * LANES : (at - begin + blocks) * LANES] = semblance.reshape(
            mids, vels, blocks * LANES
        )
        at += blocks
    semblance_copy = pltpu.make_async_copy(
        semblance_ref,
        semblance_out.at[:, :, (first + begin) * LANES : (first + end) * LANES],
        copies.at[1],
    )
    semblance_copy.start()
    if first > 0:
        carry_ref[0] = window_ref[1]
        carry_ref[1] = window_ref[2]
    stacked_copy.wait()
    semblance_copy.wait()


def panels(first, last, count, classes, vels, tables, rows, after, later):
    span = last - first
    held = count - first
    samples = count * LANES
    group = 2 * classes
    window_rows = 2 * CMP_DEV * vels
    done = span - (first > 0) + (last < count)
    outs = [
        jax.ShapeDtypeStruct((CMP_DEV, vels, samples), BF16),
        jax.ShapeDtypeStruct((CMP_DEV, vels, samples), F32),
    ]
    specs = [ANY] * 2
    if first > 0:
        outs.append(jax.ShapeDtypeStruct((2, window_rows, LANES), BF16))
        specs.append(VMEM)
    flat = [piece for chunk in rows for piece in chunk]
    *tables, blocks = tables
    operands = [blocks, *flat, *tables, *after]
    in_specs = [SMEM] + [VMEM] * (len(flat) + len(tables)) + [ANY] * len(after)
    aliases = {}
    if later is not None:
        stacked, semblance, carry = later
        aliases = {len(operands) + 1: 0, len(operands) + 2: 1}
        operands += [carry, stacked, semblance]
        in_specs += [VMEM, ANY, ANY]
    return pl.pallas_call(
        functools.partial(panel_kernel, classes, vels, first, last, count, [len(c) for c in rows], len(after)),
        in_specs=in_specs,
        out_specs=specs,
        out_shape=outs,
        input_output_aliases=aliases,
        scratch_shapes=[
            pltpu.VMEM((held + 1, flat[0].shape[0], LANES), F32),
            pltpu.VMEM((classes, held + 2, 16, LANES), BF16),
            pltpu.VMEM((held + 2, 16, LANES), BF16),
            pltpu.VMEM((span, CMP_DEV * vels, LANES), F32),
            pltpu.VMEM((span, CMP_DEV * vels, LANES), F32),
            pltpu.VMEM((span, group * vels, LANES), F32),
            pltpu.VMEM((span + 3, window_rows, LANES), BF16),
            pltpu.VMEM((CMP_DEV, LANES), F32),
            pltpu.VMEM((CMP_DEV, vels, span * LANES), BF16),
            pltpu.VMEM((CMP_DEV, vels, done * LANES), F32),
            pltpu.SemaphoreType.DMA((2,)),
        ],
        compiler_params=pltpu.CompilerParams(vmem_limit_bytes=VMEM_BYTES),
        cost_estimate=pl.CostEstimate(
            flops=14000 * CMP_DEV * vels * classes * span * LANES,
            bytes_accessed=(1 + span) * 512 * 1024,
            transcendentals=0,
        ),
    )(*operands)


def table_kernel(classes, start, samples, offsets_ref, velocities_ref, *refs):
    local_ref, low_ref, high_ref, blocks_ref = refs[-4:]
    vels, rows, cols = local_ref.shape
    lane = lax.broadcasted_iota(jnp.int32, (rows, LANES), 1)
    sub = lax.broadcasted_iota(jnp.int32, (rows, LANES), 0)
    offset = jnp.full((rows, LANES), offsets_ref[0], F32)
    for h in range(1, classes):
        offset = jnp.where(sub % classes == h, offsets_ref[h], offset)

    def per_velocity(j, blocks):
        blocks = list(blocks)
        slowness = offset / jnp.full((rows, LANES), velocities_ref[j], F32)
        square = slowness * slowness
        for at in range(cols // LANES):
            begin = start + at * LANES
            first = jnp.sqrt(square + float(begin) * float(begin)) - 0.01
            first = jnp.minimum(jnp.maximum(first, float(begin)), float(samples)).astype(jnp.int32)
            base = first // LANES
            flat = j * (cols // LANES) + at
            for wide in range(len(blocks)):
                blocks[wide] = jnp.where(lane == flat - wide * LANES, base, blocks[wide])
            time = (lane + begin).astype(F32)
            position = jnp.sqrt(time * time + square)
            floored = jnp.floor(position)
            fraction = position - floored
            index = jnp.minimum(floored, float(samples)).astype(jnp.int32)
            where = slice(at * LANES, (at + 1) * LANES)
            local_ref[j, :, where] = index - base * LANES
            low_ref[j, :, where] = (1.0 - fraction).astype(BF16).astype(F32)
            high_ref[j, :, where] = fraction.astype(BF16).astype(F32)
        return tuple(blocks)

    width = blocks_ref.shape[1] // LANES
    blocks = lax.fori_loop(
        0,
        vels,
        per_velocity,
        tuple(jnp.zeros((rows, LANES), jnp.int32) for _ in range(width)),
        unroll=math.gcd(vels, 4),
    )
    for wide in range(width):
        blocks_ref[:, wide * LANES : (wide + 1) * LANES] = blocks[wide]


def moveout(offsets, velocities, samples, start, stop, after):
    vels, classes = velocities.shape[0], offsets.shape[0]
    shape = (vels, 2 * classes, stop - start)
    width = pl.cdiv(vels * (stop - start) // LANES, LANES) * LANES
    return pl.pallas_call(
        functools.partial(table_kernel, classes, start, samples),
        in_specs=[SMEM, SMEM] + [ANY] * len(after),
        out_specs=[VMEM] * 4,
        out_shape=[
            jax.ShapeDtypeStruct(shape, jnp.int32),
            jax.ShapeDtypeStruct(shape, F32),
            jax.ShapeDtypeStruct(shape, F32),
            jax.ShapeDtypeStruct((2 * classes, width), jnp.int32),
        ],
        compiler_params=pltpu.CompilerParams(vmem_limit_bytes=VMEM_BYTES),
        cost_estimate=pl.CostEstimate(
            flops=14000 * math.prod(shape), bytes_accessed=12 * math.prod(shape), transcendentals=0
        ),
    )(offsets, velocities, *after)


def per_device(traces, owners, midpoint, offset_class, offsets, velocities):
    samples = traces.shape[1]
    classes, vels = offsets.shape[0], velocities.shape[0]
    count = samples // LANES
    key = (owners[:, 0] * CMP_DEV + midpoint) * classes + offset_class
    plan = Plan(traces, key, classes)
    cuts = [0, samples // 2, samples]
    chunks = list(zip(cuts[:-1], cuts[1:]))[::-1]
    parts, after = [], [plan.places]
    for start, stop in chunks:
        parts.append(plan.bin(start, stop - start, stop == samples, after))
        after = [parts[-1][-1][2]]
    steps = len(plan.orders[0])
    tables, rows, tokens = [], [], []
    for at, chunk in enumerate(chunks):
        tables.append(moveout(offsets, velocities, samples, *chunk, after))
        part = plan.exchange(0, parts[at])
        for place in range(1, steps):
            part, token = plan.merge(part, after)
            part = plan.exchange(place, part)
        *spread, token = plan.spread(part, [rows[-1][1]] if rows else [])
        rows.append(plan.across(spread))
        tokens.append(token)
        after = [token]
    out = None
    for at, (start, stop) in enumerate(chunks):
        out = panels(
            start // LANES,
            stop // LANES,
            count,
            classes,
            vels,
            tables[at],
            rows[: at + 1][::-1],
            tokens[at + 1 : at + 2],
            out,
        )
    return (out[0], out[1])


def solution(mesh):
    in_specs = (
        P(("inline", "xline"), None),
        P(("inline", "xline"), None),
        P(("inline", "xline")),
        P(("inline", "xline")),
        P(),
        P(),
    )
    out_specs = (P(("inline", "xline"), None, None), P(("inline", "xline"), None, None))
    return jax.shard_map(
        per_device, mesh=mesh, in_specs=in_specs, out_specs=out_specs, check_vma=False
    )
```

time: 72.1 us -> 56 us (0.78); the launches traced: 70.9 us -> 55.9 us
  starting transfers between devices: 29.3 us -> 18.4 us
  Pallas kernels: 16.2 us -> 21.1 us
  local copies, waits for them, and re-layouts: 4.06 us -> 0.01 us
  other arithmetic: 6.08 us -> 2.26 us
  waiting for transfers between devices: 14.2 us -> 13.3 us
    ppermute x9 -> x6, starting transfers between devices: 15.5 us -> 8.91 us  [across(): lax.ppermute(block, 'xline', pairs)]
    pallas_call x4 -> x10, Pallas kernels: 2.87 us -> 8.72 us  [the longest x2 3.05 us: moveout(): pl.pallas_call(functools.partial(table_kernel, classes, start, samples),...]
    ppermute x17 -> x10, starting transfers between devices: 13.8 us -> 9.52 us  [swap(): lax.ppermute(value, 'inline', [(i, i ^ bit) for i in range(self.inline)])]
    ppermute x9 -> x6, waiting for transfers between devices: 3.44 us -> 0.02 us  [across(): lax.ppermute(block, 'xline', pairs)]
    ppermute x17 -> x10, waiting for transfers between devices: 10.8 us -> 13.3 us  [swap(): lax.ppermute(value, 'inline', [(i, i ^ bit) for i in range(self.inline)])]
    slice x2 -> x0, local copies, waits for them, and re-layouts: 2.27 us -> none  [the longest x1 2.19 us: raw(): lax.slice_in_dim(self.traces, begin, begin + width, axis=1)]
    reduce_precision x1 -> x0, other arithmetic: 1.55 us -> none  [moveout(): high = lax.reduce_precision(fraction, 8, 7)]
    sub x1 -> x0, other arithmetic: 1.49 us -> none  [moveout(): local = sample_index - jnp.repeat(base, LANES, axis=1)]
  transfers between devices with their start and end apart: 26 -> 16, of which waited for: 6 -> 6; matrix products, arithmetic and copies ran while one was open for 12% -> 4% of each run, Pallas kernels for 13% -> 25%
where the time goes in v3:
time: 56 us; the launch traced here: 55.9 us
  Pallas kernels  21.1 us (38%)
  starting transfers between devices  18.4 us (33%)
  waiting for transfers between devices  13.3 us (24%)
  other arithmetic  2.26 us (4%)
  between operations  0.77 us (1%)
    ppermute x10, waiting for transfers between devices, swap(): lax.ppermute(value, 'inline', [(i, i ^ bit) for i in range(self.inline)])  13.3 us
    pallas_call x2, Pallas kernels, panels(): pl.pallas_call(functools.partial(panel_kernel, classes, vels, first, last...  12.3 us
    ppermute x10, starting transfers between devices, swap(): lax.ppermute(value, 'inline', [(i, i ^ bit) for i in range(self.inline)])  9.52 us
    ppermute x6, starting transfers between devices, across(): lax.ppermute(block, 'xline', pairs)  8.91 us
    pallas_call x2, Pallas kernels, moveout(): pl.pallas_call(functools.partial(table_kernel, classes, start, samples),...  3.05 us
    pallas_call x4, Pallas kernels, bin_rows(): pl.pallas_call(functools.partial(bin_kernel, kept_rows, width, len(data))...  3.01 us
    pallas_call x2, Pallas kernels, merge(): pl.pallas_call(functools.partial(merge_kernel, len(parts)), in_specs=[VME...  1.39 us
    pallas_call x2, Pallas kernels, spread(): pl.pallas_call(functools.partial(spread_kernel, len(parts), len(kinds)),...  1.28 us
  transfers between devices with their start and end apart: 16, of which 6 were waited for; matrix products, arithmetic and copies ran while one was open for 4% of the time, Pallas kernels for 25%

profile of v3, /device:TPU:0, one launch (start us, length us, event | category | flops | bytes accessed | tf_op | source)
XLA Modules:
  0.0 55.9 jit_solution(13067805666800674406)
XLA Ops:
  0.6 0.5 collective-permute-start.1
  1.2 0.7 %broadcast_multiply_fusion = s32[256,1]{0,1:T(1,128)S(1)} fusion(s32[256,1]{0,1:T(1,128)} %param.7), kind=kLoop, calls=%fused_computation.72 | loop fusion | flops 256 | bytes 2048 | tf_op jit(solution)/shard_map/mul | solution.py:553
  1.8 0.7 %multiply_add_fusion = s32[256]{0:T(256)S(1)} fusion(s32[256]{0:T(256)} %param.9, s32[256]{0:T(256)S(1)} %bitcast.5, s32[256]{0:T(256)} %param.8), kind=kLoop, calls=%fused_computation.70 | loop fusion | flops 768 | bytes 4096 | tf_op jit(solution)/shard_map/add | solution.py:553
  2.5 0.1 collective-permute-start
  2.7 0.1 add_multiply_fusion.refs_2_.places_ref
  2.7 0.9 %collective-permute-done = s32[256]{0:T(256)S(1)} collective-permute-done((s32[256]{0:T(256)S(1)}, s32[256]{0:T(256)S(1)}, u32[]{:S(2)}, u32[]{:S(2)}) %collective-permute-start) | collective-permute-done | bytes 1056 | tf_op jit(solution)/shard_map/ppermute | solution.py:116
  3.8 0.7 %fusion.1 = (bf16[544,512]{1,0:T(8,128)(2,1)S(1)}, bf16[544,512]{1,0:T(8,128)(2,1)S(1)}) fusion(s32[512]{0:T(512)S(1)} %fusion.17, s32[512]{0:T(512)S(1)} %get-tuple-element.90, s32[512]{0:T(512)S(1)} %get-tuple-element.85, s32[512]{0:T(512)S(1)} %get-tuple-element.80), kind=kLoop, calls=%fused_computation.5 | loop fusion | flops 2228224 | bytes 1122304 | tf_op jit(solution)/shard_map/convert_element_type | solution.py:137
  4.5 0.0 collective-permute-done.1.refs_1_
  4.5 0.6 %shard_map.78 = (f32[272,640]{1,0:T(8,128)S(1)}, bf16[272,640]{1,0:T(8,128)(2,1)S(1)}, f32[8,128]{1,0:T(8,128)S(1)}) custom-call(bf16[544,512]{1,0:T(8,128)(2,1)S(1)} %get-tuple-element.92.member_ref, bf16[256,2048]{1,0:T(8,128)(2,1)S(1)} %copy-done, bf16[256,2048]{1,0:T(8,128)(2,1)S(1)} %collective-permute-done.1.refs_1_, ...), custom_call_target="tpu_custom_call" | custom-call | flops 356515840 | bytes 2744320 | tf_op jit(solution)/shard_map/pallas_call | solution.py:71
  5.1 2.8 %collective-permute-start.3 = (bf16[272,640]{1,0:T(8,128)(2,1)S(1)}, bf16[272,640]{1,0:T(8,128)(2,1)S(1)}, u32[]{:S(2)}, u32[]{:S(2)}) collective-permute-start(bf16[272,640]{1,0:T(8,128)(2,1)S(1)} %get-tuple-element.44), channel_id=1, source_target_pairs={{0,16},{4,20},{8,24},{12,28},{16,0},{20,4},{24,8},{28,12},{1,17},{... | collective-permute-start | bytes 1044488 | tf_op jit(solution)/shard_map/ppermute | solution.py:116
  7.9 1.0 %shard_map.77 = (f32[272,512]{1,0:T(8,128)S(1)}, bf16[272,512]{1,0:T(8,128)(2,1)S(1)}, f32[8,128]{1,0:T(8,128)}) custom-call(bf16[544,512]{1,0:T(8,128)(2,1)S(1)} %get-tuple-element.91.member_ref, bf16[256,2048]{1,0:T(8,128)(2,1)S(1)} %copy-done, bf16[256,2048]{1,0:T(8,128)(2,1)S(1)} %collective-permute-done.1.refs_1_, s32[4]{0:T(128)S(1)} %add_multiply_fusion.refs_2_.places_ref), custom_call_target="tpu_custom_call" | custom-call | flops 285212672 | bytes 2195456 | tf_op jit(solution)/shard_map/pallas_call | solution.py:71
  8.9 1.5 %collective-permute-start.2 = (bf16[272,512]{1,0:T(8,128)(2,1)S(1)}, bf16[272,512]{1,0:T(8,128)(2,1)S(1)}, u32[]{:S(2)}, u32[]{:S(2)}) collective-permute-start(bf16[272,512]{1,0:T(8,128)(2,1)S(1)} %get-tuple-element.42), channel_id=1, source_target_pairs={{0,8},{4,12},{8,0},{12,4},{16,24},{20,28},{24,16},{28,20},{1,9},{5... | collective-permute-start | bytes 835592 | tf_op jit(solution)/shard_map/ppermute | solution.py:116
  10.4 0.5 shard_map.79
  10.8 0.6 %collective-permute-start.7 = (bf16[272,512]{1,0:T(8,128)(2,1)S(1)}, bf16[272,512]{1,0:T(8,128)(2,1)S(1)}, u32[]{:S(2)}, u32[]{:S(2)}) collective-permute-start(bf16[272,512]{1,0:T(8,128)(2,1)S(1)} %get-tuple-element.56), channel_id=1, source_target_pairs={{0,16},{4,20},{8,24},{12,28},{16,0},{20,4},{24,8},{28,12},{1,17},{... | collective-permute-start | bytes 835592 | tf_op jit(solution)/shard_map/ppermute | solution.py:116
  11.4 1.0 %shard_map.83 = (f32[272,512]{1,0:T(8,128)S(1)}, bf16[272,512]{1,0:T(8,128)(2,1)S(1)}, f32[8,128]{1,0:T(8,128)}) custom-call(bf16[544,512]{1,0:T(8,128)(2,1)S(1)} %get-tuple-element.91.member_ref, bf16[256,2048]{1,0:T(8,128)(2,1)S(1)} %copy-done, bf16[256,2048]{1,0:T(8,128)(2,1)S(1)} %collective-permute-done.1.refs_1_, f32[8,128]{1,0:T(8,128)S(1)} %get-tuple-element.45.refs_2_), custom_call_target="tpu_custom_call" | custom-call | flops 285212672 | bytes 2195456 | tf_op jit(solution)/shard_map/pallas_call | solution.py:71
  12.4 0.0 collective-permute-start.6
  12.4 6.0 %collective-permute-done.2.refs_1_ = bf16[272,512]{1,0:T(8,128)(2,1)S(1)} collective-permute-done((bf16[272,512]{1,0:T(8,128)(2,1)S(1)}, bf16[272,512]{1,0:T(8,128)(2,1)S(1)}, u32[]{:S(2)}, u32[]{:S(2)}) %collective-permute-start.2) | collective-permute-done | bytes 278560 | tf_op jit(solution)/shard_map/ppermute | solution.py:116
  18.4 0.0 collective-permute-done.3.refs_3_
  18.4 0.7 %shard_map.80 = (f32[136,512]{1,0:T(8,128)S(1)}, bf16[136,512]{1,0:T(8,128)(2,1)S(1)}, f32[136,640]{1,0:T(8,128)S(1)}, bf16[136,640]{1,0:T(8,128)(2,1)S(1)}, f32[8,128]{1,0:T(8,128)}) custom-call(f32[272,512]{1,0:T(8,128)S(1)} %get-tuple-element.41.refs_0_, bf16[272,512]{1,0:T(8,128)(2,1)S(1)} %collective-permute-done.2.refs_1_, ...), custom_call_target="tpu_custom_call" | custom-call | bytes 3760128 | tf_op jit(solution)/shard_map/pallas_call | solution.py:182
  19.1 1.5 %collective-permute-start.5 = (bf16[136,640]{1,0:T(8,128)(2,1)S(1)}, bf16[136,640]{1,0:T(8,128)(2,1)S(1)}, u32[]{:S(2)}, u32[]{:S(2)}) collective-permute-start(bf16[136,640]{1,0:T(8,128)(2,1)S(1)} %get-tuple-element.50), channel_id=1, source_target_pairs={{0,8},{4,12},{8,0},{12,4},{16,24},{20,28},{24,16},{28,20},{1,9},{5... | collective-permute-start | bytes 522248 | tf_op jit(solution)/shard_map/ppermute | solution.py:116
  20.6 0.5 collective-permute-start.4
  21.1 1.5 %shard_map.86 = (s32[16,8,1024]{2,1,0:T(8,128)S(1)}, f32[16,8,1024]{2,1,0:T(8,128)S(1)}, f32[16,8,1024]{2,1,0:T(8,128)S(1)}, s32[8,128]{1,0:T(8,128)S(1)}) custom-call(f32[4]{0:T(128)S(1)} %copy-done.1, f32[16]{0:T(128)S(1)} %copy-done.2, f32[8,128]{1,0:T(8,128)S(1)} %get-tuple-element.46.refs_4_.refs_0_), custom_call_target="tpu_custom_call" | custom-call | flops 1835008000 | bytes 1572864 | tf_op jit(solution)/shard_map/pallas_call | solution.py:532
  22.6 3.0 %collective-permute-done.4.refs_1_ = bf16[136,512]{1,0:T(8,128)(2,1)S(1)} collective-permute-done((bf16[136,512]{1,0:T(8,128)(2,1)S(1)}, bf16[136,512]{1,0:T(8,128)(2,1)S(1)}, u32[]{:S(2)}, u32[]{:S(2)}) %collective-permute-start.4) | collective-permute-done | bytes 139296 | tf_op jit(solution)/shard_map/ppermute | solution.py:116
  25.7 1.5 %collective-permute-done.5.refs_3_ = bf16[136,640]{1,0:T(8,128)(2,1)S(1)} collective-permute-done((bf16[136,640]{1,0:T(8,128)(2,1)S(1)}, bf16[136,640]{1,0:T(8,128)(2,1)S(1)}, u32[]{:S(2)}, u32[]{:S(2)}) %collective-permute-start.5) | collective-permute-done | bytes 174112 | tf_op jit(solution)/shard_map/ppermute | solution.py:116
  27.2 0.6 %shard_map.81 = (f32[40,1152]{1,0:T(8,128)S(1)}, bf16[40,1152]{1,0:T(8,128)(2,1)S(1)}, bf16[40,1152]{1,0:T(8,128)(2,1)S(1)}, bf16[40,1152]{1,0:T(8,128)(2,1)S(1)}, f32[8,128]{1,0:T(8,128)S(1)}) custom-call(s32[4]{0:T(128)S(1)} %add_multiply_fusion.refs_2_.places_ref, f32[136,512]{1,0:T(8,128)S(1)} %get-tuple-element.47.refs_0_, ...), custom_call_target="tpu_custom_call" | custom-call | bytes 1880064 | tf_op jit(solution)/shard_map/pallas_call | solution.py:197
  27.8 3.7 %collective-permute-start.10 = (bf16[40,1152]{1,0:T(8,128)(2,1)S(1)}, bf16[40,1152]{1,0:T(8,128)(2,1)S(1)}, u32[]{:S(2)}, u32[]{:S(2)}) collective-permute-start(bf16[40,1152]{1,0:T(8,128)(2,1)S(1)} %get-tuple-element.61), channel_id=1, source_target_pairs={{0,3},{1,2},{2,1},{3,0},{4,7},{5,6},{6,5},{7,4},{8,11},{9,10},{10,... | collective-permute-start | bytes 276488 | tf_op jit(solution)/shard_map/ppermute | solution.py:210
  31.5 0.0 collective-permute-start.14
  31.5 0.8 %collective-permute-start.15 = (bf16[40,1152]{1,0:T(8,128)(2,1)S(1)}, bf16[40,1152]{1,0:T(8,128)(2,1)S(1)}, u32[]{:S(2)}, u32[]{:S(2)}) collective-permute-start(bf16[40,1152]{1,0:T(8,128)(2,1)S(1)} %get-tuple-element.68), channel_id=1, source_target_pairs={{0,1},{1,0},{2,3},{3,2},{4,5},{5,4},{6,7},{7,6},{8,9},{9,8},{10,11... | collective-permute-start | bytes 276488 | tf_op jit(solution)/shard_map/ppermute | solution.py:210
  32.3 0.0 collective-permute-done.7.refs_3_
  32.3 0.0 collective-permute-done.6.refs_1_
  32.3 0.7 %shard_map.84 = (f32[136,512]{1,0:T(8,128)S(1)}, bf16[136,512]{1,0:T(8,128)(2,1)S(1)}, f32[136,512]{1,0:T(8,128)S(1)}, bf16[136,512]{1,0:T(8,128)(2,1)S(1)}, f32[8,128]{1,0:T(8,128)}) custom-call(f32[272,512]{1,0:T(8,128)S(1)} %get-tuple-element.53.refs_0_, bf16[272,512]{1,0:T(8,128)(2,1)S(1)} %collective-permute-done.6.refs_1_, ...), custom_call_target="tpu_custom_call" | custom-call | bytes 3342336 | tf_op jit(solution)/shard_map/pallas_call | solution.py:182
  33.0 0.4 collective-permute-start.8
  33.3 1.6 %collective-permute-start.9 = (bf16[136,512]{1,0:T(8,128)(2,1)S(1)}, bf16[136,512]{1,0:T(8,128)(2,1)S(1)}, u32[]{:S(2)}, u32[]{:S(2)}) collective-permute-start(bf16[136,512]{1,0:T(8,128)(2,1)S(1)} %get-tuple-element.60), channel_id=1, source_target_pairs={{0,8},{4,12},{8,0},{12,4},{16,24},{20,28},{24,16},{28,20},{1,9},{5... | collective-permute-start | bytes 417800 | tf_op jit(solution)/shard_map/ppermute | solution.py:116
  35.0 1.5 %shard_map.82 = (s32[16,8,1024]{2,1,0:T(8,128)S(1)}, f32[16,8,1024]{2,1,0:T(8,128)S(1)}, f32[16,8,1024]{2,1,0:T(8,128)S(1)}, s32[8,128]{1,0:T(8,128)S(1)}) custom-call(f32[4]{0:T(128)S(1)} %copy-done.1, f32[16]{0:T(128)S(1)} %copy-done.2, f32[8,128]{1,0:T(8,128)S(1)} %get-tuple-element.51.refs_0_.refs_4_), custom_call_target="tpu_custom_call" | custom-call | flops 1835008000 | bytes 1572864 | tf_op jit(solution)/shard_map/pallas_call | solution.py:532
  36.5 0.0 collective-permute-done.10.refs_4_.refs_2_.refs_6_
  36.5 1.5 %collective-permute-done.8.refs_1_ = bf16[136,512]{1,0:T(8,128)(2,1)S(1)} collective-permute-done((bf16[136,512]{1,0:T(8,128)(2,1)S(1)}, bf16[136,512]{1,0:T(8,128)(2,1)S(1)}, u32[]{:S(2)}, u32[]{:S(2)}) %collective-permute-start.8) | collective-permute-done | bytes 139296 | tf_op jit(solution)/shard_map/ppermute | solution.py:116
  38.0 0.4 collective-permute-done.9.refs_3_
  38.4 0.6 %shard_map.85 = (f32[40,1024]{1,0:T(8,128)S(1)}, bf16[40,1024]{1,0:T(8,128)(2,1)S(1)}, bf16[40,1024]{1,0:T(8,128)(2,1)S(1)}, bf16[40,1024]{1,0:T(8,128)(2,1)S(1)}, f32[8,128]{1,0:T(8,128)S(1)}) custom-call(s32[4]{0:T(128)S(1)} %add_multiply_fusion.refs_2_.places_ref, f32[136,512]{1,0:T(8,128)S(1)} %get-tuple-element.57.refs_0_, ...), custom_call_target="tpu_custom_call" | custom-call | bytes 1671168 | tf_op jit(solution)/shard_map/pallas_call | solution.py:197
  39.0 3.8 %collective-permute-start.11 = (bf16[40,1024]{1,0:T(8,128)(2,1)S(1)}, bf16[40,1024]{1,0:T(8,128)(2,1)S(1)}, u32[]{:S(2)}, u32[]{:S(2)}) collective-permute-start(bf16[40,1024]{1,0:T(8,128)(2,1)S(1)} %get-tuple-element.63), channel_id=1, source_target_pairs={{0,3},{1,2},{2,1},{3,0},{4,7},{5,6},{6,5},{7,4},{8,11},{9,10},{10,... | collective-permute-start | bytes 245768 | tf_op jit(solution)/shard_map/ppermute | solution.py:210
  42.8 0.0 collective-permute-start.12
  42.8 0.6 %collective-permute-start.13 = (bf16[40,1024]{1,0:T(8,128)(2,1)S(1)}, bf16[40,1024]{1,0:T(8,128)(2,1)S(1)}, u32[]{:S(2)}, u32[]{:S(2)}) collective-permute-start(bf16[40,1024]{1,0:T(8,128)(2,1)S(1)} %get-tuple-element.65), channel_id=1, source_target_pairs={{0,1},{1,0},{2,3},{3,2},{4,5},{5,4},{6,7},{7,6},{8,9},{9,8},{10,11... | collective-permute-start | bytes 245768 | tf_op jit(solution)/shard_map/ppermute | solution.py:210
  43.5 0.0 collective-permute-done.14.refs_3_.refs_7_
  43.5 0.0 collective-permute-done.15.refs_4_.refs_8_
  43.5 6.1 %shard_map.87 = (bf16[8,16,2048]{2,1,0:T(8,128)(2,1)}, f32[8,16,2048]{2,1,0:T(8,128)}, bf16[2,256,128]{2,1,0:T(8,128)(2,1)S(1)}) custom-call(s32[8,128]{1,0:T(8,128)S(1)} %get-tuple-element.72.refs_0_, f32[40,1152]{1,0:T(8,128)S(1)} %get-tuple-element.66.refs_1_.refs_5_, bf16[40,1152]{1,0:T(8,128)(2,1)S(1)} %collective-permute-done.10.refs_4_.refs_2_.refs_6_, ...), custom_call_target="tpu_custom_call" | custom-call | flops 7340032000 | bytes 4718592 | tf_op jit(solution)/shard_map/pallas_call | solution.py:456
  49.6 0.0 collective-permute-done.11.refs_2_
  49.6 0.0 collective-permute-done.12.refs_3_
  49.6 0.0 collective-permute-done.13.refs_4_
  49.6 6.3 %shard_map.88 = (bf16[8,16,2048]{2,1,0:T(8,128)(2,1)}, f32[8,16,2048]{2,1,0:T(8,128)}) custom-call(s32[8,128]{1,0:T(8,128)S(1)} %get-tuple-element.52.refs_0_, f32[40,1024]{1,0:T(8,128)S(1)} %get-tuple-element.62.refs_1_, bf16[40,1024]{1,0:T(8,128)(2,1)S(1)} %collective-permute-done.11.refs_2_, ...), custom_call_target="tpu_custom_call", output_to_operand_aliasing={{0}: (13, {}), {1}: (14, {})} | custom-call | flops 7340032000 | bytes 4718592 | tf_op jit(solution)/shard_map/pallas_call | solution.py:456
  (9 shorter events, 0.1 us)
Async XLA Ops:
  0.6 3.9 %copy-start = (bf16[256,2048]{1,0:T(8,128)(2,1)S(1)}, bf16[256,2048]{1,0:T(8,128)(2,1)}, u32[]{:S(2)}) copy-start(bf16[256,2048]{1,0:T(8,128)(2,1)} %refs_0_.7) | copy-start | bytes 3145732
  0.6 3.9 %collective-permute-start.1 = (bf16[256,2048]{1,0:T(8,128)(2,1)}, bf16[256,2048]{1,0:T(8,128)(2,1)S(1)}, u32[]{:S(2)}, u32[]{:S(2)}) collective-permute-start(bf16[256,2048]{1,0:T(8,128)(2,1)} %refs_0_.7), channel_id=1, source_target_pairs={{0,4},{4,0},{8,12},{12,8},{16,20},{20,16},{24,28},{28,24},{1,5},{5... | collective-permute-start | bytes 3145736 | tf_op jit(solution)/shard_map/ppermute | solution.py:116
  2.5 1.1 %collective-permute-start = (s32[256]{0:T(256)S(1)}, s32[256]{0:T(256)S(1)}, u32[]{:S(2)}, u32[]{:S(2)}) collective-permute-start(s32[256]{0:T(256)S(1)} %multiply_add_fusion), channel_id=1, source_target_pairs={{0,4},{4,0},{8,12},{12,8},{16,20},{20,16},{24,28},{28,24},{1,5},{5... | collective-permute-start | bytes 3080 | tf_op jit(solution)/shard_map/ppermute | solution.py:116
  5.1 13.3 %collective-permute-start.3 = (bf16[272,640]{1,0:T(8,128)(2,1)S(1)}, bf16[272,640]{1,0:T(8,128)(2,1)S(1)}, u32[]{:S(2)}, u32[]{:S(2)}) collective-permute-start(bf16[272,640]{1,0:T(8,128)(2,1)S(1)} %get-tuple-element.44), channel_id=1, source_target_pairs={{0,16},{4,20},{8,24},{12,28},{16,0},{20,4},{24,8},{28,12},{1,17},{... | collective-permute-start | bytes 1044488 | tf_op jit(solution)/shard_map/ppermute | solution.py:116
  8.9 9.5 %collective-permute-start.2 = (bf16[272,512]{1,0:T(8,128)(2,1)S(1)}, bf16[272,512]{1,0:T(8,128)(2,1)S(1)}, u32[]{:S(2)}, u32[]{:S(2)}) collective-permute-start(bf16[272,512]{1,0:T(8,128)(2,1)S(1)} %get-tuple-element.42), channel_id=1, source_target_pairs={{0,8},{4,12},{8,0},{12,4},{16,24},{20,28},{24,16},{28,20},{1,9},{5... | collective-permute-start | bytes 835592 | tf_op jit(solution)/shard_map/ppermute | solution.py:116
  10.8 21.5 %collective-permute-start.7 = (bf16[272,512]{1,0:T(8,128)(2,1)S(1)}, bf16[272,512]{1,0:T(8,128)(2,1)S(1)}, u32[]{:S(2)}, u32[]{:S(2)}) collective-permute-start(bf16[272,512]{1,0:T(8,128)(2,1)S(1)} %get-tuple-element.56), channel_id=1, source_target_pairs={{0,16},{4,20},{8,24},{12,28},{16,0},{20,4},{24,8},{28,12},{1,17},{... | collective-permute-start | bytes 835592 | tf_op jit(solution)/shard_map/ppermute | solution.py:116
  12.4 8.7 %copy-start.1 = (f32[4]{0:T(128)S(1)}, f32[4]{0:T(128)}, u32[]{:S(2)}) copy-start(f32[4]{0:T(128)} %offsets_ref.3) | copy-start | bytes 52
  12.4 8.7 %copy-start.2 = (f32[16]{0:T(128)S(1)}, f32[16]{0:T(128)}, u32[]{:S(2)}) copy-start(f32[16]{0:T(128)} %velocities_ref.3) | copy-start | bytes 196
  12.4 19.9 %collective-permute-start.6 = (bf16[272,512]{1,0:T(8,128)(2,1)S(1)}, bf16[272,512]{1,0:T(8,128)(2,1)S(1)}, u32[]{:S(2)}, u32[]{:S(2)}) collective-permute-start(bf16[272,512]{1,0:T(8,128)(2,1)S(1)} %get-tuple-element.54), channel_id=1, source_target_pairs={{0,8},{4,12},{8,0},{12,4},{16,24},{20,28},{24,16},{28,20},{1,9},{5... | collective-permute-start | bytes 835592 | tf_op jit(solution)/shard_map/ppermute | solution.py:116
  19.1 8.1 %collective-permute-start.5 = (bf16[136,640]{1,0:T(8,128)(2,1)S(1)}, bf16[136,640]{1,0:T(8,128)(2,1)S(1)}, u32[]{:S(2)}, u32[]{:S(2)}) collective-permute-start(bf16[136,640]{1,0:T(8,128)(2,1)S(1)} %get-tuple-element.50), channel_id=1, source_target_pairs={{0,8},{4,12},{8,0},{12,4},{16,24},{20,28},{24,16},{28,20},{1,9},{5... | collective-permute-start | bytes 522248 | tf_op jit(solution)/shard_map/ppermute | solution.py:116
  20.6 5.1 %collective-permute-start.4 = (bf16[136,512]{1,0:T(8,128)(2,1)S(1)}, bf16[136,512]{1,0:T(8,128)(2,1)S(1)}, u32[]{:S(2)}, u32[]{:S(2)}) collective-permute-start(bf16[136,512]{1,0:T(8,128)(2,1)S(1)} %get-tuple-element.48), channel_id=1, source_target_pairs={{0,16},{4,20},{8,24},{12,28},{16,0},{20,4},{24,8},{28,12},{1,17},{... | collective-permute-start | bytes 417800 | tf_op jit(solution)/shard_map/ppermute | solution.py:116
  27.8 8.7 %collective-permute-start.10 = (bf16[40,1152]{1,0:T(8,128)(2,1)S(1)}, bf16[40,1152]{1,0:T(8,128)(2,1)S(1)}, u32[]{:S(2)}, u32[]{:S(2)}) collective-permute-start(bf16[40,1152]{1,0:T(8,128)(2,1)S(1)} %get-tuple-element.61), channel_id=1, source_target_pairs={{0,3},{1,2},{2,1},{3,0},{4,7},{5,6},{6,5},{7,4},{8,11},{9,10},{10,... | collective-permute-start | bytes 276488 | tf_op jit(solution)/shard_map/ppermute | solution.py:210
  31.5 12.0 %collective-permute-start.14 = (bf16[40,1152]{1,0:T(8,128)(2,1)S(1)}, bf16[40,1152]{1,0:T(8,128)(2,1)S(1)}, u32[]{:S(2)}, u32[]{:S(2)}) collective-permute-start(bf16[40,1152]{1,0:T(8,128)(2,1)S(1)} %get-tuple-element.67), channel_id=1, source_target_pairs={{0,2},{1,3},{2,0},{3,1},{4,6},{5,7},{6,4},{7,5},{8,10},{9,11},{10,... | collective-permute-start | bytes 276488 | tf_op jit(solution)/shard_map/ppermute | solution.py:210
  31.5 12.0 %collective-permute-start.15 = (bf16[40,1152]{1,0:T(8,128)(2,1)S(1)}, bf16[40,1152]{1,0:T(8,128)(2,1)S(1)}, u32[]{:S(2)}, u32[]{:S(2)}) collective-permute-start(bf16[40,1152]{1,0:T(8,128)(2,1)S(1)} %get-tuple-element.68), channel_id=1, source_target_pairs={{0,1},{1,0},{2,3},{3,2},{4,5},{5,4},{6,7},{7,6},{8,9},{9,8},{10,11... | collective-permute-start | bytes 276488 | tf_op jit(solution)/shard_map/ppermute | solution.py:210
  33.0 5.1 %collective-permute-start.8 = (bf16[136,512]{1,0:T(8,128)(2,1)S(1)}, bf16[136,512]{1,0:T(8,128)(2,1)S(1)}, u32[]{:S(2)}, u32[]{:S(2)}) collective-permute-start(bf16[136,512]{1,0:T(8,128)(2,1)S(1)} %get-tuple-element.58), channel_id=1, source_target_pairs={{0,16},{4,20},{8,24},{12,28},{16,0},{20,4},{24,8},{28,12},{1,17},{... | collective-permute-start | bytes 417800 | tf_op jit(solution)/shard_map/ppermute | solution.py:116
  33.3 5.1 %collective-permute-start.9 = (bf16[136,512]{1,0:T(8,128)(2,1)S(1)}, bf16[136,512]{1,0:T(8,128)(2,1)S(1)}, u32[]{:S(2)}, u32[]{:S(2)}) collective-permute-start(bf16[136,512]{1,0:T(8,128)(2,1)S(1)} %get-tuple-element.60), channel_id=1, source_target_pairs={{0,8},{4,12},{8,0},{12,4},{16,24},{20,28},{24,16},{28,20},{1,9},{5... | collective-permute-start | bytes 417800 | tf_op jit(solution)/shard_map/ppermute | solution.py:116
  39.0 10.5 %collective-permute-start.11 = (bf16[40,1024]{1,0:T(8,128)(2,1)S(1)}, bf16[40,1024]{1,0:T(8,128)(2,1)S(1)}, u32[]{:S(2)}, u32[]{:S(2)}) collective-permute-start(bf16[40,1024]{1,0:T(8,128)(2,1)S(1)} %get-tuple-element.63), channel_id=1, source_target_pairs={{0,3},{1,2},{2,1},{3,0},{4,7},{5,6},{6,5},{7,4},{8,11},{9,10},{10,... | collective-permute-start | bytes 245768 | tf_op jit(solution)/shard_map/ppermute | solution.py:210
  42.8 6.7 %collective-permute-start.12 = (bf16[40,1024]{1,0:T(8,128)(2,1)S(1)}, bf16[40,1024]{1,0:T(8,128)(2,1)S(1)}, u32[]{:S(2)}, u32[]{:S(2)}) collective-permute-start(bf16[40,1024]{1,0:T(8,128)(2,1)S(1)} %get-tuple-element.64), channel_id=1, source_target_pairs={{0,2},{1,3},{2,0},{3,1},{4,6},{5,7},{6,4},{7,5},{8,10},{9,11},{10,... | collective-permute-start | bytes 245768 | tf_op jit(solution)/shard_map/ppermute | solution.py:210
  42.8 6.7 %collective-permute-start.13 = (bf16[40,1024]{1,0:T(8,128)(2,1)S(1)}, bf16[40,1024]{1,0:T(8,128)(2,1)S(1)}, u32[]{:S(2)}, u32[]{:S(2)}) collective-permute-start(bf16[40,1024]{1,0:T(8,128)(2,1)S(1)} %get-tuple-element.65), channel_id=1, source_target_pairs={{0,1},{1,0},{2,3},{3,2},{4,5},{5,4},{6,7},{7,6},{8,9},{9,8},{10,11... | collective-permute-start | bytes 245768 | tf_op jit(solution)/shard_map/ppermute | solution.py:210

commit v4 on v3

--- a/solution.py
+++ b/solution.py
@@ -11,6 +11,8 @@
 HALF_WIN = 4
 CMP_DEV = 8
 LANES = 128
+UNROLL = 8
+PIECES = 2
 VMEM_BYTES = 16 * 1024 * 1024
 F32 = jnp.float32
 BF16 = jnp.bfloat16
@@ -38,57 +40,63 @@
     )
 
 
-def bin_kernel(kept_rows, width, count, member_ref, *refs):
-    data, (kept_ref, sent_ref, token_ref) = refs[:count], refs[-3:]
+def bin_kernel(orders, count, kept_rows, *refs):
+    members, data = refs[:orders], refs[orders : orders + count]
+    outs, token_ref = refs[-2 * orders - 1 : -1], refs[-1]
     token_ref[...] = jnp.zeros(token_ref.shape, F32)
+    per, cols = data[0].shape
+    width = cols // orders
+    tile = math.gcd(width, 256)
+    for order in range(orders):
+        member_ref = members[order]
+        kept_ref, sent_ref = outs[2 * order : 2 * order + 2]
+        rows = member_ref.shape[0]
+        for start in range(0, kept_ref.shape[1], tile):
+            stop = min(start + tile, kept_ref.shape[1])
+            total = None
+            for at, block in enumerate(data):
+                if start < width:
+                    values = block[:, order * width + start : order * width + stop]
+                else:
+                    values = jnp.ones((per, stop - start), BF16)
+                part = jnp.dot(
+                    member_ref[:, at * per : (at + 1) * per], values, preferred_element_type=F32
+                )
+                total = part if total is None else total + part
+            kept_ref[:, start:stop] = total[:kept_rows]
+            if kept_rows < rows:
+                sent_ref[:, start:stop] = total[kept_rows:].astype(BF16)
+            else:
+                sent_ref[:, start:stop] = jnp.zeros((sent_ref.shape[0], stop - start), BF16)
+
+
+def bin_rows(members, data, start, cols, counted, kept_rows, after):
+    rows = members[0].shape[0]
     per = data[0].shape[0]
-    cols = kept_ref.shape[1]
-    tile = math.gcd(width, 256)
-    for start in range(0, cols, tile):
-        where = slice(start, min(start + tile, cols))
-        total = None
-        for at, block in enumerate(data):
-            values = block[:, where] if start < width else jnp.ones((per, cols - width), BF16)
-            part = jnp.dot(
-                member_ref[:, at * per : (at + 1) * per], values, preferred_element_type=F32
-            )
-            total = part if total is None else total + part
-        kept_ref[:, where] = total[:kept_rows]
-        if kept_rows < total.shape[0]:
-            sent_ref[:, where] = total[kept_rows:].astype(BF16)
-        else:
-            sent_ref[:, where] = jnp.zeros((sent_ref.shape[0], total.shape[1]), BF16)
-
-
-def bin_rows(member, data, start, width, counted, kept_rows, after):
-    rows = member.shape[0]
-    per = data[0].shape[0]
-    cols = width + (LANES if counted else 0)
     sent_rows = max(rows - kept_rows, 16)
-    in_specs = [pl.BlockSpec(member.shape, lambda t: (0, 0))]
-    in_specs += [pl.BlockSpec((per, width), lambda t: (0, start // width))] * len(data)
+    in_specs = [pl.BlockSpec(member.shape, lambda t: (0, 0)) for member in members]
+    in_specs += [pl.BlockSpec((per, cols), lambda t: (0, start // cols))] * len(data)
     in_specs += [ANY] * len(after)
-    return pl.pallas_call(
-        functools.partial(bin_kernel, kept_rows, width, len(data)),
+    shapes = []
+    for at in range(len(members)):
+        width = cols // len(members) + (LANES if counted and at == len(members) - 1 else 0)
+        shapes.append(jax.ShapeDtypeStruct((kept_rows, width), F32))
+        shapes.append(jax.ShapeDtypeStruct((sent_rows, width), BF16))
+    shapes.append(TOKEN)
+    outs = pl.pallas_call(
+        functools.partial(bin_kernel, len(members), len(data), kept_rows),
         grid=(1,),
         in_specs=in_specs,
-        out_specs=[
-            pl.BlockSpec((kept_rows, cols), lambda t: (0, 0)),
-            pl.BlockSpec((sent_rows, cols), lambda t: (0, 0)),
-            pl.BlockSpec(TOKEN.shape, lambda t: (0, 0)),
-        ],
-        out_shape=[
-            jax.ShapeDtypeStruct((kept_rows, cols), F32),
-            jax.ShapeDtypeStruct((sent_rows, cols), BF16),
-            TOKEN,
-        ],
+        out_specs=[pl.BlockSpec(shape.shape, lambda t: (0, 0)) for shape in shapes],
+        out_shape=shapes,
         compiler_params=pltpu.CompilerParams(vmem_limit_bytes=VMEM_BYTES),
         cost_estimate=pl.CostEstimate(
             flops=2 * rows * len(data) * per * cols,
-            bytes_accessed=2 * len(data) * per * cols + 6 * rows * cols,
+            bytes_accessed=0,
             transcendentals=0,
         ),
-    )(member, *data, *after)
+    )(*members, *data, *after)
+    return list(zip(outs[0:-1:2], outs[1:-1:2])), outs[-1]
 
 
 class Plan:
@@ -137,27 +145,13 @@
         return ((row == own[None, :]) | (row == rim[None, :])).astype(BF16)
 
     def bin(self, start, cols, counted, after):
-        width = cols // len(self.orders)
         rows = self.codes * self.block_rows
-        parts = []
-        for at, order in enumerate(self.orders):
-            count_here = counted and at == len(self.orders) - 1
-            parts.append(
-                bin_rows(
-                    self.members[at],
-                    self.data,
-                    start + at * width,
-                    width,
-                    count_here,
-                    rows // 2 if order else rows,
-                    after,
-                )
-            )
-        return parts
+        kept_rows = rows // 2 if self.orders[0] else rows
+        return bin_rows(self.members, self.data, start, cols, counted, kept_rows, after)
 
     def exchange(self, place, parts):
         return [
-            (kept, self.swap(sent, order[place])) for order, (kept, sent, *_) in zip(self.orders, parts)
+            (kept, self.swap(sent, order[place])) for order, (kept, sent) in zip(self.orders, parts)
         ]
 
     def targets(self):
@@ -248,10 +242,10 @@
     for number in pieces:
         chunk_refs.append(refs[at : at + number])
         at += number
-    local_ref, low_ref, high_ref = refs[at : at + 3]
+    index_ref, low_ref, high_ref = refs[at : at + 3]
     at += 3 + waits
     if last < count:
-        later_ref = refs[at]
+        later_ref, stacked_later, semblance_later = refs[at : at + 3]
         at += 3
     stacked_out, semblance_out = refs[at : at + 2]
     at += 2
@@ -267,9 +261,8 @@
         rim_ref,
         window_ref,
         scale_ref,
-        stacked_ref,
-        semblance_ref,
-        copies,
+        band_ref,
+        *staged,
     ) = refs[at:]
     mids = CMP_DEV
     span = last - first
@@ -321,48 +314,11 @@
 
     own_class = [sub16 % classes == h for h in range(classes)]
     group = 2 * classes
-
-    def per_velocity(j, _):
-        for at in range(span):
-            where = slice(at * LANES, (at + 1) * LANES)
-            base = [blocks_ref[h, j * span + at] - first for h in range(classes)]
-            total = energy = None
-            for h in range(classes):
-                row = slice(h, h + 1)
-                index = jnp.broadcast_to(local_ref[j, row, where], (16, LANES)).astype(jnp.int16)
-                low = jnp.broadcast_to(low_ref[j, row, where], (8, LANES))
-                high = jnp.broadcast_to(high_ref[j, row, where], (8, LANES))
-                inner = index & (LANES - 1)
-                got = jnp.where(
-                    index < LANES,
-                    take_lanes(source_ref[h, base[h]], inner),
-                    take_lanes(source_ref[h, base[h] + 1], inner),
-                ).astype(F32)
-                moved = low * got[:8] + high * got[8:]
-                total = moved if total is None else total + moved
-                energy = moved * moved if energy is None else energy + moved * moved
-            sum_ref[at, pl.ds(j, mids, stride=vels), :] = total
-            energy_ref[at, pl.ds(j, mids, stride=vels), :] = energy
-            near = rim_source_ref[base[0]]
-            far = rim_source_ref[base[0] + 1]
-            for h in range(1, classes):
-                near = jnp.where(own_class[h], rim_source_ref[base[h]], near)
-                far = jnp.where(own_class[h], rim_source_ref[base[h] + 1], far)
-            local = local_ref[j, :, where]
-            index = jnp.concatenate([local, local], axis=0).astype(jnp.int16)
-            inner = index & (LANES - 1)
-            got = jnp.where(
-                index < LANES, take_lanes(near, inner), take_lanes(far, inner)
-            ).astype(F32)
-            rim_ref[at, pl.ds(j, group, stride=vels), :] = (
-                low_ref[j, :, where] * got[:8] + high_ref[j, :, where] * got[8:]
-            )
-        return 0
-
-    lax.fori_loop(0, vels, per_velocity, 0, unroll=2)
-
     shape = (mids, vels, LANES)
     rows = mids * vels
+    source = lax.broadcasted_iota(jnp.int32, band_ref.shape, 0) - LANES
+    target = lax.broadcasted_iota(jnp.int32, band_ref.shape, 1)
+    band_ref[...] = jnp.where(jnp.abs(source - target) <= HALF_WIN, 1.0, 0.0).astype(BF16)
     edge = jnp.zeros(window_ref.shape[1:], BF16)
     window_ref[0] = edge
     if last < count:
@@ -371,10 +327,61 @@
     else:
         window_ref[span + 1] = edge
 
+    def moved_out(j, at, where):
+        base = [blocks_ref[h, j * span + at] - first for h in range(classes)]
+        total = energy = None
+        for h in range(classes):
+            row = slice(h, h + 1)
+            local = jnp.broadcast_to(index_ref[j, row, where], (8, LANES))
+            index = jnp.concatenate([local, local], axis=0).astype(jnp.int16)
+            low = jnp.broadcast_to(low_ref[j, row, where], (8, LANES))
+            high = jnp.broadcast_to(high_ref[j, row, where], (8, LANES))
+            inner = index & (LANES - 1)
+            got = jnp.where(
+                index < LANES,
+                take_lanes(source_ref[h, base[h]], inner),
+                take_lanes(source_ref[h, base[h] + 1], inner),
+            ).astype(F32)
+            moved = low * got[:8] + high * got[8:]
+            total = moved if total is None else total + moved
+            energy = moved * moved if energy is None else energy + moved * moved
+        sum_ref[at, pl.ds(j, mids, stride=vels), :] = total
+        energy_ref[at, pl.ds(j, mids, stride=vels), :] = energy
+        near = rim_source_ref[base[0]]
+        far = rim_source_ref[base[0] + 1]
+        for h in range(1, classes):
+            near = jnp.where(own_class[h], rim_source_ref[base[h]], near)
+            far = jnp.where(own_class[h], rim_source_ref[base[h] + 1], far)
+        local = index_ref[j, :, where]
+        index = jnp.concatenate([local, local], axis=0).astype(jnp.int16)
+        inner = index & (LANES - 1)
+        got = jnp.where(index < LANES, take_lanes(near, inner), take_lanes(far, inner)).astype(F32)
+        rim_ref[at, pl.ds(j, group, stride=vels), :] = (
+            low_ref[j, :, where] * got[:8] + high_ref[j, :, where] * got[8:]
+        )
+
     def three(low, mid, high):
         return jnp.concatenate([low, mid[:-1]], axis=0) + mid + jnp.concatenate([mid[1:], high], axis=0)
 
+    begin = 0 if first == 0 else 1
+    end = span + 1 if last < count else span
+    copies = []
+    if first > 0:
+        stacked_ref, semblance_ref = stacked_out, semblance_out
+    else:
+        stacked_ref, semblance_ref, semaphores = staged
+
+        def leave(source, out, begin, end):
+            place = out.at[:, :, begin * LANES : end * LANES]
+            copies.append(pltpu.make_async_copy(source, place, semaphores.at[len(copies)]))
+            copies[-1].start()
+
+        if last < count:
+            leave(stacked_later, stacked_out, last, count)
+            leave(semblance_later, semblance_out, last + 1, count)
+
     def per_block(at, _):
+        where = pl.ds(pl.multiple_of(at * LANES, LANES), LANES)
         total = sum_ref[at].reshape(shape)
         rim = rim_ref[at].reshape(2, classes, vels, LANES)
         rim_sum = jnp.sum(rim, axis=1)
@@ -384,81 +391,86 @@
         energy = three(rim_energy[0:1], energy_ref[at].reshape(shape), rim_energy[1:2])
         window_ref[at + 1, :rows] = power.reshape(rows, LANES).astype(BF16)
         window_ref[at + 1, rows:] = energy.reshape(rows, LANES).astype(BF16)
-        where = pl.ds(pl.multiple_of(at * LANES, LANES), LANES)
         for m in range(mids):
             stacked_ref[m, :, where] = (total[m] * scale_ref[m : m + 1, :]).astype(BF16)
         return 0
 
-    lax.fori_loop(0, span, per_block, 0)
-    stacked_copy = pltpu.make_async_copy(
-        stacked_ref, stacked_out.at[:, :, first * LANES : last * LANES], copies.at[0]
-    )
-    stacked_copy.start()
-
-    def band(blocks):
-        shape = ((blocks + 2) * LANES, blocks * LANES)
-        source = lax.broadcasted_iota(jnp.int32, shape, 0) - LANES
-        target = lax.broadcasted_iota(jnp.int32, shape, 1)
-        return jnp.where(jnp.abs(source - target) <= HALF_WIN, 1.0, 0.0).astype(BF16)
-
-    begin = 0 if first == 0 else 1
-    end = span + 1 if last < count else span
-    wide = band(2)
-    narrow = band(1)
-    at = begin
-    while at < end:
-        blocks = min(2, end - at)
+    def per_window(at, blocks):
         values = jnp.concatenate([window_ref[at + i] for i in range(blocks + 2)], axis=1)
-        summed = jnp.dot(values, wide if blocks == 2 else narrow, preferred_element_type=F32)
+        band = band_ref[: (blocks + 2) * LANES, : blocks * LANES]
+        summed = jnp.dot(values, band, preferred_element_type=F32)
         semblance = summed[:rows] / jnp.maximum(classes * summed[rows:], 1.0)
         semblance_ref[:, :, (at - begin) * LANES : (at - begin + blocks) * LANES] = semblance.reshape(
             mids, vels, blocks * LANES
         )
-        at += blocks
-    semblance_copy = pltpu.make_async_copy(
-        semblance_ref,
-        semblance_out.at[:, :, (first + begin) * LANES : (first + end) * LANES],
-        copies.at[1],
-    )
-    semblance_copy.start()
+
+    pieces = PIECES if first == 0 and span % PIECES == 0 else 1
+    top, finished = span, end
+    for piece in range(pieces):
+        low = top - span // pieces
+
+        def per_velocity(j, _, blocks=range(low, top)):
+            for at in blocks:
+                moved_out(j, at, slice(at * LANES, (at + 1) * LANES))
+            return 0
+
+        lax.fori_loop(0, vels, per_velocity, 0, unroll=math.gcd(vels, UNROLL * pieces))
+        lax.fori_loop(low, top, per_block, 0)
+        if first == 0:
+            leave(stacked_ref.at[:, :, low * LANES : top * LANES], stacked_out, low, top)
+        ready = low + 1 if low else begin
+        for at in range(ready, finished, 2):
+            per_window(at, min(2, finished - at))
+        if first == 0:
+            leave(semblance_ref.at[:, :, ready * LANES : finished * LANES], semblance_out, ready, finished)
+        top, finished = low, ready
     if first > 0:
         carry_ref[0] = window_ref[1]
         carry_ref[1] = window_ref[2]
-    stacked_copy.wait()
-    semblance_copy.wait()
+    for copy in copies:
+        copy.wait()
 
 
 def panels(first, last, count, classes, vels, tables, rows, after, later):
     span = last - first
     held = count - first
-    samples = count * LANES
     group = 2 * classes
     window_rows = 2 * CMP_DEV * vels
-    done = span - (first > 0) + (last < count)
-    outs = [
-        jax.ShapeDtypeStruct((CMP_DEV, vels, samples), BF16),
-        jax.ShapeDtypeStruct((CMP_DEV, vels, samples), F32),
-    ]
-    specs = [ANY] * 2
-    if first > 0:
-        outs.append(jax.ShapeDtypeStruct((2, window_rows, LANES), BF16))
-        specs.append(VMEM)
     flat = [piece for chunk in rows for piece in chunk]
     *tables, blocks = tables
     operands = [blocks, *flat, *tables, *after]
     in_specs = [SMEM] + [VMEM] * (len(flat) + len(tables)) + [ANY] * len(after)
-    aliases = {}
     if later is not None:
         stacked, semblance, carry = later
-        aliases = {len(operands) + 1: 0, len(operands) + 2: 1}
         operands += [carry, stacked, semblance]
-        in_specs += [VMEM, ANY, ANY]
+        in_specs += [VMEM] * 3
+    staged = []
+    if first > 0:
+        outs = [
+            jax.ShapeDtypeStruct((CMP_DEV, vels, span * LANES), BF16),
+            jax.ShapeDtypeStruct((CMP_DEV, vels, (span - 1) * LANES), F32),
+            jax.ShapeDtypeStruct((2, window_rows, LANES), BF16),
+        ]
+        specs = [VMEM] * 3
+    else:
+        outs = [
+            jax.ShapeDtypeStruct((CMP_DEV, vels, count * LANES), BF16),
+            jax.ShapeDtypeStruct((CMP_DEV, vels, count * LANES), F32),
+        ]
+        specs = [ANY] * 2
+        done = span + (last < count)
+        staged = [
+            pltpu.VMEM((CMP_DEV, vels, span * LANES), BF16),
+            pltpu.VMEM((CMP_DEV, vels, done * LANES), F32),
+            pltpu.SemaphoreType.DMA((2 + 2 * PIECES,)),
+        ]
     return pl.pallas_call(
-        functools.partial(panel_kernel, classes, vels, first, last, count, [len(c) for c in rows], len(after)),
+        functools.partial(
+            panel_kernel, classes, vels, first, last, count, [len(c) for c in rows], len(after)
+        ),
         in_specs=in_specs,
         out_specs=specs,
         out_shape=outs,
-        input_output_aliases=aliases,
         scratch_shapes=[
             pltpu.VMEM((held + 1, flat[0].shape[0], LANES), F32),
             pltpu.VMEM((classes, held + 2, 16, LANES), BF16),
@@ -468,9 +480,8 @@
             pltpu.VMEM((span, group * vels, LANES), F32),
             pltpu.VMEM((span + 3, window_rows, LANES), BF16),
             pltpu.VMEM((CMP_DEV, LANES), F32),
-            pltpu.VMEM((CMP_DEV, vels, span * LANES), BF16),
-            pltpu.VMEM((CMP_DEV, vels, done * LANES), F32),
-            pltpu.SemaphoreType.DMA((2,)),
+            pltpu.VMEM((4 * LANES, 2 * LANES), BF16),
+            *staged,
         ],
         compiler_params=pltpu.CompilerParams(vmem_limit_bytes=VMEM_BYTES),
         cost_estimate=pl.CostEstimate(
@@ -482,8 +493,9 @@
 
 
 def table_kernel(classes, start, samples, offsets_ref, velocities_ref, *refs):
-    local_ref, low_ref, high_ref, blocks_ref = refs[-4:]
-    vels, rows, cols = local_ref.shape
+    index_ref, low_ref, high_ref, blocks_ref, token_ref = refs[-5:]
+    token_ref[...] = jnp.zeros(token_ref.shape, F32)
+    vels, rows, cols = low_ref.shape
     lane = lax.broadcasted_iota(jnp.int32, (rows, LANES), 1)
     sub = lax.broadcasted_iota(jnp.int32, (rows, LANES), 0)
     offset = jnp.full((rows, LANES), offsets_ref[0], F32)
@@ -508,7 +520,7 @@
             fraction = position - floored
             index = jnp.minimum(floored, float(samples)).astype(jnp.int32)
             where = slice(at * LANES, (at + 1) * LANES)
-            local_ref[j, :, where] = index - base * LANES
+            index_ref[j, :, where] = index - base * LANES
             low_ref[j, :, where] = (1.0 - fraction).astype(BF16).astype(F32)
             high_ref[j, :, where] = fraction.astype(BF16).astype(F32)
         return tuple(blocks)
@@ -532,16 +544,17 @@
     return pl.pallas_call(
         functools.partial(table_kernel, classes, start, samples),
         in_specs=[SMEM, SMEM] + [ANY] * len(after),
-        out_specs=[VMEM] * 4,
+        out_specs=[VMEM] * 5,
         out_shape=[
             jax.ShapeDtypeStruct(shape, jnp.int32),
             jax.ShapeDtypeStruct(shape, F32),
             jax.ShapeDtypeStruct(shape, F32),
             jax.ShapeDtypeStruct((2 * classes, width), jnp.int32),
+            TOKEN,
         ],
         compiler_params=pltpu.CompilerParams(vmem_limit_bytes=VMEM_BYTES),
         cost_estimate=pl.CostEstimate(
-            flops=14000 * math.prod(shape), bytes_accessed=12 * math.prod(shape), transcendentals=0
+            flops=0, bytes_accessed=0, transcendentals=0
         ),
     )(offsets, velocities, *after)
 
@@ -550,26 +563,35 @@
     samples = traces.shape[1]
     classes, vels = offsets.shape[0], velocities.shape[0]
     count = samples // LANES
-    key = (owners[:, 0] * CMP_DEV + midpoint) * classes + offset_class
+    key = (owners.reshape(-1) * CMP_DEV + midpoint) * classes + offset_class
     plan = Plan(traces, key, classes)
     cuts = [0, samples // 2, samples]
     chunks = list(zip(cuts[:-1], cuts[1:]))[::-1]
-    parts, after = [], [plan.places]
+    parts, tokens = [], [plan.places]
     for start, stop in chunks:
-        parts.append(plan.bin(start, stop - start, stop == samples, after))
-        after = [parts[-1][-1][2]]
-    steps = len(plan.orders[0])
-    tables, rows, tokens = [], [], []
-    for at, chunk in enumerate(chunks):
-        tables.append(moveout(offsets, velocities, samples, *chunk, after))
+        part, token = plan.bin(start, stop - start, stop == samples, tokens[-1:])
+        parts.append(part)
+        tokens.append(token)
+    tables, spreads = [], []
+    *table, token = moveout(offsets, velocities, samples, *chunks[0], tokens[-1:])
+    tables.append(table)
+    tokens.append(token)
+    for at in range(len(chunks)):
         part = plan.exchange(0, parts[at])
-        for place in range(1, steps):
-            part, token = plan.merge(part, after)
+        for place in range(1, len(plan.orders[0])):
+            part, token = plan.merge(part, tokens[-1:])
             part = plan.exchange(place, part)
-        *spread, token = plan.spread(part, [rows[-1][1]] if rows else [])
+            tokens.append(token)
+        spreads.append(part)
+    rows, tokens = [], []
+    for part in spreads:
+        *spread, token = plan.spread(part, tokens[-1:])
         rows.append(plan.across(spread))
         tokens.append(token)
-        after = [token]
+    for chunk in chunks[1:]:
+        *table, token = moveout(offsets, velocities, samples, *chunk, tokens[-1:])
+        tables.append(table)
+        tokens.append(token)
     out = None
     for at, (start, stop) in enumerate(chunks):
         out = panels(
@@ -580,7 +602,7 @@
             vels,
             tables[at],
             rows[: at + 1][::-1],
-            tokens[at + 1 : at + 2],
+            tokens[-1:] if not at else [],
             out,
         )
     return (out[0], out[1])

time: 56 us -> 53.6 us (0.957)
  Pallas kernels: 21.1 us -> 17.5 us
  starting transfers between devices: 18.4 us -> 20.8 us
  waiting for transfers between devices: 13.3 us -> 12 us
    ppermute x10, waiting for transfers between devices: 13.3 us -> 8.83 us  [swap(): lax.ppermute(value, 'inline', [(i, i ^ bit) for i in range(self.inline)])]
    ppermute x6, waiting for transfers between devices: 0.02 us -> 3.19 us  [across(): lax.ppermute(block, 'xline', pairs)]
    ppermute x10, starting transfers between devices: 9.52 us -> 11.5 us  [swap(): lax.ppermute(value, 'inline', [(i, i ^ bit) for i in range(self.inline)])]
    pallas_call x2, Pallas kernels: 12.3 us -> 10.7 us  [panels(): pl.pallas_call(functools.partial(panel_kernel, classes, vels, first, last...]
    pallas_call x4 -> x2, Pallas kernels: 3.01 us -> 1.66 us  [bin_rows(): pl.pallas_call(functools.partial(bin_kernel, len(members), len(data), kep...]
    pallas_call x2, Pallas kernels: 1.39 us -> 0.82 us  [merge(): pl.pallas_call(functools.partial(merge_kernel, len(parts)), in_specs=[VME...]
  transfers between devices with their start and end apart: 16 -> 16, of which waited for: 6 -> 4; matrix products, arithmetic and copies ran while one was open for 4% -> 4% of each run, Pallas kernels for 25% -> 20%
where the time goes in v4:
time: 53.6 us; the launch traced here: 53.4 us
  starting transfers between devices  20.8 us (39%)
  Pallas kernels  17.5 us (33%)
  waiting for transfers between devices  12 us (22%)
  other arithmetic  2.26 us (4%)
  between operations  0.77 us (1%)
    ppermute x10, starting transfers between devices, swap(): lax.ppermute(value, 'inline', [(i, i ^ bit) for i in range(self.inline)])  11.5 us
    pallas_call x2, Pallas kernels, panels(): pl.pallas_call(functools.partial(panel_kernel, classes, vels, first, last...  10.7 us
    ppermute x6, starting transfers between devices, across(): lax.ppermute(block, 'xline', pairs)  9.28 us
    ppermute x10, waiting for transfers between devices, swap(): lax.ppermute(value, 'inline', [(i, i ^ bit) for i in range(self.inline)])  8.83 us
    ppermute x6, waiting for transfers between devices, across(): lax.ppermute(block, 'xline', pairs)  3.19 us
    pallas_call x2, Pallas kernels, moveout(): pl.pallas_call(functools.partial(table_kernel, classes, start, samples),...  3.05 us
    pallas_call x2, Pallas kernels, bin_rows(): pl.pallas_call(functools.partial(bin_kernel, len(members), len(data), kep...  1.66 us
    pallas_call x2, Pallas kernels, spread(): pl.pallas_call(functools.partial(spread_kernel, len(parts), len(kinds)),...  1.28 us
  transfers between devices with their start and end apart: 16, of which 4 were waited for; matrix products, arithmetic and copies ran while one was open for 4% of the time, Pallas kernels for 20%

profile of v4, /device:TPU:0, one launch (start us, length us, event | category | flops | bytes accessed | tf_op | source)
XLA Modules:
  0.0 53.4 jit_solution(330495735604629479)
XLA Ops:
  0.6 0.0 copy-start
  0.6 0.5 collective-permute-start.1
  1.2 0.7 %broadcast_multiply_fusion = s32[256,1]{0,1:T(1,128)S(1)} fusion(s32[256,1]{0,1:T(1,128)} %param.7), kind=kLoop, calls=%fused_computation.72 | loop fusion | flops 256 | bytes 2048 | tf_op jit(solution)/shard_map/mul | solution.py:566
  1.8 0.7 %multiply_add_fusion = s32[256]{0:T(256)S(1)} fusion(s32[256]{0:T(256)} %param.9, s32[256]{0:T(256)S(1)} %bitcast.5, s32[256]{0:T(256)} %param.8), kind=kLoop, calls=%fused_computation.70 | loop fusion | flops 768 | bytes 4096 | tf_op jit(solution)/shard_map/add | solution.py:566
  2.5 0.1 collective-permute-start
  2.7 0.1 add_multiply_fusion.refs_4_.places_ref
  2.7 0.9 %collective-permute-done = s32[256]{0:T(256)S(1)} collective-permute-done((s32[256]{0:T(256)S(1)}, s32[256]{0:T(256)S(1)}, u32[]{:S(2)}, u32[]{:S(2)}) %collective-permute-start) | collective-permute-done | bytes 1056 | tf_op jit(solution)/shard_map/ppermute | solution.py:124
  3.8 0.7 %fusion.1 = (bf16[544,512]{1,0:T(8,128)(2,1)S(1)}, bf16[544,512]{1,0:T(8,128)(2,1)S(1)}) fusion(s32[512]{0:T(512)S(1)} %fusion.17, s32[512]{0:T(512)S(1)} %get-tuple-element.96, s32[512]{0:T(512)S(1)} %get-tuple-element.91, s32[512]{0:T(512)S(1)} %get-tuple-element.86), kind=kLoop, calls=%fused_computation.5 | loop fusion | flops 2228224 | bytes 1122304 | tf_op jit(solution)/shard_map/convert_element_type | solution.py:145
  4.5 0.0 collective-permute-done.1.refs_3_
  4.5 0.0 copy-done
  4.5 0.9 %shard_map.77 = (f32[272,512]{1,0:T(8,128)S(1)}, bf16[272,512]{1,0:T(8,128)(2,1)S(1)}, f32[272,640]{1,0:T(8,128)S(1)}, bf16[272,640]{1,0:T(8,128)(2,1)S(1)}, f32[8,128]{1,0:T(8,128)S(1)}) custom-call(bf16[544,512]{1,0:T(8,128)(2,1)S(1)} %get-tuple-element.97.refs_0_, bf16[544,512]{1,0:T(8,128)(2,1)S(1)} %get-tuple-element.98.refs_1_, ...), custom_call_target="tpu_custom_call" | custom-call | flops 570425344 | tf_op jit(solution)/shard_map/pallas_call | solution.py:86
  5.4 2.8 %collective-permute-start.5 = (bf16[272,640]{1,0:T(8,128)(2,1)S(1)}, bf16[272,640]{1,0:T(8,128)(2,1)S(1)}, u32[]{:S(2)}, u32[]{:S(2)}) collective-permute-start(bf16[272,640]{1,0:T(8,128)(2,1)S(1)} %get-tuple-element.52), channel_id=1, source_target_pairs={{0,16},{4,20},{8,24},{12,28},{16,0},{20,4},{24,8},{28,12},{1,17},{... | collective-permute-start | bytes 1044488 | tf_op jit(solution)/shard_map/ppermute | solution.py:124
  8.2 1.5 %collective-permute-start.4 = (bf16[272,512]{1,0:T(8,128)(2,1)S(1)}, bf16[272,512]{1,0:T(8,128)(2,1)S(1)}, u32[]{:S(2)}, u32[]{:S(2)}) collective-permute-start(bf16[272,512]{1,0:T(8,128)(2,1)S(1)} %get-tuple-element.50), channel_id=1, source_target_pairs={{0,8},{4,12},{8,0},{12,4},{16,24},{20,28},{24,16},{28,20},{1,9},{5... | collective-permute-start | bytes 835592 | tf_op jit(solution)/shard_map/ppermute | solution.py:124
  9.7 0.7 %shard_map.78 = (f32[272,512]{1,0:T(8,128)S(1)}, bf16[272,512]{1,0:T(8,128)(2,1)S(1)}, f32[272,512]{1,0:T(8,128)S(1)}, bf16[272,512]{1,0:T(8,128)(2,1)S(1)}, f32[8,128]{1,0:T(8,128)S(1)}) custom-call(bf16[544,512]{1,0:T(8,128)(2,1)S(1)} %get-tuple-element.97.refs_0_, bf16[544,512]{1,0:T(8,128)(2,1)S(1)} %get-tuple-element.98.refs_1_, ...), custom_call_target="tpu_custom_call" | custom-call | flops 570425344 | tf_op jit(solution)/shard_map/pallas_call | solution.py:86
  10.5 0.6 %collective-permute-start.2 = (bf16[272,512]{1,0:T(8,128)(2,1)S(1)}, bf16[272,512]{1,0:T(8,128)(2,1)S(1)}, u32[]{:S(2)}, u32[]{:S(2)}) collective-permute-start(bf16[272,512]{1,0:T(8,128)(2,1)S(1)} %get-tuple-element.46), channel_id=1, source_target_pairs={{0,8},{4,12},{8,0},{12,4},{16,24},{20,28},{24,16},{28,20},{1,9},{5... | collective-permute-start | bytes 835592 | tf_op jit(solution)/shard_map/ppermute | solution.py:124
  11.1 0.1 collective-permute-start.3
  11.1 1.5 %shard_map.79 = (s32[16,8,1024]{2,1,0:T(8,128)S(1)}, f32[16,8,1024]{2,1,0:T(8,128)S(1)}, f32[16,8,1024]{2,1,0:T(8,128)S(1)}, s32[8,128]{1,0:T(8,128)S(1)}, f32[8,128]{1,0:T(8,128)S(1)}) custom-call(f32[4]{0:T(128)S(1)} %copy-done.1, f32[16]{0:T(128)S(1)} %copy-done.2, f32[8,128]{1,0:T(8,128)S(1)} %get-tuple-element.53.refs_0_), custom_call_target="tpu_custom_call" | custom-call | tf_op jit(solution)/shard_map/pallas_call | solution.py:544
  12.7 5.1 %collective-permute-done.4.refs_1_ = bf16[272,512]{1,0:T(8,128)(2,1)S(1)} collective-permute-done((bf16[272,512]{1,0:T(8,128)(2,1)S(1)}, bf16[272,512]{1,0:T(8,128)(2,1)S(1)}, u32[]{:S(2)}, u32[]{:S(2)}) %collective-permute-start.4) | collective-permute-done | bytes 278560 | tf_op jit(solution)/shard_map/ppermute | solution.py:124
  17.7 0.0 collective-permute-done.5.refs_3_
  17.7 0.1 shard_map.80
  17.9 1.5 %collective-permute-start.9 = (bf16[136,640]{1,0:T(8,128)(2,1)S(1)}, bf16[136,640]{1,0:T(8,128)(2,1)S(1)}, u32[]{:S(2)}, u32[]{:S(2)}) collective-permute-start(bf16[136,640]{1,0:T(8,128)(2,1)S(1)} %get-tuple-element.63), channel_id=1, source_target_pairs={{0,8},{4,12},{8,0},{12,4},{16,24},{20,28},{24,16},{28,20},{1,9},{5... | collective-permute-start | bytes 522248 | tf_op jit(solution)/shard_map/ppermute | solution.py:124
  19.4 1.4 %collective-permute-start.8 = (bf16[136,512]{1,0:T(8,128)(2,1)S(1)}, bf16[136,512]{1,0:T(8,128)(2,1)S(1)}, u32[]{:S(2)}, u32[]{:S(2)}) collective-permute-start(bf16[136,512]{1,0:T(8,128)(2,1)S(1)} %get-tuple-element.61), channel_id=1, source_target_pairs={{0,16},{4,20},{8,24},{12,28},{16,0},{20,4},{24,8},{28,12},{1,17},{... | collective-permute-start | bytes 417800 | tf_op jit(solution)/shard_map/ppermute | solution.py:124
  20.9 2.8 %collective-permute-done.2.refs_1_ = bf16[272,512]{1,0:T(8,128)(2,1)S(1)} collective-permute-done((bf16[272,512]{1,0:T(8,128)(2,1)S(1)}, bf16[272,512]{1,0:T(8,128)(2,1)S(1)}, u32[]{:S(2)}, u32[]{:S(2)}) %collective-permute-start.2) | collective-permute-done | bytes 278560 | tf_op jit(solution)/shard_map/ppermute | solution.py:124
  23.7 0.0 collective-permute-done.3.refs_3_
  23.7 0.7 %shard_map.81 = (f32[136,512]{1,0:T(8,128)S(1)}, bf16[136,512]{1,0:T(8,128)(2,1)S(1)}, f32[136,512]{1,0:T(8,128)S(1)}, bf16[136,512]{1,0:T(8,128)(2,1)S(1)}, f32[8,128]{1,0:T(8,128)}) custom-call(f32[272,512]{1,0:T(8,128)S(1)} %get-tuple-element.45.refs_0_, bf16[272,512]{1,0:T(8,128)(2,1)S(1)} %collective-permute-done.2.refs_1_, ...), custom_call_target="tpu_custom_call" | custom-call | bytes 3342336 | tf_op jit(solution)/shard_map/pallas_call | solution.py:176
  24.4 1.4 %collective-permute-start.6 = (bf16[136,512]{1,0:T(8,128)(2,1)S(1)}, bf16[136,512]{1,0:T(8,128)(2,1)S(1)}, u32[]{:S(2)}, u32[]{:S(2)}) collective-permute-start(bf16[136,512]{1,0:T(8,128)(2,1)S(1)} %get-tuple-element.57), channel_id=1, source_target_pairs={{0,16},{4,20},{8,24},{12,28},{16,0},{20,4},{24,8},{28,12},{1,17},{... | collective-permute-start | bytes 417800 | tf_op jit(solution)/shard_map/ppermute | solution.py:124
  25.8 1.5 %collective-permute-start.7 = (bf16[136,512]{1,0:T(8,128)(2,1)S(1)}, bf16[136,512]{1,0:T(8,128)(2,1)S(1)}, u32[]{:S(2)}, u32[]{:S(2)}) collective-permute-start(bf16[136,512]{1,0:T(8,128)(2,1)S(1)} %get-tuple-element.59), channel_id=1, source_target_pairs={{0,8},{4,12},{8,0},{12,4},{16,24},{20,28},{24,16},{28,20},{1,9},{5... | collective-permute-start | bytes 417800 | tf_op jit(solution)/shard_map/ppermute | solution.py:124
  27.3 0.0 collective-permute-done.8.refs_1_
  27.3 0.0 collective-permute-done.9.refs_3_
  27.3 0.6 %shard_map.82 = (f32[40,1152]{1,0:T(8,128)S(1)}, bf16[40,1152]{1,0:T(8,128)(2,1)S(1)}, bf16[40,1152]{1,0:T(8,128)(2,1)S(1)}, bf16[40,1152]{1,0:T(8,128)(2,1)S(1)}, f32[8,128]{1,0:T(8,128)S(1)}) custom-call(s32[4]{0:T(128)S(1)} %add_multiply_fusion.refs_4_.places_ref, f32[136,512]{1,0:T(8,128)S(1)} %get-tuple-element.60.refs_0_, ...), custom_call_target="tpu_custom_call" | custom-call | bytes 1880064 | tf_op jit(solution)/shard_map/pallas_call | solution.py:191
  28.0 3.7 %collective-permute-start.13 = (bf16[40,1152]{1,0:T(8,128)(2,1)S(1)}, bf16[40,1152]{1,0:T(8,128)(2,1)S(1)}, u32[]{:S(2)}, u32[]{:S(2)}) collective-permute-start(bf16[40,1152]{1,0:T(8,128)(2,1)S(1)} %get-tuple-element.72), channel_id=1, source_target_pairs={{0,3},{1,2},{2,1},{3,0},{4,7},{5,6},{6,5},{7,4},{8,11},{9,10},{10,... | collective-permute-start | bytes 276488 | tf_op jit(solution)/shard_map/ppermute | solution.py:204
  31.6 0.0 collective-permute-start.14
  31.7 0.8 %collective-permute-start.15 = (bf16[40,1152]{1,0:T(8,128)(2,1)S(1)}, bf16[40,1152]{1,0:T(8,128)(2,1)S(1)}, u32[]{:S(2)}, u32[]{:S(2)}) collective-permute-start(bf16[40,1152]{1,0:T(8,128)(2,1)S(1)} %get-tuple-element.74), channel_id=1, source_target_pairs={{0,1},{1,0},{2,3},{3,2},{4,5},{5,4},{6,7},{7,6},{8,9},{9,8},{10,11... | collective-permute-start | bytes 276488 | tf_op jit(solution)/shard_map/ppermute | solution.py:204
  32.4 0.0 collective-permute-done.6.refs_1_
  32.4 0.0 collective-permute-done.7.refs_3_
  32.4 0.6 %shard_map.83 = (f32[40,1024]{1,0:T(8,128)S(1)}, bf16[40,1024]{1,0:T(8,128)(2,1)S(1)}, bf16[40,1024]{1,0:T(8,128)(2,1)S(1)}, bf16[40,1024]{1,0:T(8,128)(2,1)S(1)}, f32[8,128]{1,0:T(8,128)S(1)}) custom-call(s32[4]{0:T(128)S(1)} %add_multiply_fusion.refs_4_.places_ref, f32[136,512]{1,0:T(8,128)S(1)} %get-tuple-element.56.refs_0_, ...), custom_call_target="tpu_custom_call" | custom-call | bytes 1671168 | tf_op jit(solution)/shard_map/pallas_call | solution.py:191
  33.1 3.7 %collective-permute-start.10 = (bf16[40,1024]{1,0:T(8,128)(2,1)S(1)}, bf16[40,1024]{1,0:T(8,128)(2,1)S(1)}, u32[]{:S(2)}, u32[]{:S(2)}) collective-permute-start(bf16[40,1024]{1,0:T(8,128)(2,1)S(1)} %get-tuple-element.68), channel_id=1, source_target_pairs={{0,3},{1,2},{2,1},{3,0},{4,7},{5,6},{6,5},{7,4},{8,11},{9,10},{10,... | collective-permute-start | bytes 245768 | tf_op jit(solution)/shard_map/ppermute | solution.py:204
  36.7 0.0 collective-permute-start.11
  36.8 1.5 %shard_map.84 = (s32[16,8,1024]{2,1,0:T(8,128)S(1)}, f32[16,8,1024]{2,1,0:T(8,128)S(1)}, f32[16,8,1024]{2,1,0:T(8,128)S(1)}, s32[8,128]{1,0:T(8,128)S(1)}, f32[8,128]{1,0:T(8,128)S(1)}) custom-call(f32[4]{0:T(128)S(1)} %copy-done.1, f32[16]{0:T(128)S(1)} %copy-done.2, f32[8,128]{1,0:T(8,128)S(1)} %get-tuple-element.65.refs_0_), custom_call_target="tpu_custom_call" | custom-call | tf_op jit(solution)/shard_map/pallas_call | solution.py:544
  38.3 0.0 collective-permute-done.13.refs_2_.refs_6_
  38.3 1.1 %collective-permute-start.12 = (bf16[40,1024]{1,0:T(8,128)(2,1)S(1)}, bf16[40,1024]{1,0:T(8,128)(2,1)S(1)}, u32[]{:S(2)}, u32[]{:S(2)}) collective-permute-start(bf16[40,1024]{1,0:T(8,128)(2,1)S(1)} %get-tuple-element.70), channel_id=1, source_target_pairs={{0,1},{1,0},{2,3},{3,2},{4,5},{5,4},{6,7},{7,6},{8,9},{9,8},{10,11... | collective-permute-start | bytes 245768 | tf_op jit(solution)/shard_map/ppermute | solution.py:204
  39.4 3.2 %collective-permute-done.14.refs_3_.refs_7_ = bf16[40,1152]{1,0:T(8,128)(2,1)S(1)} collective-permute-done((bf16[40,1152]{1,0:T(8,128)(2,1)S(1)}, bf16[40,1152]{1,0:T(8,128)(2,1)S(1)}, u32[]{:S(2)}, u32[]{:S(2)}) %collective-permute-start.14) | collective-permute-done | bytes 92192 | tf_op jit(solution)/shard_map/ppermute | solution.py:204
  42.6 0.0 collective-permute-done.15.refs_4_.refs_8_
  42.6 4.9 %shard_map.85 = (bf16[8,16,1024]{2,1,0:T(8,128)(2,1)S(1)}, f32[8,16,896]{2,1,0:T(8,128)S(1)}, bf16[2,256,128]{2,1,0:T(8,128)(2,1)S(1)}) custom-call(s32[8,128]{1,0:T(8,128)S(1)} %get-tuple-element.78.refs_0_, f32[40,1152]{1,0:T(8,128)S(1)} %get-tuple-element.71.refs_1_.refs_5_, bf16[40,1152]{1,0:T(8,128)(2,1)S(1)} %collective-permute-done.13.refs_2_.refs_6_, ...), custom_call_target="tpu_custom_call" | custom-call | flops 7340032000 | bytes 4718592 | tf_op jit(solution)/shard_map/pallas_call | solution.py:467
  47.5 0.0 collective-permute-done.10.refs_2_
  47.5 0.0 collective-permute-done.11.refs_3_
  47.5 0.0 collective-permute-done.12.refs_4_
  47.6 5.8 %shard_map.86 = (bf16[8,16,2048]{2,1,0:T(8,128)(2,1)}, f32[8,16,2048]{2,1,0:T(8,128)}) custom-call(s32[8,128]{1,0:T(8,128)S(1)} %get-tuple-element.66.refs_0_, f32[40,1024]{1,0:T(8,128)S(1)} %get-tuple-element.67.refs_1_, bf16[40,1024]{1,0:T(8,128)(2,1)S(1)} %collective-permute-done.10.refs_2_, bf16[40,1024]{1,0:T(8,128)(2,1)S(1)} %collective-permute-done.11.refs_3_, ...), custom_call_target="tpu_custom_call" | custom-call | flops 7340032000 | bytes 4718592 | tf_op jit(solution)/shard_map/pallas_call | solution.py:467
  (7 shorter events, 0.1 us)
Async XLA Ops:
  0.6 3.9 %copy-start = (bf16[256,2048]{1,0:T(8,128)(2,1)S(1)}, bf16[256,2048]{1,0:T(8,128)(2,1)}, u32[]{:S(2)}) copy-start(bf16[256,2048]{1,0:T(8,128)(2,1)} %refs_2_.3) | copy-start | bytes 3145732
  0.6 3.9 %collective-permute-start.1 = (bf16[256,2048]{1,0:T(8,128)(2,1)}, bf16[256,2048]{1,0:T(8,128)(2,1)S(1)}, u32[]{:S(2)}, u32[]{:S(2)}) collective-permute-start(bf16[256,2048]{1,0:T(8,128)(2,1)} %refs_2_.3), channel_id=1, source_target_pairs={{0,4},{4,0},{8,12},{12,8},{16,20},{20,16},{24,28},{28,24},{1,5},{5... | collective-permute-start | bytes 3145736 | tf_op jit(solution)/shard_map/ppermute | solution.py:124
  2.5 1.1 %collective-permute-start = (s32[256]{0:T(256)S(1)}, s32[256]{0:T(256)S(1)}, u32[]{:S(2)}, u32[]{:S(2)}) collective-permute-start(s32[256]{0:T(256)S(1)} %multiply_add_fusion), channel_id=1, source_target_pairs={{0,4},{4,0},{8,12},{12,8},{16,20},{20,16},{24,28},{28,24},{1,5},{5... | collective-permute-start | bytes 3080 | tf_op jit(solution)/shard_map/ppermute | solution.py:124
  5.4 12.3 %collective-permute-start.5 = (bf16[272,640]{1,0:T(8,128)(2,1)S(1)}, bf16[272,640]{1,0:T(8,128)(2,1)S(1)}, u32[]{:S(2)}, u32[]{:S(2)}) collective-permute-start(bf16[272,640]{1,0:T(8,128)(2,1)S(1)} %get-tuple-element.52), channel_id=1, source_target_pairs={{0,16},{4,20},{8,24},{12,28},{16,0},{20,4},{24,8},{28,12},{1,17},{... | collective-permute-start | bytes 1044488 | tf_op jit(solution)/shard_map/ppermute | solution.py:124
  8.2 9.5 %collective-permute-start.4 = (bf16[272,512]{1,0:T(8,128)(2,1)S(1)}, bf16[272,512]{1,0:T(8,128)(2,1)S(1)}, u32[]{:S(2)}, u32[]{:S(2)}) collective-permute-start(bf16[272,512]{1,0:T(8,128)(2,1)S(1)} %get-tuple-element.50), channel_id=1, source_target_pairs={{0,8},{4,12},{8,0},{12,4},{16,24},{20,28},{24,16},{28,20},{1,9},{5... | collective-permute-start | bytes 835592 | tf_op jit(solution)/shard_map/ppermute | solution.py:124
  9.7 1.4 %copy-start.1 = (f32[4]{0:T(128)S(1)}, f32[4]{0:T(128)}, u32[]{:S(2)}) copy-start(f32[4]{0:T(128)} %offsets_ref.3) | copy-start | bytes 52
  9.7 1.4 %copy-start.2 = (f32[16]{0:T(128)S(1)}, f32[16]{0:T(128)}, u32[]{:S(2)}) copy-start(f32[16]{0:T(128)} %velocities_ref.3) | copy-start | bytes 196
  10.5 13.2 %collective-permute-start.2 = (bf16[272,512]{1,0:T(8,128)(2,1)S(1)}, bf16[272,512]{1,0:T(8,128)(2,1)S(1)}, u32[]{:S(2)}, u32[]{:S(2)}) collective-permute-start(bf16[272,512]{1,0:T(8,128)(2,1)S(1)} %get-tuple-element.46), channel_id=1, source_target_pairs={{0,8},{4,12},{8,0},{12,4},{16,24},{20,28},{24,16},{28,20},{1,9},{5... | collective-permute-start | bytes 835592 | tf_op jit(solution)/shard_map/ppermute | solution.py:124
  11.1 12.6 %collective-permute-start.3 = (bf16[272,512]{1,0:T(8,128)(2,1)S(1)}, bf16[272,512]{1,0:T(8,128)(2,1)S(1)}, u32[]{:S(2)}, u32[]{:S(2)}) collective-permute-start(bf16[272,512]{1,0:T(8,128)(2,1)S(1)} %get-tuple-element.48), channel_id=1, source_target_pairs={{0,16},{4,20},{8,24},{12,28},{16,0},{20,4},{24,8},{28,12},{1,17},{... | collective-permute-start | bytes 835592 | tf_op jit(solution)/shard_map/ppermute | solution.py:124
  17.9 9.4 %collective-permute-start.9 = (bf16[136,640]{1,0:T(8,128)(2,1)S(1)}, bf16[136,640]{1,0:T(8,128)(2,1)S(1)}, u32[]{:S(2)}, u32[]{:S(2)}) collective-permute-start(bf16[136,640]{1,0:T(8,128)(2,1)S(1)} %get-tuple-element.63), channel_id=1, source_target_pairs={{0,8},{4,12},{8,0},{12,4},{16,24},{20,28},{24,16},{28,20},{1,9},{5... | collective-permute-start | bytes 522248 | tf_op jit(solution)/shard_map/ppermute | solution.py:124
  19.4 7.9 %collective-permute-start.8 = (bf16[136,512]{1,0:T(8,128)(2,1)S(1)}, bf16[136,512]{1,0:T(8,128)(2,1)S(1)}, u32[]{:S(2)}, u32[]{:S(2)}) collective-permute-start(bf16[136,512]{1,0:T(8,128)(2,1)S(1)} %get-tuple-element.61), channel_id=1, source_target_pairs={{0,16},{4,20},{8,24},{12,28},{16,0},{20,4},{24,8},{28,12},{1,17},{... | collective-permute-start | bytes 417800 | tf_op jit(solution)/shard_map/ppermute | solution.py:124
  24.4 8.0 %collective-permute-start.6 = (bf16[136,512]{1,0:T(8,128)(2,1)S(1)}, bf16[136,512]{1,0:T(8,128)(2,1)S(1)}, u32[]{:S(2)}, u32[]{:S(2)}) collective-permute-start(bf16[136,512]{1,0:T(8,128)(2,1)S(1)} %get-tuple-element.57), channel_id=1, source_target_pairs={{0,16},{4,20},{8,24},{12,28},{16,0},{20,4},{24,8},{28,12},{1,17},{... | collective-permute-start | bytes 417800 | tf_op jit(solution)/shard_map/ppermute | solution.py:124
  25.8 6.6 %collective-permute-start.7 = (bf16[136,512]{1,0:T(8,128)(2,1)S(1)}, bf16[136,512]{1,0:T(8,128)(2,1)S(1)}, u32[]{:S(2)}, u32[]{:S(2)}) collective-permute-start(bf16[136,512]{1,0:T(8,128)(2,1)S(1)} %get-tuple-element.59), channel_id=1, source_target_pairs={{0,8},{4,12},{8,0},{12,4},{16,24},{20,28},{24,16},{28,20},{1,9},{5... | collective-permute-start | bytes 417800 | tf_op jit(solution)/shard_map/ppermute | solution.py:124
  28.0 10.3 %collective-permute-start.13 = (bf16[40,1152]{1,0:T(8,128)(2,1)S(1)}, bf16[40,1152]{1,0:T(8,128)(2,1)S(1)}, u32[]{:S(2)}, u32[]{:S(2)}) collective-permute-start(bf16[40,1152]{1,0:T(8,128)(2,1)S(1)} %get-tuple-element.72), channel_id=1, source_target_pairs={{0,3},{1,2},{2,1},{3,0},{4,7},{5,6},{6,5},{7,4},{8,11},{9,10},{10,... | collective-permute-start | bytes 276488 | tf_op jit(solution)/shard_map/ppermute | solution.py:204
  31.6 11.0 %collective-permute-start.14 = (bf16[40,1152]{1,0:T(8,128)(2,1)S(1)}, bf16[40,1152]{1,0:T(8,128)(2,1)S(1)}, u32[]{:S(2)}, u32[]{:S(2)}) collective-permute-start(bf16[40,1152]{1,0:T(8,128)(2,1)S(1)} %get-tuple-element.73), channel_id=1, source_target_pairs={{0,2},{1,3},{2,0},{3,1},{4,6},{5,7},{6,4},{7,5},{8,10},{9,11},{10,... | collective-permute-start | bytes 276488 | tf_op jit(solution)/shard_map/ppermute | solution.py:204
  31.7 11.0 %collective-permute-start.15 = (bf16[40,1152]{1,0:T(8,128)(2,1)S(1)}, bf16[40,1152]{1,0:T(8,128)(2,1)S(1)}, u32[]{:S(2)}, u32[]{:S(2)}) collective-permute-start(bf16[40,1152]{1,0:T(8,128)(2,1)S(1)} %get-tuple-element.74), channel_id=1, source_target_pairs={{0,1},{1,0},{2,3},{3,2},{4,5},{5,4},{6,7},{7,6},{8,9},{9,8},{10,11... | collective-permute-start | bytes 276488 | tf_op jit(solution)/shard_map/ppermute | solution.py:204
  33.1 14.5 %collective-permute-start.10 = (bf16[40,1024]{1,0:T(8,128)(2,1)S(1)}, bf16[40,1024]{1,0:T(8,128)(2,1)S(1)}, u32[]{:S(2)}, u32[]{:S(2)}) collective-permute-start(bf16[40,1024]{1,0:T(8,128)(2,1)S(1)} %get-tuple-element.68), channel_id=1, source_target_pairs={{0,3},{1,2},{2,1},{3,0},{4,7},{5,6},{6,5},{7,4},{8,11},{9,10},{10,... | collective-permute-start | bytes 245768 | tf_op jit(solution)/shard_map/ppermute | solution.py:204
  36.7 10.8 %collective-permute-start.11 = (bf16[40,1024]{1,0:T(8,128)(2,1)S(1)}, bf16[40,1024]{1,0:T(8,128)(2,1)S(1)}, u32[]{:S(2)}, u32[]{:S(2)}) collective-permute-start(bf16[40,1024]{1,0:T(8,128)(2,1)S(1)} %get-tuple-element.69), channel_id=1, source_target_pairs={{0,2},{1,3},{2,0},{3,1},{4,6},{5,7},{6,4},{7,5},{8,10},{9,11},{10,... | collective-permute-start | bytes 245768 | tf_op jit(solution)/shard_map/ppermute | solution.py:204
  38.3 9.3 %collective-permute-start.12 = (bf16[40,1024]{1,0:T(8,128)(2,1)S(1)}, bf16[40,1024]{1,0:T(8,128)(2,1)S(1)}, u32[]{:S(2)}, u32[]{:S(2)}) collective-permute-start(bf16[40,1024]{1,0:T(8,128)(2,1)S(1)} %get-tuple-element.70), channel_id=1, source_target_pairs={{0,1},{1,0},{2,3},{3,2},{4,5},{5,4},{6,7},{7,6},{8,9},{9,8},{10,11... | collective-permute-start | bytes 245768 | tf_op jit(solution)/shard_map/ppermute | solution.py:204

commit v5 on v4

--- a/solution.py
+++ b/solution.py
@@ -198,11 +198,12 @@
             cost_estimate=cost_of(flat),
         )(self.places, *flat, *after)
 
-    def across(self, blocks):
+    def across(self, blocks, near_first):
         own, *sent = blocks
-        return [own] + [
-            lax.ppermute(block, "xline", pairs) for block, (_, pairs) in zip(sent, self.targets())
-        ]
+        moves = [(block, pairs) for block, (_, pairs) in zip(sent, self.targets())]
+        if near_first:
+            moves = moves[::-1]
+        return [own] + [lax.ppermute(block, "xline", pairs) for block, pairs in moves]
 
 
 def cost_of(values):
@@ -415,7 +416,7 @@
             return 0
 
         lax.fori_loop(0, vels, per_velocity, 0, unroll=math.gcd(vels, UNROLL * pieces))
-        lax.fori_loop(low, top, per_block, 0)
+        lax.fori_loop(low, top, per_block, 0, unroll=math.gcd(top - low, 2 * pieces))
         if first == 0:
             leave(stacked_ref.at[:, :, low * LANES : top * LANES], stacked_out, low, top)
         ready = low + 1 if low else begin
@@ -584,13 +585,13 @@
             tokens.append(token)
         spreads.append(part)
     rows, tokens = [], []
-    for part in spreads:
+    for at, part in enumerate(spreads):
+        if at:
+            *table, token = moveout(offsets, velocities, samples, *chunks[at], tokens[-1:])
+            tables.append(table)
+            tokens.append(token)
         *spread, token = plan.spread(part, tokens[-1:])
-        rows.append(plan.across(spread))
-        tokens.append(token)
-    for chunk in chunks[1:]:
-        *table, token = moveout(offsets, velocities, samples, *chunk, tokens[-1:])
-        tables.append(table)
+        rows.append(plan.across(spread, at > 0))
         tokens.append(token)
     out = None
     for at, (start, stop) in enumerate(chunks):

time: 53.6 us -> 51 us (0.951)
  waiting for transfers between devices: 12 us -> 10 us
    ppermute x6, waiting for transfers between devices: 3.19 us -> 1.19 us  [across(): lax.ppermute(block, 'xline', pairs)]
  transfers between devices with their start and end apart: 16 -> 16, of which waited for: 4 -> 5; matrix products, arithmetic and copies ran while one was open for 4% -> 4% of each run, Pallas kernels for 20% -> 21%
where the time goes in v5:
time: 51 us; the launch traced here: 50.8 us
  starting transfers between devices  20.4 us (40%)
  Pallas kernels  17.3 us (34%)
  waiting for transfers between devices  10 us (20%)
  other arithmetic  2.26 us (4%)
  between operations  0.77 us (2%)
    ppermute x10, starting transfers between devices, swap(): lax.ppermute(value, 'inline', [(i, i ^ bit) for i in range(self.inline)])  11.5 us
    pallas_call x2, Pallas kernels, panels(): pl.pallas_call(functools.partial(panel_kernel, classes, vels, first, last...  10.5 us
    ppermute x6, starting transfers between devices, across(): lax.ppermute(block, 'xline', pairs)  8.91 us
    ppermute x10, waiting for transfers between devices, swap(): lax.ppermute(value, 'inline', [(i, i ^ bit) for i in range(self.inline)])  8.83 us
    pallas_call x2, Pallas kernels, moveout(): pl.pallas_call(functools.partial(table_kernel, classes, start, samples),...  3.05 us
    pallas_call x2, Pallas kernels, bin_rows(): pl.pallas_call(functools.partial(bin_kernel, len(members), len(data), kep...  1.66 us
    pallas_call x2, Pallas kernels, spread(): pl.pallas_call(functools.partial(spread_kernel, len(parts), len(kinds)),...  1.28 us
    ppermute x6, waiting for transfers between devices, across(): lax.ppermute(block, 'xline', pairs)  1.19 us
  transfers between devices with their start and end apart: 16, of which 5 were waited for; matrix products, arithmetic and copies ran while one was open for 4% of the time, Pallas kernels for 21%

profile of v5, /device:TPU:0, one launch (start us, length us, event | category | flops | bytes accessed | tf_op | source)
XLA Modules:
  0.0 50.8 jit_solution(11313383459157643512)
XLA Ops:
  0.6 0.0 copy-start
  0.6 0.5 %collective-permute-start.1 = (bf16[256,2048]{1,0:T(8,128)(2,1)}, bf16[256,2048]{1,0:T(8,128)(2,1)S(1)}, u32[]{:S(2)}, u32[]{:S(2)}) collective-permute-start(bf16[256,2048]{1,0:T(8,128)(2,1)} %refs_2_.3), channel_id=1, source_target_pairs={{0,4},{4,0},{8,12},{12,8},{16,20},{20,16},{24,28},{28,24},{1,5},{5... | collective-permute-start | bytes 3145736 | tf_op jit(solution)/shard_map/ppermute | solution.py:124
  1.2 0.7 %broadcast_multiply_fusion = s32[256,1]{0,1:T(1,128)S(1)} fusion(s32[256,1]{0,1:T(1,128)} %param.7), kind=kLoop, calls=%fused_computation.72 | loop fusion | flops 256 | bytes 2048 | tf_op jit(solution)/shard_map/mul | solution.py:567
  1.8 0.7 %multiply_add_fusion = s32[256]{0:T(256)S(1)} fusion(s32[256]{0:T(256)} %param.9, s32[256]{0:T(256)S(1)} %bitcast.5, s32[256]{0:T(256)} %param.8), kind=kLoop, calls=%fused_computation.70 | loop fusion | flops 768 | bytes 4096 | tf_op jit(solution)/shard_map/add | solution.py:567
  2.5 0.1 collective-permute-start
  2.7 0.1 add_multiply_fusion.refs_4_.places_ref
  2.7 0.9 %collective-permute-done = s32[256]{0:T(256)S(1)} collective-permute-done((s32[256]{0:T(256)S(1)}, s32[256]{0:T(256)S(1)}, u32[]{:S(2)}, u32[]{:S(2)}) %collective-permute-start) | collective-permute-done | bytes 1056 | tf_op jit(solution)/shard_map/ppermute | solution.py:124
  3.8 0.7 %fusion.1 = (bf16[544,512]{1,0:T(8,128)(2,1)S(1)}, bf16[544,512]{1,0:T(8,128)(2,1)S(1)}) fusion(s32[512]{0:T(512)S(1)} %fusion.17, s32[512]{0:T(512)S(1)} %get-tuple-element.96, s32[512]{0:T(512)S(1)} %get-tuple-element.91, s32[512]{0:T(512)S(1)} %get-tuple-element.86), kind=kLoop, calls=%fused_computation.5 | loop fusion | flops 2228224 | bytes 1122304 | tf_op jit(solution)/shard_map/convert_element_type | solution.py:145
  4.5 0.0 collective-permute-done.1.refs_3_
  4.5 0.9 %shard_map.77 = (f32[272,512]{1,0:T(8,128)S(1)}, bf16[272,512]{1,0:T(8,128)(2,1)S(1)}, f32[272,640]{1,0:T(8,128)S(1)}, bf16[272,640]{1,0:T(8,128)(2,1)S(1)}, f32[8,128]{1,0:T(8,128)S(1)}) custom-call(bf16[544,512]{1,0:T(8,128)(2,1)S(1)} %get-tuple-element.97.refs_0_, bf16[544,512]{1,0:T(8,128)(2,1)S(1)} %get-tuple-element.98.refs_1_, ...), custom_call_target="tpu_custom_call" | custom-call | flops 570425344 | tf_op jit(solution)/shard_map/pallas_call | solution.py:86
  5.4 2.8 %collective-permute-start.3 = (bf16[272,640]{1,0:T(8,128)(2,1)S(1)}, bf16[272,640]{1,0:T(8,128)(2,1)S(1)}, u32[]{:S(2)}, u32[]{:S(2)}) collective-permute-start(bf16[272,640]{1,0:T(8,128)(2,1)S(1)} %get-tuple-element.47), channel_id=1, source_target_pairs={{0,16},{4,20},{8,24},{12,28},{16,0},{20,4},{24,8},{28,12},{1,17},{... | collective-permute-start | bytes 1044488 | tf_op jit(solution)/shard_map/ppermute | solution.py:124
  8.2 1.5 %collective-permute-start.2 = (bf16[272,512]{1,0:T(8,128)(2,1)S(1)}, bf16[272,512]{1,0:T(8,128)(2,1)S(1)}, u32[]{:S(2)}, u32[]{:S(2)}) collective-permute-start(bf16[272,512]{1,0:T(8,128)(2,1)S(1)} %get-tuple-element.45), channel_id=1, source_target_pairs={{0,8},{4,12},{8,0},{12,4},{16,24},{20,28},{24,16},{28,20},{1,9},{5... | collective-permute-start | bytes 835592 | tf_op jit(solution)/shard_map/ppermute | solution.py:124
  9.7 0.7 %shard_map.78 = (f32[272,512]{1,0:T(8,128)S(1)}, bf16[272,512]{1,0:T(8,128)(2,1)S(1)}, f32[272,512]{1,0:T(8,128)S(1)}, bf16[272,512]{1,0:T(8,128)(2,1)S(1)}, f32[8,128]{1,0:T(8,128)S(1)}) custom-call(bf16[544,512]{1,0:T(8,128)(2,1)S(1)} %get-tuple-element.97.refs_0_, bf16[544,512]{1,0:T(8,128)(2,1)S(1)} %get-tuple-element.98.refs_1_, ...), custom_call_target="tpu_custom_call" | custom-call | flops 570425344 | tf_op jit(solution)/shard_map/pallas_call | solution.py:86
  10.5 0.6 %collective-permute-start.6 = (bf16[272,512]{1,0:T(8,128)(2,1)S(1)}, bf16[272,512]{1,0:T(8,128)(2,1)S(1)}, u32[]{:S(2)}, u32[]{:S(2)}) collective-permute-start(bf16[272,512]{1,0:T(8,128)(2,1)S(1)} %get-tuple-element.58), channel_id=1, source_target_pairs={{0,8},{4,12},{8,0},{12,4},{16,24},{20,28},{24,16},{28,20},{1,9},{5... | collective-permute-start | bytes 835592 | tf_op jit(solution)/shard_map/ppermute | solution.py:124
  11.1 0.1 collective-permute-start.7
  11.1 0.0 copy-done.1
  11.1 1.5 %shard_map.79 = (s32[16,8,1024]{2,1,0:T(8,128)S(1)}, f32[16,8,1024]{2,1,0:T(8,128)S(1)}, f32[16,8,1024]{2,1,0:T(8,128)S(1)}, s32[8,128]{1,0:T(8,128)S(1)}, f32[8,128]{1,0:T(8,128)S(1)}) custom-call(f32[4]{0:T(128)S(1)} %copy-done.1, f32[16]{0:T(128)S(1)} %copy-done.2, f32[8,128]{1,0:T(8,128)S(1)} %get-tuple-element.49.refs_0_), custom_call_target="tpu_custom_call" | custom-call | tf_op jit(solution)/shard_map/pallas_call | solution.py:545
  12.7 5.1 %collective-permute-done.2.refs_1_ = bf16[272,512]{1,0:T(8,128)(2,1)S(1)} collective-permute-done((bf16[272,512]{1,0:T(8,128)(2,1)S(1)}, bf16[272,512]{1,0:T(8,128)(2,1)S(1)}, u32[]{:S(2)}, u32[]{:S(2)}) %collective-permute-start.2) | collective-permute-done | bytes 278560 | tf_op jit(solution)/shard_map/ppermute | solution.py:124
  17.7 0.0 collective-permute-done.3.refs_3_
  17.7 0.1 shard_map.80
  17.9 1.5 %collective-permute-start.5 = (bf16[136,640]{1,0:T(8,128)(2,1)S(1)}, bf16[136,640]{1,0:T(8,128)(2,1)S(1)}, u32[]{:S(2)}, u32[]{:S(2)}) collective-permute-start(bf16[136,640]{1,0:T(8,128)(2,1)S(1)} %get-tuple-element.54), channel_id=1, source_target_pairs={{0,8},{4,12},{8,0},{12,4},{16,24},{20,28},{24,16},{28,20},{1,9},{5... | collective-permute-start | bytes 522248 | tf_op jit(solution)/shard_map/ppermute | solution.py:124
  19.4 1.4 %collective-permute-start.4 = (bf16[136,512]{1,0:T(8,128)(2,1)S(1)}, bf16[136,512]{1,0:T(8,128)(2,1)S(1)}, u32[]{:S(2)}, u32[]{:S(2)}) collective-permute-start(bf16[136,512]{1,0:T(8,128)(2,1)S(1)} %get-tuple-element.52), channel_id=1, source_target_pairs={{0,16},{4,20},{8,24},{12,28},{16,0},{20,4},{24,8},{28,12},{1,17},{... | collective-permute-start | bytes 417800 | tf_op jit(solution)/shard_map/ppermute | solution.py:124
  20.9 2.8 %collective-permute-done.6.refs_1_ = bf16[272,512]{1,0:T(8,128)(2,1)S(1)} collective-permute-done((bf16[272,512]{1,0:T(8,128)(2,1)S(1)}, bf16[272,512]{1,0:T(8,128)(2,1)S(1)}, u32[]{:S(2)}, u32[]{:S(2)}) %collective-permute-start.6) | collective-permute-done | bytes 278560 | tf_op jit(solution)/shard_map/ppermute | solution.py:124
  23.7 0.0 collective-permute-done.7.refs_3_
  23.7 0.7 %shard_map.83 = (f32[136,512]{1,0:T(8,128)S(1)}, bf16[136,512]{1,0:T(8,128)(2,1)S(1)}, f32[136,512]{1,0:T(8,128)S(1)}, bf16[136,512]{1,0:T(8,128)(2,1)S(1)}, f32[8,128]{1,0:T(8,128)}) custom-call(f32[272,512]{1,0:T(8,128)S(1)} %get-tuple-element.57.refs_0_, bf16[272,512]{1,0:T(8,128)(2,1)S(1)} %collective-permute-done.6.refs_1_, ...), custom_call_target="tpu_custom_call" | custom-call | bytes 3342336 | tf_op jit(solution)/shard_map/pallas_call | solution.py:176
  24.4 1.4 %collective-permute-start.8 = (bf16[136,512]{1,0:T(8,128)(2,1)S(1)}, bf16[136,512]{1,0:T(8,128)(2,1)S(1)}, u32[]{:S(2)}, u32[]{:S(2)}) collective-permute-start(bf16[136,512]{1,0:T(8,128)(2,1)S(1)} %get-tuple-element.63), channel_id=1, source_target_pairs={{0,16},{4,20},{8,24},{12,28},{16,0},{20,4},{24,8},{28,12},{1,17},{... | collective-permute-start | bytes 417800 | tf_op jit(solution)/shard_map/ppermute | solution.py:124
  25.8 1.5 %collective-permute-start.9 = (bf16[136,512]{1,0:T(8,128)(2,1)S(1)}, bf16[136,512]{1,0:T(8,128)(2,1)S(1)}, u32[]{:S(2)}, u32[]{:S(2)}) collective-permute-start(bf16[136,512]{1,0:T(8,128)(2,1)S(1)} %get-tuple-element.65), channel_id=1, source_target_pairs={{0,8},{4,12},{8,0},{12,4},{16,24},{20,28},{24,16},{28,20},{1,9},{5... | collective-permute-start | bytes 417800 | tf_op jit(solution)/shard_map/ppermute | solution.py:124
  27.3 0.0 collective-permute-done.4.refs_1_
  27.3 0.0 collective-permute-done.5.refs_3_
  27.3 0.6 %shard_map.81 = (f32[40,1152]{1,0:T(8,128)S(1)}, bf16[40,1152]{1,0:T(8,128)(2,1)S(1)}, bf16[40,1152]{1,0:T(8,128)(2,1)S(1)}, bf16[40,1152]{1,0:T(8,128)(2,1)S(1)}, f32[8,128]{1,0:T(8,128)S(1)}) custom-call(s32[4]{0:T(128)S(1)} %add_multiply_fusion.refs_4_.places_ref, f32[136,512]{1,0:T(8,128)S(1)} %get-tuple-element.51.refs_0_, ...), custom_call_target="tpu_custom_call" | custom-call | bytes 1880064 | tf_op jit(solution)/shard_map/pallas_call | solution.py:191
  28.0 3.7 %collective-permute-start.13 = (bf16[40,1152]{1,0:T(8,128)(2,1)S(1)}, bf16[40,1152]{1,0:T(8,128)(2,1)S(1)}, u32[]{:S(2)}, u32[]{:S(2)}) collective-permute-start(bf16[40,1152]{1,0:T(8,128)(2,1)S(1)} %get-tuple-element.72), channel_id=1, source_target_pairs={{0,3},{1,2},{2,1},{3,0},{4,7},{5,6},{6,5},{7,4},{8,11},{9,10},{10,... | collective-permute-start | bytes 276488 | tf_op jit(solution)/shard_map/ppermute | solution.py:206
  31.6 0.0 collective-permute-start.14
  31.7 0.8 %collective-permute-start.15 = (bf16[40,1152]{1,0:T(8,128)(2,1)S(1)}, bf16[40,1152]{1,0:T(8,128)(2,1)S(1)}, u32[]{:S(2)}, u32[]{:S(2)}) collective-permute-start(bf16[40,1152]{1,0:T(8,128)(2,1)S(1)} %get-tuple-element.74), channel_id=1, source_target_pairs={{0,1},{1,0},{2,3},{3,2},{4,5},{5,4},{6,7},{7,6},{8,9},{9,8},{10,11... | collective-permute-start | bytes 276488 | tf_op jit(solution)/shard_map/ppermute | solution.py:206
  32.4 1.5 %shard_map.82 = (s32[16,8,1024]{2,1,0:T(8,128)S(1)}, f32[16,8,1024]{2,1,0:T(8,128)S(1)}, f32[16,8,1024]{2,1,0:T(8,128)S(1)}, s32[8,128]{1,0:T(8,128)S(1)}, f32[8,128]{1,0:T(8,128)S(1)}) custom-call(f32[4]{0:T(128)S(1)} %copy-done.1, f32[16]{0:T(128)S(1)} %copy-done.2, f32[8,128]{1,0:T(8,128)S(1)} %get-tuple-element.55.refs_0_), custom_call_target="tpu_custom_call" | custom-call | tf_op jit(solution)/shard_map/pallas_call | solution.py:545
  33.9 0.0 collective-permute-done.8.refs_1_
  34.0 0.0 collective-permute-done.9.refs_3_
  34.0 0.6 %shard_map.84 = (f32[40,1024]{1,0:T(8,128)S(1)}, bf16[40,1024]{1,0:T(8,128)(2,1)S(1)}, bf16[40,1024]{1,0:T(8,128)(2,1)S(1)}, bf16[40,1024]{1,0:T(8,128)(2,1)S(1)}, f32[8,128]{1,0:T(8,128)S(1)}) custom-call(s32[4]{0:T(128)S(1)} %add_multiply_fusion.refs_4_.places_ref, f32[136,512]{1,0:T(8,128)S(1)} %get-tuple-element.62.refs_0_, ...), custom_call_target="tpu_custom_call" | custom-call | bytes 1671168 | tf_op jit(solution)/shard_map/pallas_call | solution.py:191
  34.6 1.3 %collective-permute-start.10 = (bf16[40,1024]{1,0:T(8,128)(2,1)S(1)}, bf16[40,1024]{1,0:T(8,128)(2,1)S(1)}, u32[]{:S(2)}, u32[]{:S(2)}) collective-permute-start(bf16[40,1024]{1,0:T(8,128)(2,1)S(1)} %get-tuple-element.68), channel_id=1, source_target_pairs={{0,1},{1,0},{2,3},{3,2},{4,5},{5,4},{6,7},{7,6},{8,9},{9,8},{10,11... | collective-permute-start | bytes 245768 | tf_op jit(solution)/shard_map/ppermute | solution.py:206
  35.9 2.9 %collective-permute-start.11 = (bf16[40,1024]{1,0:T(8,128)(2,1)S(1)}, bf16[40,1024]{1,0:T(8,128)(2,1)S(1)}, u32[]{:S(2)}, u32[]{:S(2)}) collective-permute-start(bf16[40,1024]{1,0:T(8,128)(2,1)S(1)} %get-tuple-element.69), channel_id=1, source_target_pairs={{0,2},{1,3},{2,0},{3,1},{4,6},{5,7},{6,4},{7,5},{8,10},{9,11},{10,... | collective-permute-start | bytes 245768 | tf_op jit(solution)/shard_map/ppermute | solution.py:206
  38.9 0.0 collective-permute-done.13.refs_2_.refs_6_
  38.9 0.2 collective-permute-start.12
  39.1 0.9 %collective-permute-done.14.refs_3_.refs_7_ = bf16[40,1152]{1,0:T(8,128)(2,1)S(1)} collective-permute-done((bf16[40,1152]{1,0:T(8,128)(2,1)S(1)}, bf16[40,1152]{1,0:T(8,128)(2,1)S(1)}, u32[]{:S(2)}, u32[]{:S(2)}) %collective-permute-start.14) | collective-permute-done | bytes 92192 | tf_op jit(solution)/shard_map/ppermute | solution.py:206
  40.0 0.0 collective-permute-done.15.refs_4_.refs_8_
  40.0 4.9 %shard_map.85 = (bf16[8,16,1024]{2,1,0:T(8,128)(2,1)S(1)}, f32[8,16,896]{2,1,0:T(8,128)S(1)}, bf16[2,256,128]{2,1,0:T(8,128)(2,1)S(1)}) custom-call(s32[8,128]{1,0:T(8,128)S(1)} %get-tuple-element.78.refs_0_, f32[40,1152]{1,0:T(8,128)S(1)} %get-tuple-element.71.refs_1_.refs_5_, bf16[40,1152]{1,0:T(8,128)(2,1)S(1)} %collective-permute-done.13.refs_2_.refs_6_, ...), custom_call_target="tpu_custom_call" | custom-call | flops 7340032000 | bytes 4718592 | tf_op jit(solution)/shard_map/pallas_call | solution.py:468
  44.9 0.0 collective-permute-done.10.refs_2_
  44.9 0.0 collective-permute-done.11.refs_3_
  44.9 0.3 collective-permute-done.12.refs_4_
  45.2 5.6 %shard_map.86 = (bf16[8,16,2048]{2,1,0:T(8,128)(2,1)}, f32[8,16,2048]{2,1,0:T(8,128)}) custom-call(s32[8,128]{1,0:T(8,128)S(1)} %get-tuple-element.56.refs_0_, f32[40,1024]{1,0:T(8,128)S(1)} %get-tuple-element.67.refs_1_, bf16[40,1024]{1,0:T(8,128)(2,1)S(1)} %collective-permute-done.10.refs_2_, bf16[40,1024]{1,0:T(8,128)(2,1)S(1)} %collective-permute-done.11.refs_3_, ...), custom_call_target="tpu_custom_call" | custom-call | flops 7340032000 | bytes 4718592 | tf_op jit(solution)/shard_map/pallas_call | solution.py:468
  (7 shorter events, 0.1 us)
Async XLA Ops:
  0.6 3.9 %copy-start = (bf16[256,2048]{1,0:T(8,128)(2,1)S(1)}, bf16[256,2048]{1,0:T(8,128)(2,1)}, u32[]{:S(2)}) copy-start(bf16[256,2048]{1,0:T(8,128)(2,1)} %refs_2_.3) | copy-start | bytes 3145732
  0.6 3.9 %collective-permute-start.1 = (bf16[256,2048]{1,0:T(8,128)(2,1)}, bf16[256,2048]{1,0:T(8,128)(2,1)S(1)}, u32[]{:S(2)}, u32[]{:S(2)}) collective-permute-start(bf16[256,2048]{1,0:T(8,128)(2,1)} %refs_2_.3), channel_id=1, source_target_pairs={{0,4},{4,0},{8,12},{12,8},{16,20},{20,16},{24,28},{28,24},{1,5},{5... | collective-permute-start | bytes 3145736 | tf_op jit(solution)/shard_map/ppermute | solution.py:124
  2.5 1.1 %collective-permute-start = (s32[256]{0:T(256)S(1)}, s32[256]{0:T(256)S(1)}, u32[]{:S(2)}, u32[]{:S(2)}) collective-permute-start(s32[256]{0:T(256)S(1)} %multiply_add_fusion), channel_id=1, source_target_pairs={{0,4},{4,0},{8,12},{12,8},{16,20},{20,16},{24,28},{28,24},{1,5},{5... | collective-permute-start | bytes 3080 | tf_op jit(solution)/shard_map/ppermute | solution.py:124
  5.4 12.3 %collective-permute-start.3 = (bf16[272,640]{1,0:T(8,128)(2,1)S(1)}, bf16[272,640]{1,0:T(8,128)(2,1)S(1)}, u32[]{:S(2)}, u32[]{:S(2)}) collective-permute-start(bf16[272,640]{1,0:T(8,128)(2,1)S(1)} %get-tuple-element.47), channel_id=1, source_target_pairs={{0,16},{4,20},{8,24},{12,28},{16,0},{20,4},{24,8},{28,12},{1,17},{... | collective-permute-start | bytes 1044488 | tf_op jit(solution)/shard_map/ppermute | solution.py:124
  8.2 9.5 %collective-permute-start.2 = (bf16[272,512]{1,0:T(8,128)(2,1)S(1)}, bf16[272,512]{1,0:T(8,128)(2,1)S(1)}, u32[]{:S(2)}, u32[]{:S(2)}) collective-permute-start(bf16[272,512]{1,0:T(8,128)(2,1)S(1)} %get-tuple-element.45), channel_id=1, source_target_pairs={{0,8},{4,12},{8,0},{12,4},{16,24},{20,28},{24,16},{28,20},{1,9},{5... | collective-permute-start | bytes 835592 | tf_op jit(solution)/shard_map/ppermute | solution.py:124
  9.7 1.4 %copy-start.1 = (f32[4]{0:T(128)S(1)}, f32[4]{0:T(128)}, u32[]{:S(2)}) copy-start(f32[4]{0:T(128)} %offsets_ref.3) | copy-start | bytes 52
  9.7 1.4 %copy-start.2 = (f32[16]{0:T(128)S(1)}, f32[16]{0:T(128)}, u32[]{:S(2)}) copy-start(f32[16]{0:T(128)} %velocities_ref.3) | copy-start | bytes 196
  10.5 13.2 %collective-permute-start.6 = (bf16[272,512]{1,0:T(8,128)(2,1)S(1)}, bf16[272,512]{1,0:T(8,128)(2,1)S(1)}, u32[]{:S(2)}, u32[]{:S(2)}) collective-permute-start(bf16[272,512]{1,0:T(8,128)(2,1)S(1)} %get-tuple-element.58), channel_id=1, source_target_pairs={{0,8},{4,12},{8,0},{12,4},{16,24},{20,28},{24,16},{28,20},{1,9},{5... | collective-permute-start | bytes 835592 | tf_op jit(solution)/shard_map/ppermute | solution.py:124
  11.1 12.6 %collective-permute-start.7 = (bf16[272,512]{1,0:T(8,128)(2,1)S(1)}, bf16[272,512]{1,0:T(8,128)(2,1)S(1)}, u32[]{:S(2)}, u32[]{:S(2)}) collective-permute-start(bf16[272,512]{1,0:T(8,128)(2,1)S(1)} %get-tuple-element.60), channel_id=1, source_target_pairs={{0,16},{4,20},{8,24},{12,28},{16,0},{20,4},{24,8},{28,12},{1,17},{... | collective-permute-start | bytes 835592 | tf_op jit(solution)/shard_map/ppermute | solution.py:124
  17.9 9.4 %collective-permute-start.5 = (bf16[136,640]{1,0:T(8,128)(2,1)S(1)}, bf16[136,640]{1,0:T(8,128)(2,1)S(1)}, u32[]{:S(2)}, u32[]{:S(2)}) collective-permute-start(bf16[136,640]{1,0:T(8,128)(2,1)S(1)} %get-tuple-element.54), channel_id=1, source_target_pairs={{0,8},{4,12},{8,0},{12,4},{16,24},{20,28},{24,16},{28,20},{1,9},{5... | collective-permute-start | bytes 522248 | tf_op jit(solution)/shard_map/ppermute | solution.py:124
  19.4 7.9 %collective-permute-start.4 = (bf16[136,512]{1,0:T(8,128)(2,1)S(1)}, bf16[136,512]{1,0:T(8,128)(2,1)S(1)}, u32[]{:S(2)}, u32[]{:S(2)}) collective-permute-start(bf16[136,512]{1,0:T(8,128)(2,1)S(1)} %get-tuple-element.52), channel_id=1, source_target_pairs={{0,16},{4,20},{8,24},{12,28},{16,0},{20,4},{24,8},{28,12},{1,17},{... | collective-permute-start | bytes 417800 | tf_op jit(solution)/shard_map/ppermute | solution.py:124
  24.4 9.6 %collective-permute-start.8 = (bf16[136,512]{1,0:T(8,128)(2,1)S(1)}, bf16[136,512]{1,0:T(8,128)(2,1)S(1)}, u32[]{:S(2)}, u32[]{:S(2)}) collective-permute-start(bf16[136,512]{1,0:T(8,128)(2,1)S(1)} %get-tuple-element.63), channel_id=1, source_target_pairs={{0,16},{4,20},{8,24},{12,28},{16,0},{20,4},{24,8},{28,12},{1,17},{... | collective-permute-start | bytes 417800 | tf_op jit(solution)/shard_map/ppermute | solution.py:124
  25.8 8.1 %collective-permute-start.9 = (bf16[136,512]{1,0:T(8,128)(2,1)S(1)}, bf16[136,512]{1,0:T(8,128)(2,1)S(1)}, u32[]{:S(2)}, u32[]{:S(2)}) collective-permute-start(bf16[136,512]{1,0:T(8,128)(2,1)S(1)} %get-tuple-element.65), channel_id=1, source_target_pairs={{0,8},{4,12},{8,0},{12,4},{16,24},{20,28},{24,16},{28,20},{1,9},{5... | collective-permute-start | bytes 417800 | tf_op jit(solution)/shard_map/ppermute | solution.py:124
  28.0 10.9 %collective-permute-start.13 = (bf16[40,1152]{1,0:T(8,128)(2,1)S(1)}, bf16[40,1152]{1,0:T(8,128)(2,1)S(1)}, u32[]{:S(2)}, u32[]{:S(2)}) collective-permute-start(bf16[40,1152]{1,0:T(8,128)(2,1)S(1)} %get-tuple-element.72), channel_id=1, source_target_pairs={{0,3},{1,2},{2,1},{3,0},{4,7},{5,6},{6,5},{7,4},{8,11},{9,10},{10,... | collective-permute-start | bytes 276488 | tf_op jit(solution)/shard_map/ppermute | solution.py:206
  31.6 8.3 %collective-permute-start.14 = (bf16[40,1152]{1,0:T(8,128)(2,1)S(1)}, bf16[40,1152]{1,0:T(8,128)(2,1)S(1)}, u32[]{:S(2)}, u32[]{:S(2)}) collective-permute-start(bf16[40,1152]{1,0:T(8,128)(2,1)S(1)} %get-tuple-element.73), channel_id=1, source_target_pairs={{0,2},{1,3},{2,0},{3,1},{4,6},{5,7},{6,4},{7,5},{8,10},{9,11},{10,... | collective-permute-start | bytes 276488 | tf_op jit(solution)/shard_map/ppermute | solution.py:206
  31.7 8.3 %collective-permute-start.15 = (bf16[40,1152]{1,0:T(8,128)(2,1)S(1)}, bf16[40,1152]{1,0:T(8,128)(2,1)S(1)}, u32[]{:S(2)}, u32[]{:S(2)}) collective-permute-start(bf16[40,1152]{1,0:T(8,128)(2,1)S(1)} %get-tuple-element.74), channel_id=1, source_target_pairs={{0,1},{1,0},{2,3},{3,2},{4,5},{5,4},{6,7},{7,6},{8,9},{9,8},{10,11... | collective-permute-start | bytes 276488 | tf_op jit(solution)/shard_map/ppermute | solution.py:206
  34.6 10.3 %collective-permute-start.10 = (bf16[40,1024]{1,0:T(8,128)(2,1)S(1)}, bf16[40,1024]{1,0:T(8,128)(2,1)S(1)}, u32[]{:S(2)}, u32[]{:S(2)}) collective-permute-start(bf16[40,1024]{1,0:T(8,128)(2,1)S(1)} %get-tuple-element.68), channel_id=1, source_target_pairs={{0,1},{1,0},{2,3},{3,2},{4,5},{5,4},{6,7},{7,6},{8,9},{9,8},{10,11... | collective-permute-start | bytes 245768 | tf_op jit(solution)/shard_map/ppermute | solution.py:206
  35.9 9.0 %collective-permute-start.11 = (bf16[40,1024]{1,0:T(8,128)(2,1)S(1)}, bf16[40,1024]{1,0:T(8,128)(2,1)S(1)}, u32[]{:S(2)}, u32[]{:S(2)}) collective-permute-start(bf16[40,1024]{1,0:T(8,128)(2,1)S(1)} %get-tuple-element.69), channel_id=1, source_target_pairs={{0,2},{1,3},{2,0},{3,1},{4,6},{5,7},{6,4},{7,5},{8,10},{9,11},{10,... | collective-permute-start | bytes 245768 | tf_op jit(solution)/shard_map/ppermute | solution.py:206
  38.9 6.3 %collective-permute-start.12 = (bf16[40,1024]{1,0:T(8,128)(2,1)S(1)}, bf16[40,1024]{1,0:T(8,128)(2,1)S(1)}, u32[]{:S(2)}, u32[]{:S(2)}) collective-permute-start(bf16[40,1024]{1,0:T(8,128)(2,1)S(1)} %get-tuple-element.70), channel_id=1, source_target_pairs={{0,3},{1,2},{2,1},{3,0},{4,7},{5,6},{6,5},{7,4},{8,11},{9,10},{10,... | collective-permute-start | bytes 245768 | tf_op jit(solution)/shard_map/ppermute | solution.py:206

commit v6 on v5

--- a/solution.py
+++ b/solution.py
@@ -99,12 +99,42 @@
     return list(zip(outs[0:-1:2], outs[1:-1:2])), outs[-1]
 
 
+def member_kernel(places_ref, *refs):
+    for at, member_ref in enumerate(refs):
+        row = lax.broadcasted_iota(jnp.int32, member_ref.shape, 0)
+        own = jnp.broadcast_to(places_ref[2 * at : 2 * at + 1, :], row.shape)
+        rim = jnp.broadcast_to(places_ref[2 * at + 1 : 2 * at + 2, :], row.shape)
+        member_ref[...] = jnp.where((row == own) | (row == rim), 1.0, 0.0).astype(BF16)
+
+
+def members_of(places, rows):
+    places = jnp.stack(places)
+    count = places.shape[0] // 2
+    return pl.pallas_call(
+        member_kernel,
+        in_specs=[VMEM],
+        out_specs=[VMEM] * count,
+        out_shape=[jax.ShapeDtypeStruct((rows, places.shape[1]), BF16)] * count,
+        compiler_params=pltpu.CompilerParams(vmem_limit_bytes=VMEM_BYTES),
+        cost_estimate=pl.CostEstimate(
+            flops=540 * rows * places.size // 2, bytes_accessed=0, transcendentals=0
+        ),
+    )(places)
+
+
+def steps_of(count):
+    return range(count - 1, 0, -1)
+
+
+def target_of(place, step, count):
+    return place ^ step if count & (count - 1) == 0 else (place + step) % count
+
+
 class Plan:
     def __init__(self, traces, key, classes):
         self.inline = lax.axis_size("inline")
         self.xline = lax.axis_size("xline")
         self.me = lax.axis_index("inline")
-        self.me_x = lax.axis_index("xline")
         self.classes = classes
         self.dev_rows = CMP_DEV * classes
         self.line_rows = self.xline * self.dev_rows
@@ -115,15 +145,16 @@
         unit = 8 if self.codes % 4 == 0 else 16
         self.block_rows = -(-(self.line_rows + 2 * classes) // unit) * unit
         self.data = [traces, self.swap(traces, self.core)]
-        self.keys = jnp.concatenate([key, self.swap(key, self.core)])
-        self.members = [self.member(order) for order in self.orders]
-        places = [self.me_x] + [target for target, _ in self.targets()]
-        self.places = jnp.stack(places) * self.dev_rows
+        self.keys = jnp.concatenate([key, self.swap(key, self.core)]).reshape(-1)
+        self.members = members_of(
+            [place for order in self.orders for place in self.places_of(order)],
+            self.codes * self.block_rows,
+        )
 
     def swap(self, value, bit):
         return lax.ppermute(value, "inline", [(i, i ^ bit) for i in range(self.inline)])
 
-    def member(self, order):
+    def places_of(self, order):
         classes, line_rows = self.classes, self.line_rows
         line, local = self.keys // line_rows, self.keys % line_rows
 
@@ -141,8 +172,7 @@
             row_of(line + 1, local - (line_rows - classes)),
             jnp.where(local < classes, row_of(line - 1, local + classes + line_rows), -1),
         )
-        row = jnp.arange(self.codes * self.block_rows)[:, None]
-        return ((row == own[None, :]) | (row == rim[None, :])).astype(BF16)
+        return own, rim
 
     def bin(self, start, cols, counted, after):
         rows = self.codes * self.block_rows
@@ -154,17 +184,9 @@
             (kept, self.swap(sent, order[place])) for order, (kept, sent) in zip(self.orders, parts)
         ]
 
-    def targets(self):
-        steps = []
-        for step in range(self.xline - 1, 0, -1):
-            if self.xline & (self.xline - 1) == 0:
-                target = self.me_x ^ step
-                pairs = [(i, i ^ step) for i in range(self.xline)]
-            else:
-                target = (self.me_x + step) % self.xline
-                pairs = [(i, (i + step) % self.xline) for i in range(self.xline)]
-            steps.append((target, pairs))
-        return steps
+    def pairs(self):
+        places = range(self.xline)
+        return [[(i, int(target_of(i, step, self.xline))) for i in places] for step in steps_of(self.xline)]
 
     def merge(self, parts, after):
         half = parts[0][0].shape[0] // 2
@@ -189,18 +211,18 @@
         flat = [value for part in parts for value in part]
         kinds = [F32] + [BF16] * (self.xline - 1)
         return pl.pallas_call(
-            functools.partial(spread_kernel, len(parts), len(kinds)),
-            in_specs=[SMEM] + [VMEM] * len(flat) + [ANY] * len(after),
+            functools.partial(spread_kernel, len(parts), self.xline, self.dev_rows),
+            in_specs=[VMEM] * len(flat) + [ANY] * len(after),
             out_specs=[VMEM] * (len(kinds) + 1),
             out_shape=[jax.ShapeDtypeStruct((window, cols), kind) for kind in kinds] + [TOKEN],
             scratch_shapes=[pltpu.VMEM((parts[0][0].shape[0], cols), F32)],
             compiler_params=pltpu.CompilerParams(vmem_limit_bytes=VMEM_BYTES),
             cost_estimate=cost_of(flat),
-        )(self.places, *flat, *after)
+        )(*flat, *after)
 
     def across(self, blocks, near_first):
         own, *sent = blocks
-        moves = [(block, pairs) for block, (_, pairs) in zip(sent, self.targets())]
+        moves = list(zip(sent, self.pairs()))
         if near_first:
             moves = moves[::-1]
         return [own] + [lax.ppermute(block, "xline", pairs) for block, pairs in moves]
@@ -222,7 +244,7 @@
         outs[2 * at + 1][...] = total[half:].astype(BF16)
 
 
-def spread_kernel(count, blocks, places_ref, *refs):
+def spread_kernel(count, blocks, stride, *refs):
     ins, outs, token_ref, total_ref = refs[: 2 * count], refs[-blocks - 2 : -2], refs[-2], refs[-1]
     token_ref[...] = jnp.zeros(token_ref.shape, F32)
     start = 0
@@ -231,8 +253,10 @@
         stop = start + kept.shape[1]
         total_ref[:, start:stop] = kept[...] + sent[...].astype(F32)
         start = stop
-    for at, out in enumerate(outs):
-        place = pl.multiple_of(places_ref[at], 8)
+    me = lax.axis_index("xline")
+    places = [me] + [target_of(me, step, blocks) for step in steps_of(blocks)]
+    for place, out in zip(places, outs):
+        place = pl.multiple_of(place * stride, 8)
         out[...] = total_ref[pl.ds(place, out.shape[0]), :].astype(out.dtype)
 
 
@@ -564,11 +588,11 @@
     samples = traces.shape[1]
     classes, vels = offsets.shape[0], velocities.shape[0]
     count = samples // LANES
-    key = (owners.reshape(-1) * CMP_DEV + midpoint) * classes + offset_class
+    key = (owners * CMP_DEV + midpoint[:, None]) * classes + offset_class[:, None]
     plan = Plan(traces, key, classes)
     cuts = [0, samples // 2, samples]
     chunks = list(zip(cuts[:-1], cuts[1:]))[::-1]
-    parts, tokens = [], [plan.places]
+    parts, tokens = [], []
     for start, stop in chunks:
         part, token = plan.bin(start, stop - start, stop == samples, tokens[-1:])
         parts.append(part)
@@ -584,7 +608,7 @@
             part = plan.exchange(place, part)
             tokens.append(token)
         spreads.append(part)
-    rows, tokens = [], []
+    rows = []
     for at, part in enumerate(spreads):
         if at:
             *table, token = moveout(offsets, velocities, samples, *chunks[at], tokens[-1:])

time: 51 us -> 49.6 us (0.973)
  other arithmetic: 2.26 us -> 0.81 us
  Pallas kernels: 17.3 us -> 15.9 us
  starting transfers between devices: 20.4 us -> 21.3 us
  local copies, waits for them, and re-layouts: 0.01 us -> 0.59 us
    pallas_call x2 -> x3, Pallas kernels: 1.28 us -> 0.51 us  [the longest x1 0.31 us: members_of(): pl.pallas_call(member_kernel, in_specs=[VMEM], out_specs=[VMEM] * count,...]
    mul x2 -> x0, other arithmetic: 0.76 us -> none  [the longest x1 0.68 us: per_device(): key = (owners.reshape(-1) * CMP_DEV + midpoint) * classes + offset_class]
    convert_element_type x1 -> x0, other arithmetic: 0.74 us -> none  [member(): return ((row == own[None, :]) | (row == rim[None, :])).astype(BF16)]
    pallas_call x2, Pallas kernels: 0.82 us -> 0.21 us  [merge(): pl.pallas_call(functools.partial(merge_kernel, len(parts)), in_specs=[VME...]
    ppermute x6, starting transfers between devices: 8.91 us -> 9.51 us  [across(): lax.ppermute(block, 'xline', pairs)]
    unnamed x6, local copies, waits for them, and re-layouts: 0.01 us -> 0.59 us
  transfers between devices with their start and end apart: 16 -> 16, of which waited for: 5 -> 4; matrix products, arithmetic and copies ran while one was open for 4% -> 2% of each run, Pallas kernels for 21% -> 19%
where the time goes in v6:
time: 49.6 us; the launch traced here: 49.4 us
  starting transfers between devices  21.3 us (43%)
  Pallas kernels  15.9 us (32%)
  waiting for transfers between devices  10 us (20%)
  other arithmetic  0.81 us (2%)
  between operations  0.79 us (2%)
  local copies, waits for them, and re-layouts  0.59 us (1%)
    ppermute x10, starting transfers between devices, swap(): lax.ppermute(value, 'inline', [(i, i ^ bit) for i in range(self.inline)])  11.7 us
    pallas_call x2, Pallas kernels, panels(): pl.pallas_call(functools.partial(panel_kernel, classes, vels, first, last...  10.5 us
    ppermute x6, starting transfers between devices, across(): lax.ppermute(block, 'xline', pairs)  9.51 us
    ppermute x10, waiting for transfers between devices, swap(): lax.ppermute(value, 'inline', [(i, i ^ bit) for i in range(self.inline)])  8.8 us
    pallas_call x2, Pallas kernels, moveout(): pl.pallas_call(functools.partial(table_kernel, classes, start, samples),...  3.05 us
    pallas_call x2, Pallas kernels, bin_rows(): pl.pallas_call(functools.partial(bin_kernel, len(members), len(data), kep...  1.63 us
    ppermute x6, waiting for transfers between devices, across(): lax.ppermute(block, 'xline', pairs)  1.22 us
  transfers between devices with their start and end apart: 16, of which 4 were waited for; matrix products, arithmetic and copies ran while one was open for 2% of the time, Pallas kernels for 19%

profile of v6, /device:TPU:0, one launch (start us, length us, event | category | flops | bytes accessed | tf_op | source)
XLA Modules:
  0.0 49.4 jit_solution(2167687808882623659)
XLA Ops:
  0.6 0.0 copy-start
  0.6 0.5 %collective-permute-start.1 = (bf16[256,2048]{1,0:T(8,128)(2,1)}, bf16[256,2048]{1,0:T(8,128)(2,1)S(1)}, u32[]{:S(2)}, u32[]{:S(2)}) collective-permute-start(bf16[256,2048]{1,0:T(8,128)(2,1)} %refs_2_.3), channel_id=1, source_target_pairs={{0,4},{4,0},{8,12},{12,8},{16,20},{20,16},{24,28},{28,24},{1,5},{5... | collective-permute-start | bytes 3145736 | tf_op jit(solution)/shard_map/ppermute | solution.py:155
  1.2 0.7 %multiply_add_fusion = s32[256,1]{0,1:T(1,128)S(1)} fusion(s32[256,1]{0,1:T(1,128)} %bitcast.10, s32[256,1]{0,1:T(1,128)} %bitcast.11, s32[256,1]{0,1:T(1,128)} %param.7), kind=kLoop, calls=%fused_computation.25 | loop fusion | flops 1024 | bytes 4096 | tf_op jit(solution)/shard_map/add | solution.py:591
  1.9 0.1 collective-permute-start
  2.0 1.4 %collective-permute-done = s32[256,1]{0,1:T(1,128)S(1)} collective-permute-done((s32[256,1]{0,1:T(1,128)S(1)}, s32[256,1]{0,1:T(1,128)S(1)}, u32[]{:S(2)}, u32[]{:S(2)}) %collective-permute-start) | collective-permute-done | bytes 1056 | tf_op jit(solution)/shard_map/ppermute | solution.py:155
  3.6 0.3 shard_map.77
  3.9 0.0 collective-permute-done.1.refs_3_
  3.9 0.0 copy-done
  3.9 0.9 %shard_map.78 = (f32[272,512]{1,0:T(8,128)S(1)}, bf16[272,512]{1,0:T(8,128)(2,1)S(1)}, f32[272,640]{1,0:T(8,128)S(1)}, bf16[272,640]{1,0:T(8,128)(2,1)S(1)}, f32[8,128]{1,0:T(8,128)S(1)}) custom-call(bf16[544,512]{1,0:T(8,128)(2,1)S(1)} %get-tuple-element.47.refs_0_, bf16[544,512]{1,0:T(8,128)(2,1)S(1)} %get-tuple-element.48.refs_1_, ...), custom_call_target="tpu_custom_call" | custom-call | flops 570425344 | tf_op jit(solution)/shard_map/pallas_call | solution.py:86
  4.8 2.9 %collective-permute-start.3 = (bf16[272,640]{1,0:T(8,128)(2,1)S(1)}, bf16[272,640]{1,0:T(8,128)(2,1)S(1)}, u32[]{:S(2)}, u32[]{:S(2)}) collective-permute-start(bf16[272,640]{1,0:T(8,128)(2,1)S(1)} %get-tuple-element.52), channel_id=1, source_target_pairs={{0,16},{4,20},{8,24},{12,28},{16,0},{20,4},{24,8},{28,12},{1,17},{... | collective-permute-start | bytes 1044488 | tf_op jit(solution)/shard_map/ppermute | solution.py:155
  7.7 1.5 %collective-permute-start.2 = (bf16[272,512]{1,0:T(8,128)(2,1)S(1)}, bf16[272,512]{1,0:T(8,128)(2,1)S(1)}, u32[]{:S(2)}, u32[]{:S(2)}) collective-permute-start(bf16[272,512]{1,0:T(8,128)(2,1)S(1)} %get-tuple-element.50), channel_id=1, source_target_pairs={{0,8},{4,12},{8,0},{12,4},{16,24},{20,28},{24,16},{28,20},{1,9},{5... | collective-permute-start | bytes 835592 | tf_op jit(solution)/shard_map/ppermute | solution.py:155
  9.2 0.7 %shard_map.79 = (f32[272,512]{1,0:T(8,128)S(1)}, bf16[272,512]{1,0:T(8,128)(2,1)S(1)}, f32[272,512]{1,0:T(8,128)S(1)}, bf16[272,512]{1,0:T(8,128)(2,1)S(1)}, f32[8,128]{1,0:T(8,128)S(1)}) custom-call(bf16[544,512]{1,0:T(8,128)(2,1)S(1)} %get-tuple-element.47.refs_0_, bf16[544,512]{1,0:T(8,128)(2,1)S(1)} %get-tuple-element.48.refs_1_, ...), custom_call_target="tpu_custom_call" | custom-call | flops 570425344 | tf_op jit(solution)/shard_map/pallas_call | solution.py:86
  10.0 0.6 %collective-permute-start.6 = (bf16[272,512]{1,0:T(8,128)(2,1)S(1)}, bf16[272,512]{1,0:T(8,128)(2,1)S(1)}, u32[]{:S(2)}, u32[]{:S(2)}) collective-permute-start(bf16[272,512]{1,0:T(8,128)(2,1)S(1)} %get-tuple-element.61), channel_id=1, source_target_pairs={{0,8},{4,12},{8,0},{12,4},{16,24},{20,28},{24,16},{28,20},{1,9},{5... | collective-permute-start | bytes 835592 | tf_op jit(solution)/shard_map/ppermute | solution.py:155
  10.6 0.1 collective-permute-start.7
  10.7 0.6 %copy-done.1 = f32[4]{0:T(128)S(1)} copy-done((f32[4]{0:T(128)S(1)}, f32[4]{0:T(128)}, u32[]{:S(2)}) %copy-start.1) | copy-done | bytes 40
  11.2 0.0 copy-done.2
  11.2 1.5 %shard_map.80 = (s32[16,8,1024]{2,1,0:T(8,128)S(1)}, f32[16,8,1024]{2,1,0:T(8,128)S(1)}, f32[16,8,1024]{2,1,0:T(8,128)S(1)}, s32[8,128]{1,0:T(8,128)S(1)}, f32[8,128]{1,0:T(8,128)S(1)}) custom-call(f32[4]{0:T(128)S(1)} %copy-done.1, f32[16]{0:T(128)S(1)} %copy-done.2, f32[8,128]{1,0:T(8,128)S(1)} %get-tuple-element.54.refs_0_), custom_call_target="tpu_custom_call" | custom-call | tf_op jit(solution)/shard_map/pallas_call | solution.py:569
  12.8 4.5 %collective-permute-done.2.refs_1_ = bf16[272,512]{1,0:T(8,128)(2,1)S(1)} collective-permute-done((bf16[272,512]{1,0:T(8,128)(2,1)S(1)}, bf16[272,512]{1,0:T(8,128)(2,1)S(1)}, u32[]{:S(2)}, u32[]{:S(2)}) %collective-permute-start.2) | collective-permute-done | bytes 278560 | tf_op jit(solution)/shard_map/ppermute | solution.py:155
  17.3 0.0 collective-permute-done.3.refs_3_
  17.3 0.1 shard_map.81
  17.4 1.6 %collective-permute-start.5 = (bf16[136,640]{1,0:T(8,128)(2,1)S(1)}, bf16[136,640]{1,0:T(8,128)(2,1)S(1)}, u32[]{:S(2)}, u32[]{:S(2)}) collective-permute-start(bf16[136,640]{1,0:T(8,128)(2,1)S(1)} %get-tuple-element.59), channel_id=1, source_target_pairs={{0,8},{4,12},{8,0},{12,4},{16,24},{20,28},{24,16},{28,20},{1,9},{5... | collective-permute-start | bytes 522248 | tf_op jit(solution)/shard_map/ppermute | solution.py:155
  19.0 1.4 %collective-permute-start.4 = (bf16[136,512]{1,0:T(8,128)(2,1)S(1)}, bf16[136,512]{1,0:T(8,128)(2,1)S(1)}, u32[]{:S(2)}, u32[]{:S(2)}) collective-permute-start(bf16[136,512]{1,0:T(8,128)(2,1)S(1)} %get-tuple-element.57), channel_id=1, source_target_pairs={{0,16},{4,20},{8,24},{12,28},{16,0},{20,4},{24,8},{28,12},{1,17},{... | collective-permute-start | bytes 417800 | tf_op jit(solution)/shard_map/ppermute | solution.py:155
  20.4 2.8 %collective-permute-done.6.refs_1_ = bf16[272,512]{1,0:T(8,128)(2,1)S(1)} collective-permute-done((bf16[272,512]{1,0:T(8,128)(2,1)S(1)}, bf16[272,512]{1,0:T(8,128)(2,1)S(1)}, u32[]{:S(2)}, u32[]{:S(2)}) %collective-permute-start.6) | collective-permute-done | bytes 278560 | tf_op jit(solution)/shard_map/ppermute | solution.py:155
  23.2 0.0 collective-permute-done.7.refs_3_
  23.2 0.1 shard_map.82
  23.3 1.5 %collective-permute-start.8 = (bf16[136,512]{1,0:T(8,128)(2,1)S(1)}, bf16[136,512]{1,0:T(8,128)(2,1)S(1)}, u32[]{:S(2)}, u32[]{:S(2)}) collective-permute-start(bf16[136,512]{1,0:T(8,128)(2,1)S(1)} %get-tuple-element.69), channel_id=1, source_target_pairs={{0,16},{4,20},{8,24},{12,28},{16,0},{20,4},{24,8},{28,12},{1,17},{... | collective-permute-start | bytes 417800 | tf_op jit(solution)/shard_map/ppermute | solution.py:155
  24.9 1.5 %collective-permute-start.9 = (bf16[136,512]{1,0:T(8,128)(2,1)S(1)}, bf16[136,512]{1,0:T(8,128)(2,1)S(1)}, u32[]{:S(2)}, u32[]{:S(2)}) collective-permute-start(bf16[136,512]{1,0:T(8,128)(2,1)S(1)} %get-tuple-element.71), channel_id=1, source_target_pairs={{0,8},{4,12},{8,0},{12,4},{16,24},{20,28},{24,16},{28,20},{1,9},{5... | collective-permute-start | bytes 417800 | tf_op jit(solution)/shard_map/ppermute | solution.py:155
  26.3 0.0 collective-permute-done.4.refs_1_
  26.3 0.0 collective-permute-done.5.refs_3_
  26.3 0.1 shard_map.83
  26.5 3.7 %collective-permute-start.13 = (bf16[40,1152]{1,0:T(8,128)(2,1)S(1)}, bf16[40,1152]{1,0:T(8,128)(2,1)S(1)}, u32[]{:S(2)}, u32[]{:S(2)}) collective-permute-start(bf16[40,1152]{1,0:T(8,128)(2,1)S(1)} %get-tuple-element.78), channel_id=1, source_target_pairs={{0,3},{1,2},{2,1},{3,0},{4,7},{5,6},{6,5},{7,4},{8,11},{9,10},{10,... | collective-permute-start | bytes 276488 | tf_op jit(solution)/shard_map/ppermute | solution.py:228
  30.1 0.0 collective-permute-start.14
  30.1 0.8 %collective-permute-start.15 = (bf16[40,1152]{1,0:T(8,128)(2,1)S(1)}, bf16[40,1152]{1,0:T(8,128)(2,1)S(1)}, u32[]{:S(2)}, u32[]{:S(2)}) collective-permute-start(bf16[40,1152]{1,0:T(8,128)(2,1)S(1)} %get-tuple-element.80), channel_id=1, source_target_pairs={{0,1},{1,0},{2,3},{3,2},{4,5},{5,4},{6,7},{7,6},{8,9},{9,8},{10,11... | collective-permute-start | bytes 276488 | tf_op jit(solution)/shard_map/ppermute | solution.py:228
  30.9 1.5 %shard_map.84 = (s32[16,8,1024]{2,1,0:T(8,128)S(1)}, f32[16,8,1024]{2,1,0:T(8,128)S(1)}, f32[16,8,1024]{2,1,0:T(8,128)S(1)}, s32[8,128]{1,0:T(8,128)S(1)}, f32[8,128]{1,0:T(8,128)S(1)}) custom-call(f32[4]{0:T(128)S(1)} %copy-done.1, f32[16]{0:T(128)S(1)} %copy-done.2, f32[8,128]{1,0:T(8,128)S(1)} %get-tuple-element.66.refs_0_), custom_call_target="tpu_custom_call" | custom-call | tf_op jit(solution)/shard_map/pallas_call | solution.py:569
  32.4 0.0 collective-permute-done.8.refs_1_
  32.4 0.0 collective-permute-done.9.refs_3_
  32.5 0.1 shard_map.85
  32.6 1.3 %collective-permute-start.10 = (bf16[40,1024]{1,0:T(8,128)(2,1)S(1)}, bf16[40,1024]{1,0:T(8,128)(2,1)S(1)}, u32[]{:S(2)}, u32[]{:S(2)}) collective-permute-start(bf16[40,1024]{1,0:T(8,128)(2,1)S(1)} %get-tuple-element.74), channel_id=1, source_target_pairs={{0,1},{1,0},{2,3},{3,2},{4,5},{5,4},{6,7},{7,6},{8,9},{9,8},{10,11... | collective-permute-start | bytes 245768 | tf_op jit(solution)/shard_map/ppermute | solution.py:228
  33.9 2.9 %collective-permute-start.11 = (bf16[40,1024]{1,0:T(8,128)(2,1)S(1)}, bf16[40,1024]{1,0:T(8,128)(2,1)S(1)}, u32[]{:S(2)}, u32[]{:S(2)}) collective-permute-start(bf16[40,1024]{1,0:T(8,128)(2,1)S(1)} %get-tuple-element.75), channel_id=1, source_target_pairs={{0,2},{1,3},{2,0},{3,1},{4,6},{5,7},{6,4},{7,5},{8,10},{9,11},{10,... | collective-permute-start | bytes 245768 | tf_op jit(solution)/shard_map/ppermute | solution.py:228
  36.8 0.0 collective-permute-done.13.refs_2_.refs_6_
  36.8 0.8 %collective-permute-start.12 = (bf16[40,1024]{1,0:T(8,128)(2,1)S(1)}, bf16[40,1024]{1,0:T(8,128)(2,1)S(1)}, u32[]{:S(2)}, u32[]{:S(2)}) collective-permute-start(bf16[40,1024]{1,0:T(8,128)(2,1)S(1)} %get-tuple-element.76), channel_id=1, source_target_pairs={{0,3},{1,2},{2,1},{3,0},{4,7},{5,6},{6,5},{7,4},{8,11},{9,10},{10,... | collective-permute-start | bytes 245768 | tf_op jit(solution)/shard_map/ppermute | solution.py:228
  37.6 1.2 %collective-permute-done.14.refs_3_.refs_7_ = bf16[40,1152]{1,0:T(8,128)(2,1)S(1)} collective-permute-done((bf16[40,1152]{1,0:T(8,128)(2,1)S(1)}, bf16[40,1152]{1,0:T(8,128)(2,1)S(1)}, u32[]{:S(2)}, u32[]{:S(2)}) %collective-permute-start.14) | collective-permute-done | bytes 92192 | tf_op jit(solution)/shard_map/ppermute | solution.py:228
  38.8 0.0 collective-permute-done.15.refs_4_.refs_8_
  38.8 4.9 %shard_map.86 = (bf16[8,16,1024]{2,1,0:T(8,128)(2,1)S(1)}, f32[8,16,896]{2,1,0:T(8,128)S(1)}, bf16[2,256,128]{2,1,0:T(8,128)(2,1)S(1)}) custom-call(s32[8,128]{1,0:T(8,128)S(1)} %get-tuple-element.84.refs_0_, f32[40,1152]{1,0:T(8,128)S(1)} %get-tuple-element.77.refs_1_.refs_5_, bf16[40,1152]{1,0:T(8,128)(2,1)S(1)} %collective-permute-done.13.refs_2_.refs_6_, ...), custom_call_target="tpu_custom_call" | custom-call | flops 7340032000 | bytes 4718592 | tf_op jit(solution)/shard_map/pallas_call | solution.py:492
  43.7 0.0 collective-permute-done.10.refs_2_
  43.8 0.0 collective-permute-done.11.refs_3_
  43.8 0.0 collective-permute-done.12.refs_4_
  43.8 5.6 %shard_map.87 = (bf16[8,16,2048]{2,1,0:T(8,128)(2,1)}, f32[8,16,2048]{2,1,0:T(8,128)}) custom-call(s32[8,128]{1,0:T(8,128)S(1)} %get-tuple-element.67.refs_0_, f32[40,1024]{1,0:T(8,128)S(1)} %get-tuple-element.73.refs_1_, bf16[40,1024]{1,0:T(8,128)(2,1)S(1)} %collective-permute-done.10.refs_2_, bf16[40,1024]{1,0:T(8,128)(2,1)S(1)} %collective-permute-done.11.refs_3_, ...), custom_call_target="tpu_custom_call" | custom-call | flops 7340032000 | bytes 4718592 | tf_op jit(solution)/shard_map/pallas_call | solution.py:492
  (5 shorter events, 0.1 us)
Async XLA Ops:
  0.6 3.3 %copy-start = (bf16[256,2048]{1,0:T(8,128)(2,1)S(1)}, bf16[256,2048]{1,0:T(8,128)(2,1)}, u32[]{:S(2)}) copy-start(bf16[256,2048]{1,0:T(8,128)(2,1)} %refs_2_.3) | copy-start | bytes 3145732
  0.6 3.2 %collective-permute-start.1 = (bf16[256,2048]{1,0:T(8,128)(2,1)}, bf16[256,2048]{1,0:T(8,128)(2,1)S(1)}, u32[]{:S(2)}, u32[]{:S(2)}) collective-permute-start(bf16[256,2048]{1,0:T(8,128)(2,1)} %refs_2_.3), channel_id=1, source_target_pairs={{0,4},{4,0},{8,12},{12,8},{16,20},{20,16},{24,28},{28,24},{1,5},{5... | collective-permute-start | bytes 3145736 | tf_op jit(solution)/shard_map/ppermute | solution.py:155
  1.9 1.6 %collective-permute-start = (s32[256,1]{0,1:T(1,128)S(1)}, s32[256,1]{0,1:T(1,128)S(1)}, u32[]{:S(2)}, u32[]{:S(2)}) collective-permute-start(s32[256,1]{0,1:T(1,128)S(1)} %multiply_add_fusion), channel_id=1, source_target_pairs={{0,4},{4,0},{8,12},{12,8},{16,20},{20,16},{24,28},{28,24},{1,5},{5... | collective-permute-start | bytes 3080 | tf_op jit(solution)/shard_map/ppermute | solution.py:155
  4.8 12.5 %collective-permute-start.3 = (bf16[272,640]{1,0:T(8,128)(2,1)S(1)}, bf16[272,640]{1,0:T(8,128)(2,1)S(1)}, u32[]{:S(2)}, u32[]{:S(2)}) collective-permute-start(bf16[272,640]{1,0:T(8,128)(2,1)S(1)} %get-tuple-element.52), channel_id=1, source_target_pairs={{0,16},{4,20},{8,24},{12,28},{16,0},{20,4},{24,8},{28,12},{1,17},{... | collective-permute-start | bytes 1044488 | tf_op jit(solution)/shard_map/ppermute | solution.py:155
  7.7 9.5 %collective-permute-start.2 = (bf16[272,512]{1,0:T(8,128)(2,1)S(1)}, bf16[272,512]{1,0:T(8,128)(2,1)S(1)}, u32[]{:S(2)}, u32[]{:S(2)}) collective-permute-start(bf16[272,512]{1,0:T(8,128)(2,1)S(1)} %get-tuple-element.50), channel_id=1, source_target_pairs={{0,8},{4,12},{8,0},{12,4},{16,24},{20,28},{24,16},{28,20},{1,9},{5... | collective-permute-start | bytes 835592 | tf_op jit(solution)/shard_map/ppermute | solution.py:155
  10.0 13.3 %collective-permute-start.6 = (bf16[272,512]{1,0:T(8,128)(2,1)S(1)}, bf16[272,512]{1,0:T(8,128)(2,1)S(1)}, u32[]{:S(2)}, u32[]{:S(2)}) collective-permute-start(bf16[272,512]{1,0:T(8,128)(2,1)S(1)} %get-tuple-element.61), channel_id=1, source_target_pairs={{0,8},{4,12},{8,0},{12,4},{16,24},{20,28},{24,16},{28,20},{1,9},{5... | collective-permute-start | bytes 835592 | tf_op jit(solution)/shard_map/ppermute | solution.py:155
  10.6 0.7 %copy-start.1 = (f32[4]{0:T(128)S(1)}, f32[4]{0:T(128)}, u32[]{:S(2)}) copy-start(f32[4]{0:T(128)} %offsets_ref.3) | copy-start | bytes 52
  10.6 0.7 %copy-start.2 = (f32[16]{0:T(128)S(1)}, f32[16]{0:T(128)}, u32[]{:S(2)}) copy-start(f32[16]{0:T(128)} %velocities_ref.3) | copy-start | bytes 196
  10.6 12.7 %collective-permute-start.7 = (bf16[272,512]{1,0:T(8,128)(2,1)S(1)}, bf16[272,512]{1,0:T(8,128)(2,1)S(1)}, u32[]{:S(2)}, u32[]{:S(2)}) collective-permute-start(bf16[272,512]{1,0:T(8,128)(2,1)S(1)} %get-tuple-element.63), channel_id=1, source_target_pairs={{0,16},{4,20},{8,24},{12,28},{16,0},{20,4},{24,8},{28,12},{1,17},{... | collective-permute-start | bytes 835592 | tf_op jit(solution)/shard_map/ppermute | solution.py:155
  17.4 8.9 %collective-permute-start.5 = (bf16[136,640]{1,0:T(8,128)(2,1)S(1)}, bf16[136,640]{1,0:T(8,128)(2,1)S(1)}, u32[]{:S(2)}, u32[]{:S(2)}) collective-permute-start(bf16[136,640]{1,0:T(8,128)(2,1)S(1)} %get-tuple-element.59), channel_id=1, source_target_pairs={{0,8},{4,12},{8,0},{12,4},{16,24},{20,28},{24,16},{28,20},{1,9},{5... | collective-permute-start | bytes 522248 | tf_op jit(solution)/shard_map/ppermute | solution.py:155
  19.0 7.4 %collective-permute-start.4 = (bf16[136,512]{1,0:T(8,128)(2,1)S(1)}, bf16[136,512]{1,0:T(8,128)(2,1)S(1)}, u32[]{:S(2)}, u32[]{:S(2)}) collective-permute-start(bf16[136,512]{1,0:T(8,128)(2,1)S(1)} %get-tuple-element.57), channel_id=1, source_target_pairs={{0,16},{4,20},{8,24},{12,28},{16,0},{20,4},{24,8},{28,12},{1,17},{... | collective-permute-start | bytes 417800 | tf_op jit(solution)/shard_map/ppermute | solution.py:155
  23.3 9.1 %collective-permute-start.8 = (bf16[136,512]{1,0:T(8,128)(2,1)S(1)}, bf16[136,512]{1,0:T(8,128)(2,1)S(1)}, u32[]{:S(2)}, u32[]{:S(2)}) collective-permute-start(bf16[136,512]{1,0:T(8,128)(2,1)S(1)} %get-tuple-element.69), channel_id=1, source_target_pairs={{0,16},{4,20},{8,24},{12,28},{16,0},{20,4},{24,8},{28,12},{1,17},{... | collective-permute-start | bytes 417800 | tf_op jit(solution)/shard_map/ppermute | solution.py:155
  24.9 7.6 %collective-permute-start.9 = (bf16[136,512]{1,0:T(8,128)(2,1)S(1)}, bf16[136,512]{1,0:T(8,128)(2,1)S(1)}, u32[]{:S(2)}, u32[]{:S(2)}) collective-permute-start(bf16[136,512]{1,0:T(8,128)(2,1)S(1)} %get-tuple-element.71), channel_id=1, source_target_pairs={{0,8},{4,12},{8,0},{12,4},{16,24},{20,28},{24,16},{28,20},{1,9},{5... | collective-permute-start | bytes 417800 | tf_op jit(solution)/shard_map/ppermute | solution.py:155
  26.5 10.3 %collective-permute-start.13 = (bf16[40,1152]{1,0:T(8,128)(2,1)S(1)}, bf16[40,1152]{1,0:T(8,128)(2,1)S(1)}, u32[]{:S(2)}, u32[]{:S(2)}) collective-permute-start(bf16[40,1152]{1,0:T(8,128)(2,1)S(1)} %get-tuple-element.78), channel_id=1, source_target_pairs={{0,3},{1,2},{2,1},{3,0},{4,7},{5,6},{6,5},{7,4},{8,11},{9,10},{10,... | collective-permute-start | bytes 276488 | tf_op jit(solution)/shard_map/ppermute | solution.py:228
  30.1 8.7 %collective-permute-start.14 = (bf16[40,1152]{1,0:T(8,128)(2,1)S(1)}, bf16[40,1152]{1,0:T(8,128)(2,1)S(1)}, u32[]{:S(2)}, u32[]{:S(2)}) collective-permute-start(bf16[40,1152]{1,0:T(8,128)(2,1)S(1)} %get-tuple-element.79), channel_id=1, source_target_pairs={{0,2},{1,3},{2,0},{3,1},{4,6},{5,7},{6,4},{7,5},{8,10},{9,11},{10,... | collective-permute-start | bytes 276488 | tf_op jit(solution)/shard_map/ppermute | solution.py:228
  30.1 8.7 %collective-permute-start.15 = (bf16[40,1152]{1,0:T(8,128)(2,1)S(1)}, bf16[40,1152]{1,0:T(8,128)(2,1)S(1)}, u32[]{:S(2)}, u32[]{:S(2)}) collective-permute-start(bf16[40,1152]{1,0:T(8,128)(2,1)S(1)} %get-tuple-element.80), channel_id=1, source_target_pairs={{0,1},{1,0},{2,3},{3,2},{4,5},{5,4},{6,7},{7,6},{8,9},{9,8},{10,11... | collective-permute-start | bytes 276488 | tf_op jit(solution)/shard_map/ppermute | solution.py:228
  32.6 11.2 %collective-permute-start.10 = (bf16[40,1024]{1,0:T(8,128)(2,1)S(1)}, bf16[40,1024]{1,0:T(8,128)(2,1)S(1)}, u32[]{:S(2)}, u32[]{:S(2)}) collective-permute-start(bf16[40,1024]{1,0:T(8,128)(2,1)S(1)} %get-tuple-element.74), channel_id=1, source_target_pairs={{0,1},{1,0},{2,3},{3,2},{4,5},{5,4},{6,7},{7,6},{8,9},{9,8},{10,11... | collective-permute-start | bytes 245768 | tf_op jit(solution)/shard_map/ppermute | solution.py:228
  33.9 9.9 %collective-permute-start.11 = (bf16[40,1024]{1,0:T(8,128)(2,1)S(1)}, bf16[40,1024]{1,0:T(8,128)(2,1)S(1)}, u32[]{:S(2)}, u32[]{:S(2)}) collective-permute-start(bf16[40,1024]{1,0:T(8,128)(2,1)S(1)} %get-tuple-element.75), channel_id=1, source_target_pairs={{0,2},{1,3},{2,0},{3,1},{4,6},{5,7},{6,4},{7,5},{8,10},{9,11},{10,... | collective-permute-start | bytes 245768 | tf_op jit(solution)/shard_map/ppermute | solution.py:228
  36.8 7.0 %collective-permute-start.12 = (bf16[40,1024]{1,0:T(8,128)(2,1)S(1)}, bf16[40,1024]{1,0:T(8,128)(2,1)S(1)}, u32[]{:S(2)}, u32[]{:S(2)}) collective-permute-start(bf16[40,1024]{1,0:T(8,128)(2,1)S(1)} %get-tuple-element.76), channel_id=1, source_target_pairs={{0,3},{1,2},{2,1},{3,0},{4,7},{5,6},{6,5},{7,4},{8,11},{9,10},{10,... | collective-permute-start | bytes 245768 | tf_op jit(solution)/shard_map/ppermute | solution.py:228

commit v7 on v6

--- a/solution.py
+++ b/solution.py
@@ -12,7 +12,7 @@
 CMP_DEV = 8
 LANES = 128
 UNROLL = 8
-PIECES = 2
+PIECES = 4
 VMEM_BYTES = 16 * 1024 * 1024
 F32 = jnp.float32
 BF16 = jnp.bfloat16
@@ -610,13 +610,13 @@
         spreads.append(part)
     rows = []
     for at, part in enumerate(spreads):
+        *spread, token = plan.spread(part, tokens[-1:])
+        tokens.append(token)
+        rows.append(plan.across(spread, at > 0))
         if at:
             *table, token = moveout(offsets, velocities, samples, *chunks[at], tokens[-1:])
             tables.append(table)
             tokens.append(token)
-        *spread, token = plan.spread(part, tokens[-1:])
-        rows.append(plan.across(spread, at > 0))
-        tokens.append(token)
     out = None
     for at, (start, stop) in enumerate(chunks):
         out = panels(

time: 49.6 us -> 49.5 us (level)
  no operation moved by 1% of the time
where the time goes in v7:
time: 49.5 us; the launch traced here: 49.4 us
  starting transfers between devices  21.2 us (43%)
  Pallas kernels  15.9 us (32%)
  waiting for transfers between devices  10.1 us (20%)
  other arithmetic  0.81 us (2%)
  between operations  0.78 us (2%)
  local copies, waits for them, and re-layouts  0.59 us (1%)
    ppermute x10, starting transfers between devices, swap(): lax.ppermute(value, 'inline', [(i, i ^ bit) for i in range(self.inline)])  11.7 us
    pallas_call x2, Pallas kernels, panels(): pl.pallas_call(functools.partial(panel_kernel, classes, vels, first, last...  10.5 us
    ppermute x6, starting transfers between devices, across(): lax.ppermute(block, 'xline', pairs)  9.42 us
    ppermute x10, waiting for transfers between devices, swap(): lax.ppermute(value, 'inline', [(i, i ^ bit) for i in range(self.inline)])  8.8 us
    pallas_call x2, Pallas kernels, moveout(): pl.pallas_call(functools.partial(table_kernel, classes, start, samples),...  3.05 us
    pallas_call x2, Pallas kernels, bin_rows(): pl.pallas_call(functools.partial(bin_kernel, len(members), len(data), kep...  1.63 us
    ppermute x6, waiting for transfers between devices, across(): lax.ppermute(block, 'xline', pairs)  1.32 us
  transfers between devices with their start and end apart: 16, of which 4 were waited for; matrix products, arithmetic and copies ran while one was open for 2% of the time, Pallas kernels for 19%

profile of v7, /device:TPU:0, one launch (start us, length us, event | category | flops | bytes accessed | tf_op | source)
XLA Modules:
  0.0 49.4 jit_solution(17347647034454694188)
XLA Ops:
  0.6 0.0 copy-start
  0.6 0.5 %collective-permute-start.1 = (bf16[256,2048]{1,0:T(8,128)(2,1)}, bf16[256,2048]{1,0:T(8,128)(2,1)S(1)}, u32[]{:S(2)}, u32[]{:S(2)}) collective-permute-start(bf16[256,2048]{1,0:T(8,128)(2,1)} %refs_2_.3), channel_id=1, source_target_pairs={{0,4},{4,0},{8,12},{12,8},{16,20},{20,16},{24,28},{28,24},{1,5},{5... | collective-permute-start | bytes 3145736 | tf_op jit(solution)/shard_map/ppermute | solution.py:155
  1.2 0.7 %multiply_add_fusion = s32[256,1]{0,1:T(1,128)S(1)} fusion(s32[256,1]{0,1:T(1,128)} %bitcast.10, s32[256,1]{0,1:T(1,128)} %bitcast.11, s32[256,1]{0,1:T(1,128)} %param.7), kind=kLoop, calls=%fused_computation.25 | loop fusion | flops 1024 | bytes 4096 | tf_op jit(solution)/shard_map/add | solution.py:591
  1.9 0.1 collective-permute-start
  2.0 1.4 %collective-permute-done = s32[256,1]{0,1:T(1,128)S(1)} collective-permute-done((s32[256,1]{0,1:T(1,128)S(1)}, s32[256,1]{0,1:T(1,128)S(1)}, u32[]{:S(2)}, u32[]{:S(2)}) %collective-permute-start) | collective-permute-done | bytes 1056 | tf_op jit(solution)/shard_map/ppermute | solution.py:155
  3.6 0.3 shard_map.77
  3.9 0.0 collective-permute-done.1.refs_3_
  3.9 0.0 copy-done
  3.9 0.9 %shard_map.78 = (f32[272,512]{1,0:T(8,128)S(1)}, bf16[272,512]{1,0:T(8,128)(2,1)S(1)}, f32[272,640]{1,0:T(8,128)S(1)}, bf16[272,640]{1,0:T(8,128)(2,1)S(1)}, f32[8,128]{1,0:T(8,128)S(1)}) custom-call(bf16[544,512]{1,0:T(8,128)(2,1)S(1)} %get-tuple-element.47.refs_0_, bf16[544,512]{1,0:T(8,128)(2,1)S(1)} %get-tuple-element.48.refs_1_, ...), custom_call_target="tpu_custom_call" | custom-call | flops 570425344 | tf_op jit(solution)/shard_map/pallas_call | solution.py:86
  4.8 2.9 %collective-permute-start.5 = (bf16[272,640]{1,0:T(8,128)(2,1)S(1)}, bf16[272,640]{1,0:T(8,128)(2,1)S(1)}, u32[]{:S(2)}, u32[]{:S(2)}) collective-permute-start(bf16[272,640]{1,0:T(8,128)(2,1)S(1)} %get-tuple-element.57), channel_id=1, source_target_pairs={{0,16},{4,20},{8,24},{12,28},{16,0},{20,4},{24,8},{28,12},{1,17},{... | collective-permute-start | bytes 1044488 | tf_op jit(solution)/shard_map/ppermute | solution.py:155
  7.7 1.5 %collective-permute-start.4 = (bf16[272,512]{1,0:T(8,128)(2,1)S(1)}, bf16[272,512]{1,0:T(8,128)(2,1)S(1)}, u32[]{:S(2)}, u32[]{:S(2)}) collective-permute-start(bf16[272,512]{1,0:T(8,128)(2,1)S(1)} %get-tuple-element.55), channel_id=1, source_target_pairs={{0,8},{4,12},{8,0},{12,4},{16,24},{20,28},{24,16},{28,20},{1,9},{5... | collective-permute-start | bytes 835592 | tf_op jit(solution)/shard_map/ppermute | solution.py:155
  9.2 0.7 %shard_map.79 = (f32[272,512]{1,0:T(8,128)S(1)}, bf16[272,512]{1,0:T(8,128)(2,1)S(1)}, f32[272,512]{1,0:T(8,128)S(1)}, bf16[272,512]{1,0:T(8,128)(2,1)S(1)}, f32[8,128]{1,0:T(8,128)S(1)}) custom-call(bf16[544,512]{1,0:T(8,128)(2,1)S(1)} %get-tuple-element.47.refs_0_, bf16[544,512]{1,0:T(8,128)(2,1)S(1)} %get-tuple-element.48.refs_1_, ...), custom_call_target="tpu_custom_call" | custom-call | flops 570425344 | tf_op jit(solution)/shard_map/pallas_call | solution.py:86
  10.0 0.6 %collective-permute-start.2 = (bf16[272,512]{1,0:T(8,128)(2,1)S(1)}, bf16[272,512]{1,0:T(8,128)(2,1)S(1)}, u32[]{:S(2)}, u32[]{:S(2)}) collective-permute-start(bf16[272,512]{1,0:T(8,128)(2,1)S(1)} %get-tuple-element.51), channel_id=1, source_target_pairs={{0,8},{4,12},{8,0},{12,4},{16,24},{20,28},{24,16},{28,20},{1,9},{5... | collective-permute-start | bytes 835592 | tf_op jit(solution)/shard_map/ppermute | solution.py:155
  10.6 0.1 collective-permute-start.3
  10.7 0.6 %copy-done.1 = f32[4]{0:T(128)S(1)} copy-done((f32[4]{0:T(128)S(1)}, f32[4]{0:T(128)}, u32[]{:S(2)}) %copy-start.1) | copy-done | bytes 40
  11.2 0.0 copy-done.2
  11.2 1.5 %shard_map.80 = (s32[16,8,1024]{2,1,0:T(8,128)S(1)}, f32[16,8,1024]{2,1,0:T(8,128)S(1)}, f32[16,8,1024]{2,1,0:T(8,128)S(1)}, s32[8,128]{1,0:T(8,128)S(1)}, f32[8,128]{1,0:T(8,128)S(1)}) custom-call(f32[4]{0:T(128)S(1)} %copy-done.1, f32[16]{0:T(128)S(1)} %copy-done.2, f32[8,128]{1,0:T(8,128)S(1)} %get-tuple-element.58.refs_0_), custom_call_target="tpu_custom_call" | custom-call | tf_op jit(solution)/shard_map/pallas_call | solution.py:569
  12.8 4.5 %collective-permute-done.4.refs_1_ = bf16[272,512]{1,0:T(8,128)(2,1)S(1)} collective-permute-done((bf16[272,512]{1,0:T(8,128)(2,1)S(1)}, bf16[272,512]{1,0:T(8,128)(2,1)S(1)}, u32[]{:S(2)}, u32[]{:S(2)}) %collective-permute-start.4) | collective-permute-done | bytes 278560 | tf_op jit(solution)/shard_map/ppermute | solution.py:155
  17.3 0.0 collective-permute-done.5.refs_3_
  17.3 0.1 shard_map.81
  17.4 1.6 %collective-permute-start.9 = (bf16[136,640]{1,0:T(8,128)(2,1)S(1)}, bf16[136,640]{1,0:T(8,128)(2,1)S(1)}, u32[]{:S(2)}, u32[]{:S(2)}) collective-permute-start(bf16[136,640]{1,0:T(8,128)(2,1)S(1)} %get-tuple-element.68), channel_id=1, source_target_pairs={{0,8},{4,12},{8,0},{12,4},{16,24},{20,28},{24,16},{28,20},{1,9},{5... | collective-permute-start | bytes 522248 | tf_op jit(solution)/shard_map/ppermute | solution.py:155
  19.0 1.4 %collective-permute-start.8 = (bf16[136,512]{1,0:T(8,128)(2,1)S(1)}, bf16[136,512]{1,0:T(8,128)(2,1)S(1)}, u32[]{:S(2)}, u32[]{:S(2)}) collective-permute-start(bf16[136,512]{1,0:T(8,128)(2,1)S(1)} %get-tuple-element.66), channel_id=1, source_target_pairs={{0,16},{4,20},{8,24},{12,28},{16,0},{20,4},{24,8},{28,12},{1,17},{... | collective-permute-start | bytes 417800 | tf_op jit(solution)/shard_map/ppermute | solution.py:155
  20.4 2.8 %collective-permute-done.2.refs_1_ = bf16[272,512]{1,0:T(8,128)(2,1)S(1)} collective-permute-done((bf16[272,512]{1,0:T(8,128)(2,1)S(1)}, bf16[272,512]{1,0:T(8,128)(2,1)S(1)}, u32[]{:S(2)}, u32[]{:S(2)}) %collective-permute-start.2) | collective-permute-done | bytes 278560 | tf_op jit(solution)/shard_map/ppermute | solution.py:155
  23.2 0.0 collective-permute-done.3.refs_3_
  23.2 0.1 shard_map.82
  23.3 1.5 %collective-permute-start.6 = (bf16[136,512]{1,0:T(8,128)(2,1)S(1)}, bf16[136,512]{1,0:T(8,128)(2,1)S(1)}, u32[]{:S(2)}, u32[]{:S(2)}) collective-permute-start(bf16[136,512]{1,0:T(8,128)(2,1)S(1)} %get-tuple-element.62), channel_id=1, source_target_pairs={{0,16},{4,20},{8,24},{12,28},{16,0},{20,4},{24,8},{28,12},{1,17},{... | collective-permute-start | bytes 417800 | tf_op jit(solution)/shard_map/ppermute | solution.py:155
  24.9 1.5 %collective-permute-start.7 = (bf16[136,512]{1,0:T(8,128)(2,1)S(1)}, bf16[136,512]{1,0:T(8,128)(2,1)S(1)}, u32[]{:S(2)}, u32[]{:S(2)}) collective-permute-start(bf16[136,512]{1,0:T(8,128)(2,1)S(1)} %get-tuple-element.64), channel_id=1, source_target_pairs={{0,8},{4,12},{8,0},{12,4},{16,24},{20,28},{24,16},{28,20},{1,9},{5... | collective-permute-start | bytes 417800 | tf_op jit(solution)/shard_map/ppermute | solution.py:155
  26.3 0.0 collective-permute-done.8.refs_1_
  26.3 0.0 collective-permute-done.9.refs_3_
  26.3 0.1 shard_map.83
  26.5 3.7 %collective-permute-start.13 = (bf16[40,1152]{1,0:T(8,128)(2,1)S(1)}, bf16[40,1152]{1,0:T(8,128)(2,1)S(1)}, u32[]{:S(2)}, u32[]{:S(2)}) collective-permute-start(bf16[40,1152]{1,0:T(8,128)(2,1)S(1)} %get-tuple-element.78), channel_id=1, source_target_pairs={{0,3},{1,2},{2,1},{3,0},{4,7},{5,6},{6,5},{7,4},{8,11},{9,10},{10,... | collective-permute-start | bytes 276488 | tf_op jit(solution)/shard_map/ppermute | solution.py:228
  30.1 0.0 collective-permute-start.14
  30.1 0.8 %collective-permute-start.15 = (bf16[40,1152]{1,0:T(8,128)(2,1)S(1)}, bf16[40,1152]{1,0:T(8,128)(2,1)S(1)}, u32[]{:S(2)}, u32[]{:S(2)}) collective-permute-start(bf16[40,1152]{1,0:T(8,128)(2,1)S(1)} %get-tuple-element.80), channel_id=1, source_target_pairs={{0,1},{1,0},{2,3},{3,2},{4,5},{5,4},{6,7},{7,6},{8,9},{9,8},{10,11... | collective-permute-start | bytes 276488 | tf_op jit(solution)/shard_map/ppermute | solution.py:228
  30.9 0.0 collective-permute-done.6.refs_1_
  30.9 0.0 collective-permute-done.7.refs_3_
  30.9 0.1 shard_map.84
  31.0 1.3 %collective-permute-start.10 = (bf16[40,1024]{1,0:T(8,128)(2,1)S(1)}, bf16[40,1024]{1,0:T(8,128)(2,1)S(1)}, u32[]{:S(2)}, u32[]{:S(2)}) collective-permute-start(bf16[40,1024]{1,0:T(8,128)(2,1)S(1)} %get-tuple-element.74), channel_id=1, source_target_pairs={{0,1},{1,0},{2,3},{3,2},{4,5},{5,4},{6,7},{7,6},{8,9},{9,8},{10,11... | collective-permute-start | bytes 245768 | tf_op jit(solution)/shard_map/ppermute | solution.py:228
  32.3 2.9 %collective-permute-start.11 = (bf16[40,1024]{1,0:T(8,128)(2,1)S(1)}, bf16[40,1024]{1,0:T(8,128)(2,1)S(1)}, u32[]{:S(2)}, u32[]{:S(2)}) collective-permute-start(bf16[40,1024]{1,0:T(8,128)(2,1)S(1)} %get-tuple-element.75), channel_id=1, source_target_pairs={{0,2},{1,3},{2,0},{3,1},{4,6},{5,7},{6,4},{7,5},{8,10},{9,11},{10,... | collective-permute-start | bytes 245768 | tf_op jit(solution)/shard_map/ppermute | solution.py:228
  35.2 1.5 %shard_map.85 = (s32[16,8,1024]{2,1,0:T(8,128)S(1)}, f32[16,8,1024]{2,1,0:T(8,128)S(1)}, f32[16,8,1024]{2,1,0:T(8,128)S(1)}, s32[8,128]{1,0:T(8,128)S(1)}, f32[8,128]{1,0:T(8,128)S(1)}) custom-call(f32[4]{0:T(128)S(1)} %copy-done.1, f32[16]{0:T(128)S(1)} %copy-done.2, f32[8,128]{1,0:T(8,128)S(1)} %get-tuple-element.71.refs_0_), custom_call_target="tpu_custom_call" | custom-call | tf_op jit(solution)/shard_map/pallas_call | solution.py:569
  36.8 0.0 collective-permute-done.13.refs_2_.refs_6_
  36.8 0.7 %collective-permute-start.12 = (bf16[40,1024]{1,0:T(8,128)(2,1)S(1)}, bf16[40,1024]{1,0:T(8,128)(2,1)S(1)}, u32[]{:S(2)}, u32[]{:S(2)}) collective-permute-start(bf16[40,1024]{1,0:T(8,128)(2,1)S(1)} %get-tuple-element.76), channel_id=1, source_target_pairs={{0,3},{1,2},{2,1},{3,0},{4,7},{5,6},{6,5},{7,4},{8,11},{9,10},{10,... | collective-permute-start | bytes 245768 | tf_op jit(solution)/shard_map/ppermute | solution.py:228
  37.5 1.3 %collective-permute-done.14.refs_3_.refs_7_ = bf16[40,1152]{1,0:T(8,128)(2,1)S(1)} collective-permute-done((bf16[40,1152]{1,0:T(8,128)(2,1)S(1)}, bf16[40,1152]{1,0:T(8,128)(2,1)S(1)}, u32[]{:S(2)}, u32[]{:S(2)}) %collective-permute-start.14) | collective-permute-done | bytes 92192 | tf_op jit(solution)/shard_map/ppermute | solution.py:228
  38.8 0.0 collective-permute-done.15.refs_4_.refs_8_
  38.8 4.9 %shard_map.86 = (bf16[8,16,1024]{2,1,0:T(8,128)(2,1)S(1)}, f32[8,16,896]{2,1,0:T(8,128)S(1)}, bf16[2,256,128]{2,1,0:T(8,128)(2,1)S(1)}) custom-call(s32[8,128]{1,0:T(8,128)S(1)} %get-tuple-element.84.refs_0_, f32[40,1152]{1,0:T(8,128)S(1)} %get-tuple-element.77.refs_1_.refs_5_, bf16[40,1152]{1,0:T(8,128)(2,1)S(1)} %collective-permute-done.13.refs_2_.refs_6_, ...), custom_call_target="tpu_custom_call" | custom-call | flops 7340032000 | bytes 4718592 | tf_op jit(solution)/shard_map/pallas_call | solution.py:492
  43.7 0.0 collective-permute-done.10.refs_2_
  43.7 0.0 collective-permute-done.11.refs_3_
  43.8 0.0 collective-permute-done.12.refs_4_
  43.8 5.6 %shard_map.87 = (bf16[8,16,2048]{2,1,0:T(8,128)(2,1)}, f32[8,16,2048]{2,1,0:T(8,128)}) custom-call(s32[8,128]{1,0:T(8,128)S(1)} %get-tuple-element.72.refs_0_, f32[40,1024]{1,0:T(8,128)S(1)} %get-tuple-element.73.refs_1_, bf16[40,1024]{1,0:T(8,128)(2,1)S(1)} %collective-permute-done.10.refs_2_, bf16[40,1024]{1,0:T(8,128)(2,1)S(1)} %collective-permute-done.11.refs_3_, ...), custom_call_target="tpu_custom_call" | custom-call | flops 7340032000 | bytes 4718592 | tf_op jit(solution)/shard_map/pallas_call | solution.py:492
  (5 shorter events, 0.1 us)
Async XLA Ops:
  0.6 3.3 %copy-start = (bf16[256,2048]{1,0:T(8,128)(2,1)S(1)}, bf16[256,2048]{1,0:T(8,128)(2,1)}, u32[]{:S(2)}) copy-start(bf16[256,2048]{1,0:T(8,128)(2,1)} %refs_2_.3) | copy-start | bytes 3145732
  0.6 3.2 %collective-permute-start.1 = (bf16[256,2048]{1,0:T(8,128)(2,1)}, bf16[256,2048]{1,0:T(8,128)(2,1)S(1)}, u32[]{:S(2)}, u32[]{:S(2)}) collective-permute-start(bf16[256,2048]{1,0:T(8,128)(2,1)} %refs_2_.3), channel_id=1, source_target_pairs={{0,4},{4,0},{8,12},{12,8},{16,20},{20,16},{24,28},{28,24},{1,5},{5... | collective-permute-start | bytes 3145736 | tf_op jit(solution)/shard_map/ppermute | solution.py:155
  1.9 1.6 %collective-permute-start = (s32[256,1]{0,1:T(1,128)S(1)}, s32[256,1]{0,1:T(1,128)S(1)}, u32[]{:S(2)}, u32[]{:S(2)}) collective-permute-start(s32[256,1]{0,1:T(1,128)S(1)} %multiply_add_fusion), channel_id=1, source_target_pairs={{0,4},{4,0},{8,12},{12,8},{16,20},{20,16},{24,28},{28,24},{1,5},{5... | collective-permute-start | bytes 3080 | tf_op jit(solution)/shard_map/ppermute | solution.py:155
  4.8 12.5 %collective-permute-start.5 = (bf16[272,640]{1,0:T(8,128)(2,1)S(1)}, bf16[272,640]{1,0:T(8,128)(2,1)S(1)}, u32[]{:S(2)}, u32[]{:S(2)}) collective-permute-start(bf16[272,640]{1,0:T(8,128)(2,1)S(1)} %get-tuple-element.57), channel_id=1, source_target_pairs={{0,16},{4,20},{8,24},{12,28},{16,0},{20,4},{24,8},{28,12},{1,17},{... | collective-permute-start | bytes 1044488 | tf_op jit(solution)/shard_map/ppermute | solution.py:155
  7.7 9.5 %collective-permute-start.4 = (bf16[272,512]{1,0:T(8,128)(2,1)S(1)}, bf16[272,512]{1,0:T(8,128)(2,1)S(1)}, u32[]{:S(2)}, u32[]{:S(2)}) collective-permute-start(bf16[272,512]{1,0:T(8,128)(2,1)S(1)} %get-tuple-element.55), channel_id=1, source_target_pairs={{0,8},{4,12},{8,0},{12,4},{16,24},{20,28},{24,16},{28,20},{1,9},{5... | collective-permute-start | bytes 835592 | tf_op jit(solution)/shard_map/ppermute | solution.py:155
  10.0 13.3 %collective-permute-start.2 = (bf16[272,512]{1,0:T(8,128)(2,1)S(1)}, bf16[272,512]{1,0:T(8,128)(2,1)S(1)}, u32[]{:S(2)}, u32[]{:S(2)}) collective-permute-start(bf16[272,512]{1,0:T(8,128)(2,1)S(1)} %get-tuple-element.51), channel_id=1, source_target_pairs={{0,8},{4,12},{8,0},{12,4},{16,24},{20,28},{24,16},{28,20},{1,9},{5... | collective-permute-start | bytes 835592 | tf_op jit(solution)/shard_map/ppermute | solution.py:155
  10.6 0.7 %copy-start.1 = (f32[4]{0:T(128)S(1)}, f32[4]{0:T(128)}, u32[]{:S(2)}) copy-start(f32[4]{0:T(128)} %offsets_ref.3) | copy-start | bytes 52
  10.6 0.7 %copy-start.2 = (f32[16]{0:T(128)S(1)}, f32[16]{0:T(128)}, u32[]{:S(2)}) copy-start(f32[16]{0:T(128)} %velocities_ref.3) | copy-start | bytes 196
  10.6 12.7 %collective-permute-start.3 = (bf16[272,512]{1,0:T(8,128)(2,1)S(1)}, bf16[272,512]{1,0:T(8,128)(2,1)S(1)}, u32[]{:S(2)}, u32[]{:S(2)}) collective-permute-start(bf16[272,512]{1,0:T(8,128)(2,1)S(1)} %get-tuple-element.53), channel_id=1, source_target_pairs={{0,16},{4,20},{8,24},{12,28},{16,0},{20,4},{24,8},{28,12},{1,17},{... | collective-permute-start | bytes 835592 | tf_op jit(solution)/shard_map/ppermute | solution.py:155
  17.4 8.9 %collective-permute-start.9 = (bf16[136,640]{1,0:T(8,128)(2,1)S(1)}, bf16[136,640]{1,0:T(8,128)(2,1)S(1)}, u32[]{:S(2)}, u32[]{:S(2)}) collective-permute-start(bf16[136,640]{1,0:T(8,128)(2,1)S(1)} %get-tuple-element.68), channel_id=1, source_target_pairs={{0,8},{4,12},{8,0},{12,4},{16,24},{20,28},{24,16},{28,20},{1,9},{5... | collective-permute-start | bytes 522248 | tf_op jit(solution)/shard_map/ppermute | solution.py:155
  19.0 7.4 %collective-permute-start.8 = (bf16[136,512]{1,0:T(8,128)(2,1)S(1)}, bf16[136,512]{1,0:T(8,128)(2,1)S(1)}, u32[]{:S(2)}, u32[]{:S(2)}) collective-permute-start(bf16[136,512]{1,0:T(8,128)(2,1)S(1)} %get-tuple-element.66), channel_id=1, source_target_pairs={{0,16},{4,20},{8,24},{12,28},{16,0},{20,4},{24,8},{28,12},{1,17},{... | collective-permute-start | bytes 417800 | tf_op jit(solution)/shard_map/ppermute | solution.py:155
  23.3 7.6 %collective-permute-start.6 = (bf16[136,512]{1,0:T(8,128)(2,1)S(1)}, bf16[136,512]{1,0:T(8,128)(2,1)S(1)}, u32[]{:S(2)}, u32[]{:S(2)}) collective-permute-start(bf16[136,512]{1,0:T(8,128)(2,1)S(1)} %get-tuple-element.62), channel_id=1, source_target_pairs={{0,16},{4,20},{8,24},{12,28},{16,0},{20,4},{24,8},{28,12},{1,17},{... | collective-permute-start | bytes 417800 | tf_op jit(solution)/shard_map/ppermute | solution.py:155
  24.9 6.1 %collective-permute-start.7 = (bf16[136,512]{1,0:T(8,128)(2,1)S(1)}, bf16[136,512]{1,0:T(8,128)(2,1)S(1)}, u32[]{:S(2)}, u32[]{:S(2)}) collective-permute-start(bf16[136,512]{1,0:T(8,128)(2,1)S(1)} %get-tuple-element.64), channel_id=1, source_target_pairs={{0,8},{4,12},{8,0},{12,4},{16,24},{20,28},{24,16},{28,20},{1,9},{5... | collective-permute-start | bytes 417800 | tf_op jit(solution)/shard_map/ppermute | solution.py:155
  26.5 10.3 %collective-permute-start.13 = (bf16[40,1152]{1,0:T(8,128)(2,1)S(1)}, bf16[40,1152]{1,0:T(8,128)(2,1)S(1)}, u32[]{:S(2)}, u32[]{:S(2)}) collective-permute-start(bf16[40,1152]{1,0:T(8,128)(2,1)S(1)} %get-tuple-element.78), channel_id=1, source_target_pairs={{0,3},{1,2},{2,1},{3,0},{4,7},{5,6},{6,5},{7,4},{8,11},{9,10},{10,... | collective-permute-start | bytes 276488 | tf_op jit(solution)/shard_map/ppermute | solution.py:228
  30.1 8.7 %collective-permute-start.14 = (bf16[40,1152]{1,0:T(8,128)(2,1)S(1)}, bf16[40,1152]{1,0:T(8,128)(2,1)S(1)}, u32[]{:S(2)}, u32[]{:S(2)}) collective-permute-start(bf16[40,1152]{1,0:T(8,128)(2,1)S(1)} %get-tuple-element.79), channel_id=1, source_target_pairs={{0,2},{1,3},{2,0},{3,1},{4,6},{5,7},{6,4},{7,5},{8,10},{9,11},{10,... | collective-permute-start | bytes 276488 | tf_op jit(solution)/shard_map/ppermute | solution.py:228
  30.1 8.7 %collective-permute-start.15 = (bf16[40,1152]{1,0:T(8,128)(2,1)S(1)}, bf16[40,1152]{1,0:T(8,128)(2,1)S(1)}, u32[]{:S(2)}, u32[]{:S(2)}) collective-permute-start(bf16[40,1152]{1,0:T(8,128)(2,1)S(1)} %get-tuple-element.80), channel_id=1, source_target_pairs={{0,1},{1,0},{2,3},{3,2},{4,5},{5,4},{6,7},{7,6},{8,9},{9,8},{10,11... | collective-permute-start | bytes 276488 | tf_op jit(solution)/shard_map/ppermute | solution.py:228
  31.0 12.7 %collective-permute-start.10 = (bf16[40,1024]{1,0:T(8,128)(2,1)S(1)}, bf16[40,1024]{1,0:T(8,128)(2,1)S(1)}, u32[]{:S(2)}, u32[]{:S(2)}) collective-permute-start(bf16[40,1024]{1,0:T(8,128)(2,1)S(1)} %get-tuple-element.74), channel_id=1, source_target_pairs={{0,1},{1,0},{2,3},{3,2},{4,5},{5,4},{6,7},{7,6},{8,9},{9,8},{10,11... | collective-permute-start | bytes 245768 | tf_op jit(solution)/shard_map/ppermute | solution.py:228
  32.3 11.4 %collective-permute-start.11 = (bf16[40,1024]{1,0:T(8,128)(2,1)S(1)}, bf16[40,1024]{1,0:T(8,128)(2,1)S(1)}, u32[]{:S(2)}, u32[]{:S(2)}) collective-permute-start(bf16[40,1024]{1,0:T(8,128)(2,1)S(1)} %get-tuple-element.75), channel_id=1, source_target_pairs={{0,2},{1,3},{2,0},{3,1},{4,6},{5,7},{6,4},{7,5},{8,10},{9,11},{10,... | collective-permute-start | bytes 245768 | tf_op jit(solution)/shard_map/ppermute | solution.py:228
  36.8 7.0 %collective-permute-start.12 = (bf16[40,1024]{1,0:T(8,128)(2,1)S(1)}, bf16[40,1024]{1,0:T(8,128)(2,1)S(1)}, u32[]{:S(2)}, u32[]{:S(2)}) collective-permute-start(bf16[40,1024]{1,0:T(8,128)(2,1)S(1)} %get-tuple-element.76), channel_id=1, source_target_pairs={{0,3},{1,2},{2,1},{3,0},{4,7},{5,6},{6,5},{7,4},{8,11},{9,10},{10,... | collective-permute-start | bytes 245768 | tf_op jit(solution)/shard_map/ppermute | solution.py:228

commit v8 on v7

--- a/solution.py
+++ b/solution.py
@@ -440,7 +440,7 @@
             return 0
 
         lax.fori_loop(0, vels, per_velocity, 0, unroll=math.gcd(vels, UNROLL * pieces))
-        lax.fori_loop(low, top, per_block, 0, unroll=math.gcd(top - low, 2 * pieces))
+        lax.fori_loop(low, top, per_block, 0, unroll=math.gcd(top - low, 4))
         if first == 0:
             leave(stacked_ref.at[:, :, low * LANES : top * LANES], stacked_out, low, top)
         ready = low + 1 if low else begin

time: 49.5 us -> 49.5 us (level)
  no operation moved by 1% of the time
where the time goes in v8:
time: 49.5 us; the launch traced here: 49.4 us
  starting transfers between devices  21.2 us (43%)
  Pallas kernels  15.9 us (32%)
  waiting for transfers between devices  10.1 us (20%)
  other arithmetic  0.81 us (2%)
  between operations  0.78 us (2%)
  local copies, waits for them, and re-layouts  0.59 us (1%)
    ppermute x10, starting transfers between devices, swap(): lax.ppermute(value, 'inline', [(i, i ^ bit) for i in range(self.inline)])  11.7 us
    pallas_call x2, Pallas kernels, panels(): pl.pallas_call(functools.partial(panel_kernel, classes, vels, first, last...  10.5 us
    ppermute x6, starting transfers between devices, across(): lax.ppermute(block, 'xline', pairs)  9.42 us
    ppermute x10, waiting for transfers between devices, swap(): lax.ppermute(value, 'inline', [(i, i ^ bit) for i in range(self.inline)])  8.8 us
    pallas_call x2, Pallas kernels, moveout(): pl.pallas_call(functools.partial(table_kernel, classes, start, samples),...  3.05 us
    pallas_call x2, Pallas kernels, bin_rows(): pl.pallas_call(functools.partial(bin_kernel, len(members), len(data), kep...  1.63 us
    ppermute x6, waiting for transfers between devices, across(): lax.ppermute(block, 'xline', pairs)  1.32 us
  transfers between devices with their start and end apart: 16, of which 4 were waited for; matrix products, arithmetic and copies ran while one was open for 2% of the time, Pallas kernels for 19%

profile of v8, /device:TPU:0, one launch (start us, length us, event | category | flops | bytes accessed | tf_op | source)
XLA Modules:
  0.0 49.4 jit_solution(7325134394643333839)
XLA Ops:
  0.6 0.0 copy-start
  0.6 0.5 %collective-permute-start.1 = (bf16[256,2048]{1,0:T(8,128)(2,1)}, bf16[256,2048]{1,0:T(8,128)(2,1)S(1)}, u32[]{:S(2)}, u32[]{:S(2)}) collective-permute-start(bf16[256,2048]{1,0:T(8,128)(2,1)} %refs_2_.3), channel_id=1, source_target_pairs={{0,4},{4,0},{8,12},{12,8},{16,20},{20,16},{24,28},{28,24},{1,5},{5... | collective-permute-start | bytes 3145736 | tf_op jit(solution)/shard_map/ppermute | solution.py:155
  1.2 0.7 %multiply_add_fusion = s32[256,1]{0,1:T(1,128)S(1)} fusion(s32[256,1]{0,1:T(1,128)} %bitcast.10, s32[256,1]{0,1:T(1,128)} %bitcast.11, s32[256,1]{0,1:T(1,128)} %param.7), kind=kLoop, calls=%fused_computation.25 | loop fusion | flops 1024 | bytes 4096 | tf_op jit(solution)/shard_map/add | solution.py:591
  1.9 0.1 collective-permute-start
  2.0 1.4 %collective-permute-done = s32[256,1]{0,1:T(1,128)S(1)} collective-permute-done((s32[256,1]{0,1:T(1,128)S(1)}, s32[256,1]{0,1:T(1,128)S(1)}, u32[]{:S(2)}, u32[]{:S(2)}) %collective-permute-start) | collective-permute-done | bytes 1056 | tf_op jit(solution)/shard_map/ppermute | solution.py:155
  3.6 0.3 shard_map.77
  3.9 0.0 collective-permute-done.1.refs_3_
  3.9 0.0 copy-done
  3.9 0.9 %shard_map.78 = (f32[272,512]{1,0:T(8,128)S(1)}, bf16[272,512]{1,0:T(8,128)(2,1)S(1)}, f32[272,640]{1,0:T(8,128)S(1)}, bf16[272,640]{1,0:T(8,128)(2,1)S(1)}, f32[8,128]{1,0:T(8,128)S(1)}) custom-call(bf16[544,512]{1,0:T(8,128)(2,1)S(1)} %get-tuple-element.47.refs_0_, bf16[544,512]{1,0:T(8,128)(2,1)S(1)} %get-tuple-element.48.refs_1_, ...), custom_call_target="tpu_custom_call" | custom-call | flops 570425344 | tf_op jit(solution)/shard_map/pallas_call | solution.py:86
  4.8 2.9 %collective-permute-start.5 = (bf16[272,640]{1,0:T(8,128)(2,1)S(1)}, bf16[272,640]{1,0:T(8,128)(2,1)S(1)}, u32[]{:S(2)}, u32[]{:S(2)}) collective-permute-start(bf16[272,640]{1,0:T(8,128)(2,1)S(1)} %get-tuple-element.57), channel_id=1, source_target_pairs={{0,16},{4,20},{8,24},{12,28},{16,0},{20,4},{24,8},{28,12},{1,17},{... | collective-permute-start | bytes 1044488 | tf_op jit(solution)/shard_map/ppermute | solution.py:155
  7.7 1.5 %collective-permute-start.4 = (bf16[272,512]{1,0:T(8,128)(2,1)S(1)}, bf16[272,512]{1,0:T(8,128)(2,1)S(1)}, u32[]{:S(2)}, u32[]{:S(2)}) collective-permute-start(bf16[272,512]{1,0:T(8,128)(2,1)S(1)} %get-tuple-element.55), channel_id=1, source_target_pairs={{0,8},{4,12},{8,0},{12,4},{16,24},{20,28},{24,16},{28,20},{1,9},{5... | collective-permute-start | bytes 835592 | tf_op jit(solution)/shard_map/ppermute | solution.py:155
  9.2 0.7 %shard_map.79 = (f32[272,512]{1,0:T(8,128)S(1)}, bf16[272,512]{1,0:T(8,128)(2,1)S(1)}, f32[272,512]{1,0:T(8,128)S(1)}, bf16[272,512]{1,0:T(8,128)(2,1)S(1)}, f32[8,128]{1,0:T(8,128)S(1)}) custom-call(bf16[544,512]{1,0:T(8,128)(2,1)S(1)} %get-tuple-element.47.refs_0_, bf16[544,512]{1,0:T(8,128)(2,1)S(1)} %get-tuple-element.48.refs_1_, ...), custom_call_target="tpu_custom_call" | custom-call | flops 570425344 | tf_op jit(solution)/shard_map/pallas_call | solution.py:86
  10.0 0.6 %collective-permute-start.2 = (bf16[272,512]{1,0:T(8,128)(2,1)S(1)}, bf16[272,512]{1,0:T(8,128)(2,1)S(1)}, u32[]{:S(2)}, u32[]{:S(2)}) collective-permute-start(bf16[272,512]{1,0:T(8,128)(2,1)S(1)} %get-tuple-element.51), channel_id=1, source_target_pairs={{0,8},{4,12},{8,0},{12,4},{16,24},{20,28},{24,16},{28,20},{1,9},{5... | collective-permute-start | bytes 835592 | tf_op jit(solution)/shard_map/ppermute | solution.py:155
  10.6 0.1 collective-permute-start.3
  10.7 0.6 %copy-done.1 = f32[4]{0:T(128)S(1)} copy-done((f32[4]{0:T(128)S(1)}, f32[4]{0:T(128)}, u32[]{:S(2)}) %copy-start.1) | copy-done | bytes 40
  11.2 0.0 copy-done.2
  11.2 1.5 %shard_map.80 = (s32[16,8,1024]{2,1,0:T(8,128)S(1)}, f32[16,8,1024]{2,1,0:T(8,128)S(1)}, f32[16,8,1024]{2,1,0:T(8,128)S(1)}, s32[8,128]{1,0:T(8,128)S(1)}, f32[8,128]{1,0:T(8,128)S(1)}) custom-call(f32[4]{0:T(128)S(1)} %copy-done.1, f32[16]{0:T(128)S(1)} %copy-done.2, f32[8,128]{1,0:T(8,128)S(1)} %get-tuple-element.58.refs_0_), custom_call_target="tpu_custom_call" | custom-call | tf_op jit(solution)/shard_map/pallas_call | solution.py:569
  12.8 4.5 %collective-permute-done.4.refs_1_ = bf16[272,512]{1,0:T(8,128)(2,1)S(1)} collective-permute-done((bf16[272,512]{1,0:T(8,128)(2,1)S(1)}, bf16[272,512]{1,0:T(8,128)(2,1)S(1)}, u32[]{:S(2)}, u32[]{:S(2)}) %collective-permute-start.4) | collective-permute-done | bytes 278560 | tf_op jit(solution)/shard_map/ppermute | solution.py:155
  17.3 0.0 collective-permute-done.5.refs_3_
  17.3 0.1 shard_map.81
  17.4 1.6 %collective-permute-start.9 = (bf16[136,640]{1,0:T(8,128)(2,1)S(1)}, bf16[136,640]{1,0:T(8,128)(2,1)S(1)}, u32[]{:S(2)}, u32[]{:S(2)}) collective-permute-start(bf16[136,640]{1,0:T(8,128)(2,1)S(1)} %get-tuple-element.68), channel_id=1, source_target_pairs={{0,8},{4,12},{8,0},{12,4},{16,24},{20,28},{24,16},{28,20},{1,9},{5... | collective-permute-start | bytes 522248 | tf_op jit(solution)/shard_map/ppermute | solution.py:155
  19.0 1.4 %collective-permute-start.8 = (bf16[136,512]{1,0:T(8,128)(2,1)S(1)}, bf16[136,512]{1,0:T(8,128)(2,1)S(1)}, u32[]{:S(2)}, u32[]{:S(2)}) collective-permute-start(bf16[136,512]{1,0:T(8,128)(2,1)S(1)} %get-tuple-element.66), channel_id=1, source_target_pairs={{0,16},{4,20},{8,24},{12,28},{16,0},{20,4},{24,8},{28,12},{1,17},{... | collective-permute-start | bytes 417800 | tf_op jit(solution)/shard_map/ppermute | solution.py:155
  20.4 2.8 %collective-permute-done.2.refs_1_ = bf16[272,512]{1,0:T(8,128)(2,1)S(1)} collective-permute-done((bf16[272,512]{1,0:T(8,128)(2,1)S(1)}, bf16[272,512]{1,0:T(8,128)(2,1)S(1)}, u32[]{:S(2)}, u32[]{:S(2)}) %collective-permute-start.2) | collective-permute-done | bytes 278560 | tf_op jit(solution)/shard_map/ppermute | solution.py:155
  23.2 0.0 collective-permute-done.3.refs_3_
  23.2 0.1 shard_map.82
  23.3 1.5 %collective-permute-start.6 = (bf16[136,512]{1,0:T(8,128)(2,1)S(1)}, bf16[136,512]{1,0:T(8,128)(2,1)S(1)}, u32[]{:S(2)}, u32[]{:S(2)}) collective-permute-start(bf16[136,512]{1,0:T(8,128)(2,1)S(1)} %get-tuple-element.62), channel_id=1, source_target_pairs={{0,16},{4,20},{8,24},{12,28},{16,0},{20,4},{24,8},{28,12},{1,17},{... | collective-permute-start | bytes 417800 | tf_op jit(solution)/shard_map/ppermute | solution.py:155
  24.9 1.5 %collective-permute-start.7 = (bf16[136,512]{1,0:T(8,128)(2,1)S(1)}, bf16[136,512]{1,0:T(8,128)(2,1)S(1)}, u32[]{:S(2)}, u32[]{:S(2)}) collective-permute-start(bf16[136,512]{1,0:T(8,128)(2,1)S(1)} %get-tuple-element.64), channel_id=1, source_target_pairs={{0,8},{4,12},{8,0},{12,4},{16,24},{20,28},{24,16},{28,20},{1,9},{5... | collective-permute-start | bytes 417800 | tf_op jit(solution)/shard_map/ppermute | solution.py:155
  26.3 0.0 collective-permute-done.8.refs_1_
  26.3 0.0 collective-permute-done.9.refs_3_
  26.3 0.1 shard_map.83
  26.5 3.7 %collective-permute-start.13 = (bf16[40,1152]{1,0:T(8,128)(2,1)S(1)}, bf16[40,1152]{1,0:T(8,128)(2,1)S(1)}, u32[]{:S(2)}, u32[]{:S(2)}) collective-permute-start(bf16[40,1152]{1,0:T(8,128)(2,1)S(1)} %get-tuple-element.78), channel_id=1, source_target_pairs={{0,3},{1,2},{2,1},{3,0},{4,7},{5,6},{6,5},{7,4},{8,11},{9,10},{10,... | collective-permute-start | bytes 276488 | tf_op jit(solution)/shard_map/ppermute | solution.py:228
  30.1 0.0 collective-permute-start.14
  30.1 0.8 %collective-permute-start.15 = (bf16[40,1152]{1,0:T(8,128)(2,1)S(1)}, bf16[40,1152]{1,0:T(8,128)(2,1)S(1)}, u32[]{:S(2)}, u32[]{:S(2)}) collective-permute-start(bf16[40,1152]{1,0:T(8,128)(2,1)S(1)} %get-tuple-element.80), channel_id=1, source_target_pairs={{0,1},{1,0},{2,3},{3,2},{4,5},{5,4},{6,7},{7,6},{8,9},{9,8},{10,11... | collective-permute-start | bytes 276488 | tf_op jit(solution)/shard_map/ppermute | solution.py:228
  30.9 0.0 collective-permute-done.6.refs_1_
  30.9 0.0 collective-permute-done.7.refs_3_
  30.9 0.1 shard_map.84
  31.0 1.3 %collective-permute-start.10 = (bf16[40,1024]{1,0:T(8,128)(2,1)S(1)}, bf16[40,1024]{1,0:T(8,128)(2,1)S(1)}, u32[]{:S(2)}, u32[]{:S(2)}) collective-permute-start(bf16[40,1024]{1,0:T(8,128)(2,1)S(1)} %get-tuple-element.74), channel_id=1, source_target_pairs={{0,1},{1,0},{2,3},{3,2},{4,5},{5,4},{6,7},{7,6},{8,9},{9,8},{10,11... | collective-permute-start | bytes 245768 | tf_op jit(solution)/shard_map/ppermute | solution.py:228
  32.3 2.9 %collective-permute-start.11 = (bf16[40,1024]{1,0:T(8,128)(2,1)S(1)}, bf16[40,1024]{1,0:T(8,128)(2,1)S(1)}, u32[]{:S(2)}, u32[]{:S(2)}) collective-permute-start(bf16[40,1024]{1,0:T(8,128)(2,1)S(1)} %get-tuple-element.75), channel_id=1, source_target_pairs={{0,2},{1,3},{2,0},{3,1},{4,6},{5,7},{6,4},{7,5},{8,10},{9,11},{10,... | collective-permute-start | bytes 245768 | tf_op jit(solution)/shard_map/ppermute | solution.py:228
  35.2 1.5 %shard_map.85 = (s32[16,8,1024]{2,1,0:T(8,128)S(1)}, f32[16,8,1024]{2,1,0:T(8,128)S(1)}, f32[16,8,1024]{2,1,0:T(8,128)S(1)}, s32[8,128]{1,0:T(8,128)S(1)}, f32[8,128]{1,0:T(8,128)S(1)}) custom-call(f32[4]{0:T(128)S(1)} %copy-done.1, f32[16]{0:T(128)S(1)} %copy-done.2, f32[8,128]{1,0:T(8,128)S(1)} %get-tuple-element.71.refs_0_), custom_call_target="tpu_custom_call" | custom-call | tf_op jit(solution)/shard_map/pallas_call | solution.py:569
  36.8 0.0 collective-permute-done.13.refs_2_.refs_6_
  36.8 0.7 %collective-permute-start.12 = (bf16[40,1024]{1,0:T(8,128)(2,1)S(1)}, bf16[40,1024]{1,0:T(8,128)(2,1)S(1)}, u32[]{:S(2)}, u32[]{:S(2)}) collective-permute-start(bf16[40,1024]{1,0:T(8,128)(2,1)S(1)} %get-tuple-element.76), channel_id=1, source_target_pairs={{0,3},{1,2},{2,1},{3,0},{4,7},{5,6},{6,5},{7,4},{8,11},{9,10},{10,... | collective-permute-start | bytes 245768 | tf_op jit(solution)/shard_map/ppermute | solution.py:228
  37.5 1.3 %collective-permute-done.14.refs_3_.refs_7_ = bf16[40,1152]{1,0:T(8,128)(2,1)S(1)} collective-permute-done((bf16[40,1152]{1,0:T(8,128)(2,1)S(1)}, bf16[40,1152]{1,0:T(8,128)(2,1)S(1)}, u32[]{:S(2)}, u32[]{:S(2)}) %collective-permute-start.14) | collective-permute-done | bytes 92192 | tf_op jit(solution)/shard_map/ppermute | solution.py:228
  38.8 0.0 collective-permute-done.15.refs_4_.refs_8_
  38.8 4.9 %shard_map.86 = (bf16[8,16,1024]{2,1,0:T(8,128)(2,1)S(1)}, f32[8,16,896]{2,1,0:T(8,128)S(1)}, bf16[2,256,128]{2,1,0:T(8,128)(2,1)S(1)}) custom-call(s32[8,128]{1,0:T(8,128)S(1)} %get-tuple-element.84.refs_0_, f32[40,1152]{1,0:T(8,128)S(1)} %get-tuple-element.77.refs_1_.refs_5_, bf16[40,1152]{1,0:T(8,128)(2,1)S(1)} %collective-permute-done.13.refs_2_.refs_6_, ...), custom_call_target="tpu_custom_call" | custom-call | flops 7340032000 | bytes 4718592 | tf_op jit(solution)/shard_map/pallas_call | solution.py:492
  43.7 0.0 collective-permute-done.10.refs_2_
  43.7 0.0 collective-permute-done.11.refs_3_
  43.8 0.0 collective-permute-done.12.refs_4_
  43.8 5.6 %shard_map.87 = (bf16[8,16,2048]{2,1,0:T(8,128)(2,1)}, f32[8,16,2048]{2,1,0:T(8,128)}) custom-call(s32[8,128]{1,0:T(8,128)S(1)} %get-tuple-element.72.refs_0_, f32[40,1024]{1,0:T(8,128)S(1)} %get-tuple-element.73.refs_1_, bf16[40,1024]{1,0:T(8,128)(2,1)S(1)} %collective-permute-done.10.refs_2_, bf16[40,1024]{1,0:T(8,128)(2,1)S(1)} %collective-permute-done.11.refs_3_, ...), custom_call_target="tpu_custom_call" | custom-call | flops 7340032000 | bytes 4718592 | tf_op jit(solution)/shard_map/pallas_call | solution.py:492
  (5 shorter events, 0.1 us)
Async XLA Ops:
  0.6 3.3 %copy-start = (bf16[256,2048]{1,0:T(8,128)(2,1)S(1)}, bf16[256,2048]{1,0:T(8,128)(2,1)}, u32[]{:S(2)}) copy-start(bf16[256,2048]{1,0:T(8,128)(2,1)} %refs_2_.3) | copy-start | bytes 3145732
  0.6 3.2 %collective-permute-start.1 = (bf16[256,2048]{1,0:T(8,128)(2,1)}, bf16[256,2048]{1,0:T(8,128)(2,1)S(1)}, u32[]{:S(2)}, u32[]{:S(2)}) collective-permute-start(bf16[256,2048]{1,0:T(8,128)(2,1)} %refs_2_.3), channel_id=1, source_target_pairs={{0,4},{4,0},{8,12},{12,8},{16,20},{20,16},{24,28},{28,24},{1,5},{5... | collective-permute-start | bytes 3145736 | tf_op jit(solution)/shard_map/ppermute | solution.py:155
  1.9 1.6 %collective-permute-start = (s32[256,1]{0,1:T(1,128)S(1)}, s32[256,1]{0,1:T(1,128)S(1)}, u32[]{:S(2)}, u32[]{:S(2)}) collective-permute-start(s32[256,1]{0,1:T(1,128)S(1)} %multiply_add_fusion), channel_id=1, source_target_pairs={{0,4},{4,0},{8,12},{12,8},{16,20},{20,16},{24,28},{28,24},{1,5},{5... | collective-permute-start | bytes 3080 | tf_op jit(solution)/shard_map/ppermute | solution.py:155
  4.8 12.5 %collective-permute-start.5 = (bf16[272,640]{1,0:T(8,128)(2,1)S(1)}, bf16[272,640]{1,0:T(8,128)(2,1)S(1)}, u32[]{:S(2)}, u32[]{:S(2)}) collective-permute-start(bf16[272,640]{1,0:T(8,128)(2,1)S(1)} %get-tuple-element.57), channel_id=1, source_target_pairs={{0,16},{4,20},{8,24},{12,28},{16,0},{20,4},{24,8},{28,12},{1,17},{... | collective-permute-start | bytes 1044488 | tf_op jit(solution)/shard_map/ppermute | solution.py:155
  7.7 9.5 %collective-permute-start.4 = (bf16[272,512]{1,0:T(8,128)(2,1)S(1)}, bf16[272,512]{1,0:T(8,128)(2,1)S(1)}, u32[]{:S(2)}, u32[]{:S(2)}) collective-permute-start(bf16[272,512]{1,0:T(8,128)(2,1)S(1)} %get-tuple-element.55), channel_id=1, source_target_pairs={{0,8},{4,12},{8,0},{12,4},{16,24},{20,28},{24,16},{28,20},{1,9},{5... | collective-permute-start | bytes 835592 | tf_op jit(solution)/shard_map/ppermute | solution.py:155
  10.0 13.3 %collective-permute-start.2 = (bf16[272,512]{1,0:T(8,128)(2,1)S(1)}, bf16[272,512]{1,0:T(8,128)(2,1)S(1)}, u32[]{:S(2)}, u32[]{:S(2)}) collective-permute-start(bf16[272,512]{1,0:T(8,128)(2,1)S(1)} %get-tuple-element.51), channel_id=1, source_target_pairs={{0,8},{4,12},{8,0},{12,4},{16,24},{20,28},{24,16},{28,20},{1,9},{5... | collective-permute-start | bytes 835592 | tf_op jit(solution)/shard_map/ppermute | solution.py:155
  10.6 0.7 %copy-start.1 = (f32[4]{0:T(128)S(1)}, f32[4]{0:T(128)}, u32[]{:S(2)}) copy-start(f32[4]{0:T(128)} %offsets_ref.3) | copy-start | bytes 52
  10.6 0.7 %copy-start.2 = (f32[16]{0:T(128)S(1)}, f32[16]{0:T(128)}, u32[]{:S(2)}) copy-start(f32[16]{0:T(128)} %velocities_ref.3) | copy-start | bytes 196
  10.6 12.7 %collective-permute-start.3 = (bf16[272,512]{1,0:T(8,128)(2,1)S(1)}, bf16[272,512]{1,0:T(8,128)(2,1)S(1)}, u32[]{:S(2)}, u32[]{:S(2)}) collective-permute-start(bf16[272,512]{1,0:T(8,128)(2,1)S(1)} %get-tuple-element.53), channel_id=1, source_target_pairs={{0,16},{4,20},{8,24},{12,28},{16,0},{20,4},{24,8},{28,12},{1,17},{... | collective-permute-start | bytes 835592 | tf_op jit(solution)/shard_map/ppermute | solution.py:155
  17.4 8.9 %collective-permute-start.9 = (bf16[136,640]{1,0:T(8,128)(2,1)S(1)}, bf16[136,640]{1,0:T(8,128)(2,1)S(1)}, u32[]{:S(2)}, u32[]{:S(2)}) collective-permute-start(bf16[136,640]{1,0:T(8,128)(2,1)S(1)} %get-tuple-element.68), channel_id=1, source_target_pairs={{0,8},{4,12},{8,0},{12,4},{16,24},{20,28},{24,16},{28,20},{1,9},{5... | collective-permute-start | bytes 522248 | tf_op jit(solution)/shard_map/ppermute | solution.py:155
  19.0 7.4 %collective-permute-start.8 = (bf16[136,512]{1,0:T(8,128)(2,1)S(1)}, bf16[136,512]{1,0:T(8,128)(2,1)S(1)}, u32[]{:S(2)}, u32[]{:S(2)}) collective-permute-start(bf16[136,512]{1,0:T(8,128)(2,1)S(1)} %get-tuple-element.66), channel_id=1, source_target_pairs={{0,16},{4,20},{8,24},{12,28},{16,0},{20,4},{24,8},{28,12},{1,17},{... | collective-permute-start | bytes 417800 | tf_op jit(solution)/shard_map/ppermute | solution.py:155
  23.3 7.6 %collective-permute-start.6 = (bf16[136,512]{1,0:T(8,128)(2,1)S(1)}, bf16[136,512]{1,0:T(8,128)(2,1)S(1)}, u32[]{:S(2)}, u32[]{:S(2)}) collective-permute-start(bf16[136,512]{1,0:T(8,128)(2,1)S(1)} %get-tuple-element.62), channel_id=1, source_target_pairs={{0,16},{4,20},{8,24},{12,28},{16,0},{20,4},{24,8},{28,12},{1,17},{... | collective-permute-start | bytes 417800 | tf_op jit(solution)/shard_map/ppermute | solution.py:155
  24.9 6.1 %collective-permute-start.7 = (bf16[136,512]{1,0:T(8,128)(2,1)S(1)}, bf16[136,512]{1,0:T(8,128)(2,1)S(1)}, u32[]{:S(2)}, u32[]{:S(2)}) collective-permute-start(bf16[136,512]{1,0:T(8,128)(2,1)S(1)} %get-tuple-element.64), channel_id=1, source_target_pairs={{0,8},{4,12},{8,0},{12,4},{16,24},{20,28},{24,16},{28,20},{1,9},{5... | collective-permute-start | bytes 417800 | tf_op jit(solution)/shard_map/ppermute | solution.py:155
  26.5 10.3 %collective-permute-start.13 = (bf16[40,1152]{1,0:T(8,128)(2,1)S(1)}, bf16[40,1152]{1,0:T(8,128)(2,1)S(1)}, u32[]{:S(2)}, u32[]{:S(2)}) collective-permute-start(bf16[40,1152]{1,0:T(8,128)(2,1)S(1)} %get-tuple-element.78), channel_id=1, source_target_pairs={{0,3},{1,2},{2,1},{3,0},{4,7},{5,6},{6,5},{7,4},{8,11},{9,10},{10,... | collective-permute-start | bytes 276488 | tf_op jit(solution)/shard_map/ppermute | solution.py:228
  30.1 8.7 %collective-permute-start.14 = (bf16[40,1152]{1,0:T(8,128)(2,1)S(1)}, bf16[40,1152]{1,0:T(8,128)(2,1)S(1)}, u32[]{:S(2)}, u32[]{:S(2)}) collective-permute-start(bf16[40,1152]{1,0:T(8,128)(2,1)S(1)} %get-tuple-element.79), channel_id=1, source_target_pairs={{0,2},{1,3},{2,0},{3,1},{4,6},{5,7},{6,4},{7,5},{8,10},{9,11},{10,... | collective-permute-start | bytes 276488 | tf_op jit(solution)/shard_map/ppermute | solution.py:228
  30.1 8.7 %collective-permute-start.15 = (bf16[40,1152]{1,0:T(8,128)(2,1)S(1)}, bf16[40,1152]{1,0:T(8,128)(2,1)S(1)}, u32[]{:S(2)}, u32[]{:S(2)}) collective-permute-start(bf16[40,1152]{1,0:T(8,128)(2,1)S(1)} %get-tuple-element.80), channel_id=1, source_target_pairs={{0,1},{1,0},{2,3},{3,2},{4,5},{5,4},{6,7},{7,6},{8,9},{9,8},{10,11... | collective-permute-start | bytes 276488 | tf_op jit(solution)/shard_map/ppermute | solution.py:228
  31.0 12.7 %collective-permute-start.10 = (bf16[40,1024]{1,0:T(8,128)(2,1)S(1)}, bf16[40,1024]{1,0:T(8,128)(2,1)S(1)}, u32[]{:S(2)}, u32[]{:S(2)}) collective-permute-start(bf16[40,1024]{1,0:T(8,128)(2,1)S(1)} %get-tuple-element.74), channel_id=1, source_target_pairs={{0,1},{1,0},{2,3},{3,2},{4,5},{5,4},{6,7},{7,6},{8,9},{9,8},{10,11... | collective-permute-start | bytes 245768 | tf_op jit(solution)/shard_map/ppermute | solution.py:228
  32.3 11.4 %collective-permute-start.11 = (bf16[40,1024]{1,0:T(8,128)(2,1)S(1)}, bf16[40,1024]{1,0:T(8,128)(2,1)S(1)}, u32[]{:S(2)}, u32[]{:S(2)}) collective-permute-start(bf16[40,1024]{1,0:T(8,128)(2,1)S(1)} %get-tuple-element.75), channel_id=1, source_target_pairs={{0,2},{1,3},{2,0},{3,1},{4,6},{5,7},{6,4},{7,5},{8,10},{9,11},{10,... | collective-permute-start | bytes 245768 | tf_op jit(solution)/shard_map/ppermute | solution.py:228
  36.8 7.0 %collective-permute-start.12 = (bf16[40,1024]{1,0:T(8,128)(2,1)S(1)}, bf16[40,1024]{1,0:T(8,128)(2,1)S(1)}, u32[]{:S(2)}, u32[]{:S(2)}) collective-permute-start(bf16[40,1024]{1,0:T(8,128)(2,1)S(1)} %get-tuple-element.76), channel_id=1, source_target_pairs={{0,3},{1,2},{2,1},{3,0},{4,7},{5,6},{6,5},{7,4},{8,11},{9,10},{10,... | collective-permute-start | bytes 245768 | tf_op jit(solution)/shard_map/ppermute | solution.py:228
